TPU v7x, 32 devices: a whole 2x2x4 slice. The times are simulated.
32 devices in a mesh: section: 2 (over x), tensor: 4 (over y, core), dp: 4 (over z).
Axes of the slice: x: 2, y: 2, z: 4, core: 2. Of those that a mesh axis runs over, the one named last changes fastest.
Arguments:
- inputs: float32 [16, 32, 512], P('dp'), may hold values from -6 to 6
- lengths: int32 [16], P('dp'), may hold values from 1 to 32, 384 in all
- cotangent: float32 [16, 32, 512], P('dp'), may hold values from -6 to 6
- norm_gain: float32 [2, 5, 512], P('section'), may hold values from 0.5 to 1.5
- norm_bias: float32 [2, 5, 512], P('section'), may hold values from -2 to 2
- ffn_in: bfloat16 [2, 2, 512, 2048], P('section', None, None, 'tensor'), may hold values from -0.25 to 0.25
- ffn_out: bfloat16 [2, 2, 2048, 512], P('section', None, 'tensor'), may hold values from -0.125 to 0.125
- attn_in: bfloat16 [2, 4, 512, 512], P('section', None, None, 'tensor'), may hold values from -0.25 to 0.25
- pos_bias: float32 [2, 2, 512], P('section', None, 'tensor'), may hold values from -3 to 3
- attn_out: bfloat16 [2, 512, 512], P('section', 'tensor'), may hold values from -0.375 to 0.375
- conv_in: bfloat16 [2, 512, 2, 512], P('section', None, None, 'tensor'), may hold values from -0.25 to 0.25
- depthwise: float32 [2, 31, 512], P('section', None, 'tensor'), may hold values from -1 to 1
- bn_gain: float32 [2, 512], P('section', 'tensor'), may hold values from 0.5 to 1.5
- bn_shift: float32 [2, 512], P('section', 'tensor'), may hold values from -3 to 3
- conv_out: bfloat16 [2, 512, 512], P('section', 'tensor'), may hold values from -0.25 to 0.25
Outputs:
- layer_out: float32 [2, 16, 32, 512], P('section', 'dp')
- input_grads: float32 [2, 16, 32, 512], P('section', 'dp')
- grad_norm_gain: float32 [2, 5, 512], P('section')
- grad_norm_bias: float32 [2, 5, 512], P('section')
- grad_ffn_in: float32 [2, 2, 512, 2048], P('section', None, None, 'tensor')
- grad_ffn_out: float32 [2, 2, 2048, 512], P('section', None, 'tensor')
- grad_attn_in: float32 [2, 4, 512, 512], P('section', None, None, 'tensor')
- grad_pos_bias: float32 [2, 2, 512], P('section', None, 'tensor')
- grad_attn_out: float32 [2, 512, 512], P('section', 'tensor')
- grad_conv_in: float32 [2, 512, 2, 512], P('section', None, None, 'tensor')
- grad_depthwise: float32 [2, 31, 512], P('section', None, 'tensor')
- grad_bn_gain: float32 [2, 512], P('section', 'tensor')
- grad_bn_shift: float32 [2, 512], P('section', 'tensor')
- grad_conv_out: float32 [2, 512, 512], P('section', 'tensor')
Inputs may be any that keep to these rules, and one draw needn't show every extreme that they name: `lengths`: frames of each utterance; they sum to 384 and the longest has exactly 32.
All inputs are finite; a program needn't handle non-finite values. No bound on the sum of `lengths` on one device may be relied on, other than what follows from the above.
Results may differ from a plain program's by a relative error of at most 0.035.
Values may be sent and summed in bfloat16 or wider, within the bound.
A program may use at most 128 MiB of HBM per device.

v0:
```python
import math

import jax
import jax.numpy as jnp
from jax import lax
from jax.sharding import PartitionSpec as P

HEAD = 64


highest_precision = lax.Precision.HIGHEST
epsilon = 1e-05


def from_behind(block, axis, distance):
    devices = range(lax.axis_size(axis))
    route = [(i - distance, i) for i in devices if i - distance in devices]
    return lax.ppermute(block, axis, route)


def rounded(member):
    return member.astype(jnp.bfloat16)


def matmul(left_side, right_side):
    return jnp.dot(left_side, right_side, preferred_element_type=jnp.float32)


def over_rows(left_side, right_side):
    return lax.dot_general(
        left_side, right_side, (((0,), (0,)), ((), ())), preferred_element_type=jnp.float32
    )


def against(left_side, right_side):
    return lax.dot_general(
        left_side, right_side, (((1,), (1,)), ((), ())), preferred_element_type=jnp.float32
    )


def layer_norm(states, norm_gain, norm_bias):
    centre = states - jnp.mean(states, -1, keepdims=True)
    spread = jnp.mean(centre * centre, -1, keepdims=True)
    return centre * lax.rsqrt(spread + epsilon) * norm_gain + norm_bias


def norm_back(states, norm_gain, norm_bias, upstream):
    primal, pull_back = jax.vjp(layer_norm, states, norm_gain, norm_bias)
    return pull_back(upstream)


def positions(frames, model_width):
    offset = jnp.arange(2 * frames - 1, dtype=jnp.float32) - (frames - 1)
    freq_rates = jnp.exp(
        jnp.arange(model_width // 2, dtype=jnp.float32) * (-2.0 * math.log(10000.0) / model_width)
    )
    angles = offset[:, None] * freq_rates[None, :]
    return jnp.stack([jnp.sin(angles), jnp.cos(angles)], -1).reshape(2 * frames - 1, model_width)


def offsets(frames):
    row_index = jnp.arange(frames, dtype=jnp.int32)
    return (row_index[:, None] - row_index[None, :] + (frames - 1)).astype(jnp.int32)


def split_heads(member):
    return member.reshape(member.shape[0], -1, HEAD).transpose(1, 0, 2)


def merge_heads(member):
    return member.transpose(1, 0, 2).reshape(member.shape[1], -1)


def depth_conv(signal, kernel):
    tap_count = kernel.shape[0]
    result = lax.conv_general_dilated(
        signal[None],
        kernel[:, None, :],
        (1,),
        [(tap_count // 2, tap_count // 2)],
        dimension_numbers=("NWC", "WIO", "NWC"),
        feature_group_count=signal.shape[-1],
        precision=highest_precision,
    )
    return result[0]


def glu_mask(gate_rows, frame_mask):
    channels = gate_rows.shape[1] // 2
    return gate_rows[:, :channels] * jax.nn.sigmoid(gate_rows[:, channels:]) * frame_mask[:, None]


def finish(states, partial_sum, factor):
    return states + factor * lax.psum(partial_sum.astype(jnp.bfloat16), "tensor").astype(
        jnp.float32
    )


def normed_rows(states, norm_gain, norm_bias):
    normed = rounded(layer_norm(states, norm_gain, norm_bias))
    return normed


def back_total(partial_sum):
    return lax.psum(partial_sum.astype(jnp.bfloat16), "tensor").astype(jnp.float32)


def feed_local(states, norm_gain, norm_bias, weight_in):
    normed = normed_rows(states, norm_gain, norm_bias)
    hidden = matmul(normed, weight_in)
    return (normed, hidden, rounded(jax.nn.silu(hidden)))


def feed_forward(states, norm_gain, norm_bias, weight_in, weight_out):
    normed, hidden, active = feed_local(states, norm_gain, norm_bias, weight_in)
    return finish(states, matmul(active, weight_out), 0.5)


def feed_backward(states, upstream, norm_gain, norm_bias, weight_in, weight_out):
    normed, hidden, active = feed_local(states, norm_gain, norm_bias, weight_in)
    branch_grad = rounded(0.5 * upstream)
    active_grad = against(branch_grad, weight_out)
    hidden_grad = rounded(jax.vjp(jax.nn.silu, hidden)[1](active_grad)[0])
    normed_grad = back_total(against(hidden_grad, weight_in))
    state_grad, gain_grad, bias_grad = norm_back(states, norm_gain, norm_bias, normed_grad)
    return (
        upstream + state_grad,
        gain_grad,
        bias_grad,
        over_rows(normed, hidden_grad),
        over_rows(active, branch_grad),
    )


def attend_local(states, frame_mask, norm_gain, norm_bias, weight_in, pos_bias, rel_table):
    normed = normed_rows(states, norm_gain, norm_bias)
    queries = matmul(normed, weight_in[0])
    key_rows = rounded(matmul(normed, weight_in[1]))
    values = rounded(matmul(normed, weight_in[2]))
    relative_key_rows = rounded(matmul(rel_table, weight_in[3]))
    query_u = rounded(queries + pos_bias[0])
    query_position_bias = rounded(queries + pos_bias[1])
    per_head_tensors = (
        split_heads(query_u),
        split_heads(query_position_bias),
        split_heads(key_rows),
        split_heads(values),
        split_heads(relative_key_rows),
    )
    frames = normed.shape[0]
    content = jnp.einsum(
        "hid,hjd->hij", per_head_tensors[0], per_head_tensors[2], preferred_element_type=jnp.float32
    )
    complete_relative = jnp.einsum(
        "nte,nve->ntv", per_head_tensors[1], per_head_tensors[4], preferred_element_type=jnp.float32
    )
    placed = jnp.take_along_axis(
        complete_relative, jnp.broadcast_to(offsets(frames)[None], content.shape), 2
    )
    scores = jnp.where(frame_mask[None, None, :] > 0, (content + placed) * HEAD ** (-0.5), -1e30)
    return (normed, per_head_tensors, scores)


def attention_forward(
    states, frame_mask, norm_gain, norm_bias, weight_in, pos_bias, weight_out, rel_table
):
    normed, per_head_tensors, scores = attend_local(
        states, frame_mask, norm_gain, norm_bias, weight_in, pos_bias, rel_table
    )
    row_max = jnp.max(scores, -1, keepdims=True)
    log_total = row_max + jnp.log(jnp.sum(jnp.exp(scores - row_max), -1, keepdims=True))
    attn_probs = rounded(jnp.exp(scores - log_total))
    mixed_out = rounded(
        merge_heads(
            jnp.einsum(
                "hij,hjd->hid", attn_probs, per_head_tensors[3], preferred_element_type=jnp.float32
            )
        )
    )
    return (finish(states, matmul(mixed_out, weight_out), 1.0), log_total)


def attention_backward(
    states,
    upstream,
    frame_mask,
    log_total,
    norm_gain,
    norm_bias,
    weight_in,
    pos_bias,
    weight_out,
    rel_table,
):
    normed, per_head_tensors, scores = attend_local(
        states, frame_mask, norm_gain, norm_bias, weight_in, pos_bias, rel_table
    )
    heads_u, heads_position_bias, heads_key, heads_val, relative_heads_split = per_head_tensors
    attn_probs = jnp.exp(scores - log_total)
    low_probs = rounded(attn_probs)
    mixed_out = rounded(
        merge_heads(
            jnp.einsum("hij,hjd->hid", low_probs, heads_val, preferred_element_type=jnp.float32)
        )
    )
    branch_grad = rounded(upstream)
    mixed_grad = split_heads(rounded(against(branch_grad, weight_out)))
    prob_grad = jnp.einsum(
        "hid,hjd->hij", mixed_grad, heads_val, preferred_element_type=jnp.float32
    )
    score_grad = rounded(
        attn_probs * (prob_grad - jnp.sum(attn_probs * prob_grad, -1, keepdims=True))
    )
    score_scale = HEAD ** (-0.5)
    frames = normed.shape[0]
    padded = jnp.pad(score_grad, ((0, 0), (0, 0), (frames - 1, frames - 1)))
    row_index = jnp.arange(frames, dtype=jnp.int32)
    col_index = jnp.arange(2 * frames - 1, dtype=jnp.int32)
    back_index = row_index[:, None] - col_index[None, :] + (2 * frames - 2)
    complete_backward = jnp.take_along_axis(
        padded, jnp.broadcast_to(back_index[None], (padded.shape[0], frames, 2 * frames - 1)), 2
    )
    grad_u = (
        merge_heads(
            jnp.einsum("hij,hjd->hid", score_grad, heads_key, preferred_element_type=jnp.float32)
        )
        * score_scale
    )
    grad_key = (
        merge_heads(
            jnp.einsum("hij,hid->hjd", score_grad, heads_u, preferred_element_type=jnp.float32)
        )
        * score_scale
    )
    grad_v = (
        merge_heads(
            jnp.einsum(
                "wlc,wcb->wlb",
                complete_backward,
                relative_heads_split,
                preferred_element_type=jnp.float32,
            )
        )
        * score_scale
    )
    grad_rel = (
        merge_heads(
            jnp.einsum(
                "yvz,yvt->yzt",
                complete_backward,
                heads_position_bias,
                preferred_element_type=jnp.float32,
            )
        )
        * score_scale
    )
    value_grad = rounded(
        merge_heads(
            jnp.einsum("hij,hid->hjd", low_probs, mixed_grad, preferred_element_type=jnp.float32)
        )
    )
    query_grad = rounded(grad_u + grad_v)
    key_grad = rounded(grad_key)
    rel_grad = rounded(grad_rel)
    normed_grad = back_total(
        against(query_grad, weight_in[0])
        + against(key_grad, weight_in[1])
        + against(value_grad, weight_in[2])
    )
    state_grad, gain_grad, bias_grad = norm_back(states, norm_gain, norm_bias, normed_grad)
    in_grad = jnp.stack(
        [
            over_rows(normed, query_grad),
            over_rows(normed, key_grad),
            over_rows(normed, value_grad),
            over_rows(rel_table, rel_grad),
        ]
    )
    pos_grad = jnp.stack([jnp.sum(grad_u, 0), jnp.sum(grad_v, 0)])
    return (
        upstream + state_grad,
        gain_grad,
        bias_grad,
        in_grad,
        pos_grad,
        over_rows(mixed_out, branch_grad),
    )


def conv_local(states, frame_mask, norm_gain, norm_bias, weight_in, kernel):
    normed = normed_rows(states, norm_gain, norm_bias)
    gate_rows = matmul(normed, weight_in.reshape(weight_in.shape[0], -1))
    signal = glu_mask(gate_rows, frame_mask)
    return (normed, gate_rows, signal, depth_conv(signal, kernel))


def conv_forward(
    states, frame_mask, norm_gain, norm_bias, weight_in, kernel, bn_gain, bn_shift, weight_out
):
    normed, gate_rows, signal, mixed_out = conv_local(
        states, frame_mask, norm_gain, norm_bias, weight_in, kernel
    )
    mask_col = frame_mask[:, None]
    first_sum, square_sum, frame_count = lax.psum(
        (
            jnp.sum(mixed_out * mask_col, 0),
            jnp.sum(mixed_out * mixed_out * mask_col, 0),
            jnp.sum(frame_mask),
        ),
        "dp",
    )
    batch_mean = first_sum / frame_count
    inv_std = lax.rsqrt(square_sum / frame_count - batch_mean * batch_mean + epsilon)
    scaled = (mixed_out - batch_mean) * inv_std * bn_gain + bn_shift
    after = finish(states, matmul(rounded(jax.nn.silu(scaled)), weight_out), 1.0)
    return (after, batch_mean, inv_std, frame_count)


def conv_backward(
    states,
    upstream,
    frame_mask,
    batch_mean,
    inv_std,
    frame_count,
    norm_gain,
    norm_bias,
    weight_in,
    kernel,
    bn_gain,
    bn_shift,
    weight_out,
):
    normed, gate_rows, signal, mixed_out = conv_local(
        states, frame_mask, norm_gain, norm_bias, weight_in, kernel
    )
    mask_col = frame_mask[:, None]
    centred = (mixed_out - batch_mean) * inv_std
    scaled = centred * bn_gain + bn_shift
    active = rounded(jax.nn.silu(scaled))
    branch_grad = rounded(upstream)
    scaled_grad = jax.vjp(jax.nn.silu, scaled)[1](against(branch_grad, weight_out))[0]
    centred_grad = scaled_grad * bn_gain
    total_grad, cross_grad = lax.psum(
        (jnp.sum(centred_grad * mask_col, 0), jnp.sum(centred_grad * centred * mask_col, 0)), "dp"
    )
    mixed_grad = (
        inv_std * (centred_grad - (total_grad + centred * cross_grad) / frame_count) * mask_col
    )
    primal, pull_back = jax.vjp(depth_conv, signal, kernel)
    signal_grad, kernel_grad = pull_back(mixed_grad)
    gate_grad = rounded(
        jax.vjp(lambda gate_in: glu_mask(gate_in, frame_mask), gate_rows)[1](signal_grad)[0]
    )
    flat_in = weight_in.reshape(weight_in.shape[0], -1)
    normed_grad = back_total(against(gate_grad, flat_in))
    state_grad, gain_grad, bias_grad = norm_back(states, norm_gain, norm_bias, normed_grad)
    return (
        upstream + state_grad,
        gain_grad,
        bias_grad,
        over_rows(normed, gate_grad).reshape(weight_in.shape),
        kernel_grad,
        jnp.sum(scaled_grad * centred, 0),
        jnp.sum(scaled_grad, 0),
        over_rows(active, branch_grad),
    )


def layer_forward(states, frame_mask, params, rel_table):
    (
        norm_gain,
        norm_bias,
        ffn_in,
        ffn_out,
        attn_in,
        pos_bias,
        attn_out,
        conv_in,
        kernel,
        bn_gain,
        bn_shift,
        conv_out,
    ) = params
    after_ffn = feed_forward(states, norm_gain[0], norm_bias[0], ffn_in[0], ffn_out[0])
    after_attn, log_total = attention_forward(
        after_ffn, frame_mask, norm_gain[1], norm_bias[1], attn_in, pos_bias, attn_out, rel_table
    )
    after_conv, batch_mean, inv_std, frame_count = conv_forward(
        after_attn,
        frame_mask,
        norm_gain[2],
        norm_bias[2],
        conv_in,
        kernel,
        bn_gain,
        bn_shift,
        conv_out,
    )
    after_last = feed_forward(after_conv, norm_gain[3], norm_bias[3], ffn_in[1], ffn_out[1])
    output = layer_norm(after_last, norm_gain[4], norm_bias[4]) * frame_mask[:, None]
    return (
        output,
        (
            states,
            after_ffn,
            after_attn,
            after_conv,
            after_last,
            log_total,
            batch_mean,
            inv_std,
            frame_count,
        ),
    )


def layer_backward(upstream, frame_mask, params, rel_table, kept_state):
    (
        norm_gain,
        norm_bias,
        ffn_in,
        ffn_out,
        attn_in,
        pos_bias,
        attn_out,
        conv_in,
        kernel,
        bn_gain,
        bn_shift,
        conv_out,
    ) = params
    (
        states,
        after_ffn,
        after_attn,
        after_conv,
        after_last,
        log_total,
        batch_mean,
        inv_std,
        frame_count,
    ) = kept_state
    last_grad, gain_four, bias_four = norm_back(
        after_last, norm_gain[4], norm_bias[4], upstream * frame_mask[:, None]
    )
    conv_state_grad, gain_three, bias_three, ffn_in_one, ffn_out_one = feed_backward(
        after_conv, last_grad, norm_gain[3], norm_bias[3], ffn_in[1], ffn_out[1]
    )
    (
        attn_state_grad,
        gain_two,
        bias_two,
        conv_in_grad,
        kernel_grad,
        bn_gain_grad,
        bn_shift_grad,
        conv_out_grad,
    ) = conv_backward(
        after_attn,
        conv_state_grad,
        frame_mask,
        batch_mean,
        inv_std,
        frame_count,
        norm_gain[2],
        norm_bias[2],
        conv_in,
        kernel,
        bn_gain,
        bn_shift,
        conv_out,
    )
    ffn_state_grad, gain_one, bias_one, attn_in_grad, pos_grad, attn_out_grad = attention_backward(
        after_ffn,
        attn_state_grad,
        frame_mask,
        log_total,
        norm_gain[1],
        norm_bias[1],
        attn_in,
        pos_bias,
        attn_out,
        rel_table,
    )
    input_grad, gain_zero, bias_zero, ffn_in_zero, ffn_out_zero = feed_backward(
        states, ffn_state_grad, norm_gain[0], norm_bias[0], ffn_in[0], ffn_out[0]
    )
    grads = [
        jnp.stack([gain_zero, gain_one, gain_two, gain_three, gain_four]),
        jnp.stack([bias_zero, bias_one, bias_two, bias_three, bias_four]),
        jnp.stack([ffn_in_zero, ffn_in_one]),
        jnp.stack([ffn_out_zero, ffn_out_one]),
        attn_in_grad,
        pos_grad,
        attn_out_grad,
        conv_in_grad,
        kernel_grad,
        bn_gain_grad,
        bn_shift_grad,
        conv_out_grad,
    ]
    return (input_grad, grads)


def on_device(
    inputs,
    lengths,
    cotangent,
    norm_gain,
    norm_bias,
    ffn_in,
    ffn_out,
    attn_in,
    pos_bias,
    attn_out,
    conv_in,
    depthwise,
    bn_gain,
    bn_shift,
    conv_out,
):
    params = tuple(
        (
            member[0]
            for member in (
                norm_gain,
                norm_bias,
                ffn_in,
                ffn_out,
                attn_in,
                pos_bias,
                attn_out,
                conv_in,
                depthwise,
                bn_gain,
                bn_shift,
                conv_out,
            )
        )
    )
    micro_count, frames, model_width = inputs.shape
    segment_index = lax.axis_index("section")
    rel_table = rounded(positions(frames, model_width))
    frame_index = jnp.arange(frames, dtype=jnp.int32)

    def mask_for(slot_index):
        length = lengths[jnp.clip(slot_index, 0, micro_count - 1)]
        return (frame_index < length).astype(jnp.float32)

    def select_slot(member, slot_index):
        return lax.dynamic_index_in_dim(
            member, jnp.clip(slot_index, 0, member.shape[0] - 1), 0, keepdims=False
        )

    arriving = jnp.zeros((frames, model_width), jnp.bfloat16)
    outputs = []
    kept_list = []
    for tick_index in range(micro_count + 1):
        slot_index = tick_index - segment_index
        layer_input = jnp.where(
            segment_index == 0, select_slot(inputs, slot_index), arriving.astype(jnp.float32)
        )
        output, kept_state = layer_forward(layer_input, mask_for(slot_index), params, rel_table)
        output = jnp.where(segment_index == 0, rounded(output).astype(jnp.float32), output)
        arriving = from_behind(rounded(output), "section", 1)
        outputs.append(output)
        kept_list.append(kept_state)
    stacked = jax.tree.map(lambda *members: jnp.stack(members), *kept_list)
    totals = [jnp.zeros(member.shape, jnp.float32) for member in params]
    returning = jnp.zeros((frames, model_width), jnp.bfloat16)
    grad_list = []
    for tick_index in range(micro_count + 1):
        slot_index = tick_index - 1 + segment_index
        is_valid = ((slot_index >= 0) & (slot_index < micro_count)).astype(jnp.float32)
        kept_state = jax.tree.map(
            lambda member: select_slot(member, slot_index + segment_index), stacked
        )
        upstream = jnp.where(
            segment_index == 1, select_slot(cotangent, slot_index), returning.astype(jnp.float32)
        )
        input_grad, step_grads = layer_backward(
            upstream, mask_for(slot_index), params, rel_table, kept_state
        )
        step_grads = [member * is_valid for member in step_grads]
        totals = [total + member for total, member in zip(totals, step_grads)]
        returning = from_behind(rounded(input_grad), "section", -1)
        grad_list.append(input_grad)
    totals = (
        lax.psum(totals[0].astype(jnp.bfloat16), "dp").astype(jnp.float32),
        lax.psum(totals[1].astype(jnp.bfloat16), "dp").astype(jnp.float32),
        lax.psum(totals[2].astype(jnp.bfloat16), "dp").astype(jnp.float32),
        lax.psum(totals[3].astype(jnp.bfloat16), "dp").astype(jnp.float32),
        lax.psum(totals[4].astype(jnp.bfloat16), "dp").astype(jnp.float32),
        lax.psum(totals[5].astype(jnp.bfloat16), "dp").astype(jnp.float32),
        lax.psum(totals[6].astype(jnp.bfloat16), "dp").astype(jnp.float32),
        lax.psum(totals[7].astype(jnp.bfloat16), "dp").astype(jnp.float32),
        lax.psum(totals[8].astype(jnp.bfloat16), "dp").astype(jnp.float32),
        lax.psum(totals[9].astype(jnp.bfloat16), "dp").astype(jnp.float32),
        lax.psum(totals[10].astype(jnp.bfloat16), "dp").astype(jnp.float32),
        lax.psum(totals[11].astype(jnp.bfloat16), "dp").astype(jnp.float32),
    )
    layer_out = lax.dynamic_slice_in_dim(jnp.stack(outputs), segment_index, micro_count, 0)
    input_grads = lax.dynamic_slice_in_dim(jnp.stack(grad_list), 1 - segment_index, micro_count, 0)
    return (
        layer_out[None],
        input_grads[None],
        totals[0][None],
        totals[1][None],
        totals[2][None],
        totals[3][None],
        totals[4][None],
        totals[5][None],
        totals[6][None],
        totals[7][None],
        totals[8][None],
        totals[9][None],
        totals[10][None],
        totals[11][None],
    )


def solution(mesh):
    placed = (
        P("dp", None, None),
        P("dp"),
        P("dp", None, None),
        P("section", None, None),
        P("section", None, None),
        P("section", None, None, "tensor"),
        P("section", None, "tensor", None),
        P("section", None, None, "tensor"),
        P("section", None, "tensor"),
        P("section", "tensor", None),
        P("section", None, None, "tensor"),
        P("section", None, "tensor"),
        P("section", "tensor"),
        P("section", "tensor"),
        P("section", "tensor", None),
    )
    return jax.shard_map(
        on_device,
        mesh=mesh,
        in_specs=placed,
        out_specs=(
            P("section", "dp", None, None),
            P("section", "dp", None, None),
            P("section", None, None),
            P("section", None, None),
            P("section", None, None, "tensor"),
            P("section", None, "tensor", None),
            P("section", None, None, "tensor"),
            P("section", None, "tensor"),
            P("section", "tensor", None),
            P("section", None, None, "tensor"),
            P("section", None, "tensor"),
            P("section", "tensor"),
            P("section", "tensor"),
            P("section", "tensor", None),
        ),
        check_vma=False,
    )
```

profile of v0, /device:TPU:0, one launch (start us, length us, event | category | flops | bytes accessed | tf_op | source)
XLA Modules:
  0.0 1814.1 jit_solution(17620760316944048284)
XLA Ops:
  15.6 12.9 psum.539
  36.2 17.4 gather_fusion
  66.1 12.7 all-reduce.24
  98.3 11.5 psum.545
  150.3 11.4 psum.546
  174.1 17.4 gather_fusion.1
  194.4 11.1 psum.547
  238.1 11.5 psum.552
  260.7 11.4 psum.553
  284.5 17.4 gather_fusion.2
  304.7 11.1 psum.554
  321.1 10.9 all-reduce.22
  334.1 11.1 psum.558
  350.7 11.9 psum.559
  376.5 11.4 psum.560
  400.4 17.4 gather_fusion.3
  420.6 11.1 psum.561
  464.4 11.5 psum.566
  489.9 11.4 psum.567
  524.3 17.4 gather_fusion.4
  545.9 11.1 psum.568
  605.8 11.5 psum.573
  623.4 26.2 %gather_fusion.5 = f32[2048]{0:T(1024)} fusion(f32[2,32,63]{2,1,0:T(8,128)S(1)} %fusion.558, s32[2048]{0:T(1024)S(1)} %reshape.3763), kind=kCustom, calls=%fused_computation.6.clone | custom fusion | bytes 40960 | tf_op jit(solution)/shard_map/jit(take_along_axis)/gather | solution.py:157
  692.8 11.8 psum.577
  717.8 47.7 %gather_fusion.6 = bf16[4032]{0:T(1024)(128)(2,1)} fusion(bf16[2,32,94]{1,2,0:T(8,128)(2,1)S(1)} %pad.48, s32[4032]{0:T(1024)S(1)} %reshape.3793), kind=kCustom, calls=%fused_computation.1.clone | custom fusion | bytes 64512 | tf_op jit(solution)/shard_map/jit(take_along_axis)/gather | solution.py:220
  776.8 11.1 psum.578
  901.2 17.4 gather_fusion.9
  919.4 17.4 gather_fusion.11
  937.6 17.4 gather_fusion.13
  955.9 17.4 gather_fusion.7
  984.8 11.3 psum.580
  1017.8 11.0 psum.583
  1039.3 47.7 %gather_fusion.8 = bf16[4032]{0:T(1024)(128)(2,1)} fusion(bf16[2,32,94]{1,2,0:T(8,128)(2,1)S(1)} %pad.51, s32[4032]{0:T(1024)S(1)} %reshape.3793), kind=kCustom, calls=%fused_computation.11.clone | custom fusion | bytes 64512 | tf_op jit(solution)/shard_map/jit(take_along_axis)/gather | solution.py:220
  1106.0 11.7 psum.584
  1168.2 11.9 psum.586
  1200.6 11.4 psum.589
  1225.0 38.7 %gather_fusion.10 = bf16[4032]{0:T(1024)(128)(2,1)S(1)} fusion(bf16[2,32,94]{1,2,0:T(8,128)(2,1)S(1)} %pad.54, s32[4032]{0:T(1024)S(1)} %reshape.3793), kind=kCustom, calls=%fused_computation.12.clone | custom fusion | bytes 64512 | tf_op jit(solution)/shard_map/jit(take_along_axis)/gather | solution.py:220
  1282.8 11.7 psum.590
  1345.4 11.0 psum.592
  1362.7 11.0 all-reduce.16
  1378.2 11.4 psum.595
  1402.4 47.7 %gather_fusion.12 = bf16[4032]{0:T(1024)(128)(2,1)} fusion(bf16[2,32,94]{1,2,0:T(8,128)(2,1)S(1)} %pad.57, s32[4032]{0:T(1024)S(1)} %reshape.3793), kind=kCustom, calls=%fused_computation.13.clone | custom fusion | bytes 64512 | tf_op jit(solution)/shard_map/jit(take_along_axis)/gather | solution.py:220
  1466.4 11.7 psum.596
  1528.9 11.9 psum.598
  1582.1 38.7 %gather_fusion.14 = bf16[4032]{0:T(1024)(128)(2,1)S(1)} fusion(bf16[2,32,94]{1,2,0:T(8,128)(2,1)S(1)} %pad.60, s32[4032]{0:T(1024)S(1)} %reshape.3793), kind=kCustom, calls=%fused_computation.14.clone | custom fusion | bytes 64512 | tf_op jit(solution)/shard_map/jit(take_along_axis)/gather | solution.py:220
  1630.6 11.4 psum.602
  1687.5 19.1 %all-reduce.25 = (bf16[1,5,512]{2,1,0:T(8,128)(2,1)S(1)}, bf16[1,31,128]{2,1,0:T(8,128)(2,1)S(1)}, bf16[1,5,512]{2,0,1:T(2,128)(2,1)S(1)}, bf16[1,2,128]{2,1,0:T...) all-reduce(bf16[1,5,512]{2,1,0:T(8,128)(2,1)S(1)} %fusion.1173, ...), channel_id=1, replica_groups=mesh['section'=2,'tensor'=4,'dp'=4] {'dp'}, use_global_device_ids=true, to_apply=%region_280.283 | all-reduce | flops 9600 | bytes 38400 | tf_op jit(solution)/shard_map/psum | solution.py:590
  1710.8 85.2 %all-reduce.29.cloned.1.call-done = (bf16[1,512,2,128]{3,1,2,0:T(8,128)(2,1)}, bf16[1,2,512,512]{3,2,1,0:T(8,128)(2,1)}, bf16[1,2,512,512]{3,2,1,0:T(8,128)(2,1)...) async-done(((bf16[1,512,2,128]{3,1,2,0:T(8,128)(2,1)}, bf16[1,2,512,512]{3,2,1,0:T(8,128)(2,1)}, ...) | async-done | bytes 3145744 | tf_op jit(solution)/shard_map/psum | solution.py:597
  (1634 shorter events, 931.1 us)
Async XLA Ops:
  7.2 72.3 %copy-start = (bf16[1,128,512]{2,1,0:T(8,128)(2,1)S(1)}, bf16[1,128,512]{2,1,0:T(8,128)(2,1)}, u32[]{:S(2)}) copy-start(bf16[1,128,512]{2,1,0:T(8,128)(2,1)} %param.33) | copy-start | bytes 393220
  7.2 1788.8 %all-reduce.29.cloned.1.call-start = ((), (), s32[]{:S(2)}) async-start(), calls=%async_computation | async-start | bytes 6291456 | tf_op jit(solution)/shard_map/psum | solution.py:597
  9.6 56.4 %copy-start.288 = (f32[32]{0:T(128)}, f32[32]{0:T(128)S(1)}, u32[]{:S(2)}) copy-start(f32[32]{0:T(128)S(1)} %compare_convert_fusion.9) | copy-start | bytes 388
  10.3 43.5 %copy-start.119 = (pred[2,32,32]{1,2,0:T(32,128)(4,1)}, pred[2,32,32]{1,2,0:T(32,128)(4,1)S(1)}, u32[]{:S(2)}) copy-start(pred[2,32,32]{1,2,0:T(32,128)(4,1)S(1)} %fusion.782) | copy-start | bytes 6148
  11.1 126.9 %copy-start.87 = (f32[1,1,512]{2,0,1:T(1,128)}, f32[1,1,512]{2,0,1:T(1,128)S(1)}, u32[]{:S(2)}) copy-start(f32[1,1,512]{2,0,1:T(1,128)S(1)} %get-tuple-element.411) | copy-start | bytes 6148
  11.1 476.6 %copy-start.77 = (f32[1,1,512]{2,0,1:T(1,128)}, f32[1,1,512]{2,0,1:T(1,128)S(1)}, u32[]{:S(2)}) copy-start(f32[1,1,512]{2,0,1:T(1,128)S(1)} %get-tuple-element.410) | copy-start | bytes 6148
  11.1 697.2 %copy-start.84 = (f32[1,1,512]{2,0,1:T(1,128)}, f32[1,1,512]{2,0,1:T(1,128)S(1)}, u32[]{:S(2)}) copy-start(f32[1,1,512]{2,0,1:T(1,128)S(1)} %get-tuple-element.408) | copy-start | bytes 6148
  11.9 53.8 %copy-start.202 = (f32[1,1,512]{2,0,1:T(1,128)}, f32[1,1,512]{2,0,1:T(1,128)S(1)}, u32[]{:S(2)}) copy-start(f32[1,1,512]{2,0,1:T(1,128)S(1)} %get-tuple-element.413) | copy-start | bytes 6148
  11.9 84.3 %copy-start.143 = (f32[1,1,512]{2,0,1:T(1,128)}, f32[1,1,512]{2,0,1:T(1,128)S(1)}, u32[]{:S(2)}) copy-start(f32[1,1,512]{2,0,1:T(1,128)S(1)} %get-tuple-element.412) | copy-start | bytes 6148
  11.9 126.1 %copy-start.150 = (f32[1,1,512]{2,0,1:T(1,128)}, f32[1,1,512]{2,0,1:T(1,128)S(1)}, u32[]{:S(2)}) copy-start(f32[1,1,512]{2,0,1:T(1,128)S(1)} %get-tuple-element.416) | copy-start | bytes 6148
  36.2 43.3 %copy-start.189 = (f32[1,128]{1,0:T(1,128)S(1)}, f32[1,128]{1,0:T(1,128)}, u32[]{:S(2)}) copy-start(f32[1,128]{1,0:T(1,128)} %param.31) | copy-start | bytes 1540
  36.2 43.3 %copy-start.232 = (f32[1,128]{1,0:T(1,128)S(1)}, f32[1,128]{1,0:T(1,128)}, u32[]{:S(2)}) copy-start(f32[1,128]{1,0:T(1,128)} %param.32) | copy-start | bytes 1540
  53.7 42.5 %copy-start.1 = (bf16[1,2,512,512]{3,2,1,0:T(8,128)(2,1)S(1)}, bf16[1,2,512,512]{3,2,1,0:T(8,128)(2,1)}, u32[]{:S(2)}) copy-start(bf16[1,2,512,512]{3,2,1,0:T(8,128)(2,1)} %param.24) | copy-start | bytes 3145732
  66.1 45.7 %copy-start.289 = (f32[32]{0:T(128)S(1)}, f32[32]{0:T(128)}, u32[]{:S(2)}) copy-start(f32[32]{0:T(128)} %copy-done.288) | copy-start | bytes 388
  79.4 57.9 %copy-start.313 = (f32[128]{0:T(128)}, f32[128]{0:T(128)S(1)}, u32[]{:S(2)}) copy-start(f32[128]{0:T(128)S(1)} %get-tuple-element.339) | copy-start | bytes 1540
  79.4 57.9 %copy-start.314 = (f32[128]{0:T(128)}, f32[128]{0:T(128)S(1)}, u32[]{:S(2)}) copy-start(f32[128]{0:T(128)S(1)} %get-tuple-element.340) | copy-start | bytes 1540
  91.9 46.1 %copy-start.27 = (f32[32,512]{1,0:T(8,128)S(1)}, f32[32,512]{1,0:T(8,128)}, u32[]{:S(2)}) copy-start(f32[32,512]{1,0:T(8,128)} %get-tuple-element.330) | copy-start | bytes 196612
  113.4 31.4 %collective-permute-start = (bf16[32,512]{1,0:T(8,128)(2,1)}, bf16[32,512]{1,0:T(8,128)(2,1)}, u32[]{:S(2)}, u32[]{:S(2)}) collective-permute-start(bf16[32,512]{1,0:T(8,128)(2,1)} %fusion.1352), channel_id=1, source_target_pairs={{0,16},{1,17},{2,18},{3,19},{4,20},{5,21},{6,22},{7,23},{8,24},{9,... | collective-permute-start | bytes 98312 | tf_op jit(solution)/shard_map/ppermute | solution.py:18
  137.4 630.4 %copy-start.80 = (pred[2,32,63]{2,1,0:T(32,128)(4,1)}, pred[2,32,63]{2,1,0:T(32,128)(4,1)S(1)}, u32[]{:S(2)}) copy-start(pred[2,32,63]{2,1,0:T(32,128)(4,1)S(1)} %fusion.783) | copy-start | bytes 12100
  252.3 2.9 collective-permute-start.1
  365.2 5.8 collective-permute-start.2
  478.6 5.8 collective-permute-start.3
  541.8 61.9 %copy-start.144 = (f32[1,1,512]{2,0,1:T(1,128)S(1)}, f32[1,1,512]{2,0,1:T(1,128)}, u32[]{:S(2)}) copy-start(f32[1,1,512]{2,0,1:T(1,128)} %copy-done.143) | copy-start | bytes 6148
  656.0 50.7 %copy-start.268 = (f32[32]{0:T(128)S(1)}, f32[32]{0:T(128)}, u32[]{:S(2)}) copy-start(f32[32]{0:T(128)} %broadcast_multiply_fusion.2) | copy-start | bytes 388
  717.7 52.5 %copy-start.354 = (f32[32]{0:T(128)S(1)}, f32[32]{0:T(128)}, u32[]{:S(2)}) copy-start(f32[32]{0:T(128)} %get-tuple-element.149) | copy-start | bytes 388
  717.8 53.0 %copy-start.353 = (f32[32]{0:T(128)S(1)}, f32[32]{0:T(128)}, u32[]{:S(2)}) copy-start(f32[32]{0:T(128)} %get-tuple-element.150) | copy-start | bytes 388
  717.8 55.8 %copy-start.135 = (bf16[2,32,32]{1,2,0:T(8,128)(2,1)S(1)}, bf16[2,32,32]{1,2,0:T(8,128)(2,1)}, u32[]{:S(2)}) copy-start(bf16[2,32,32]{1,2,0:T(8,128)(2,1)} %copy-done.134) | copy-start | bytes 12292
  864.2 113.9 %collective-permute-start.4 = (bf16[32,512]{1,0:T(8,128)(2,1)}, bf16[32,512]{1,0:T(8,128)(2,1)}, u32[]{:S(2)}, u32[]{:S(2)}) collective-permute-start(bf16[32,512]{1,0:T(8,128)(2,1)} %fusion.1099), channel_id=1, source_target_pairs={{16,0},{17,1},{18,2},{19,3},{20,4},{21,5},{22,6},{23,7},{24,8},{25... | collective-permute-start | bytes 98312 | tf_op jit(solution)/shard_map/ppermute | solution.py:18
  973.3 43.7 %copy-start.5 = (bf16[1,512,2,128]{3,2,1,0:T(2,128)(2,1)S(1)}, bf16[1,512,2,128]{3,2,1,0:T(2,128)(2,1)}, u32[]{:S(2)}) copy-start(bf16[1,512,2,128]{3,2,1,0:T(2,128)(2,1)} %param.29) | copy-start | bytes 786436
  976.7 57.9 %copy-start.124 = (pred[2,32,32]{1,2,0:T(32,128)(4,1)S(1)}, pred[2,32,32]{1,2,0:T(32,128)(4,1)}, u32[]{:S(2)}) copy-start(pred[2,32,32]{1,2,0:T(32,128)(4,1)} %copy-done.119) | copy-start | bytes 6148
  981.4 51.6 %copy-start.328 = (f32[32]{0:T(128)}, f32[32]{0:T(128)S(1)}, u32[]{:S(2)}) copy-start(f32[32]{0:T(128)S(1)} %negate_multiply_fusion.19) | copy-start | bytes 388
  1039.3 48.6 %copy-start.81 = (pred[2,32,63]{2,1,0:T(32,128)(4,1)S(1)}, pred[2,32,63]{2,1,0:T(32,128)(4,1)}, u32[]{:S(2)}) copy-start(pred[2,32,63]{2,1,0:T(32,128)(4,1)} %copy-done.80) | copy-start | bytes 12100
  1147.4 14.6 collective-permute-start.5
  1153.9 58.1 %copy-start.86 = (f32[1,1,512]{2,0,1:T(1,128)S(1)}, f32[1,1,512]{2,0,1:T(1,128)}, u32[]{:S(2)}) copy-start(f32[1,1,512]{2,0,1:T(1,128)} %copy-done.84) | copy-start | bytes 6148
  1156.8 57.4 %copy-start.271 = (f32[32]{0:T(128)S(1)}, f32[32]{0:T(128)}, u32[]{:S(2)}) copy-start(f32[32]{0:T(128)} %broadcast_multiply_fusion.12) | copy-start | bytes 388
  1160.7 58.9 %copy-start.125 = (pred[2,32,32]{1,2,0:T(32,128)(4,1)S(1)}, pred[2,32,32]{1,2,0:T(32,128)(4,1)}, u32[]{:S(2)}) copy-start(pred[2,32,32]{1,2,0:T(32,128)(4,1)} %copy-done.119) | copy-start | bytes 6148
  1165.3 50.3 %copy-start.97 = (f32[32,512]{1,0:T(8,128)}, f32[32,512]{1,0:T(8,128)S(1)}, u32[]{:S(2)}) copy-start(f32[32,512]{1,0:T(8,128)S(1)} %get-tuple-element.284) | copy-start | bytes 196612
  1165.3 50.3 %copy-start.329 = (f32[32]{0:T(128)}, f32[32]{0:T(128)S(1)}, u32[]{:S(2)}) copy-start(f32[32]{0:T(128)S(1)} %negate_multiply_fusion.14) | copy-start | bytes 388
  1225.0 44.1 %copy-start.203 = (f32[1,1,512]{2,0,1:T(1,128)S(1)}, f32[1,1,512]{2,0,1:T(1,128)}, u32[]{:S(2)}) copy-start(f32[1,1,512]{2,0,1:T(1,128)} %copy-done.202) | copy-start | bytes 6148
  1225.0 44.1 %copy-start.272 = (f32[32]{0:T(128)S(1)}, f32[32]{0:T(128)}, u32[]{:S(2)}) copy-start(f32[32]{0:T(128)} %broadcast_multiply_fusion.12) | copy-start | bytes 388
  1324.0 15.3 collective-permute-start.6
  1342.6 58.2 %copy-start.330 = (f32[32]{0:T(128)}, f32[32]{0:T(128)S(1)}, u32[]{:S(2)}) copy-start(f32[32]{0:T(128)S(1)} %negate_multiply_fusion.9) | copy-start | bytes 388
  1402.4 59.8 %copy-start.33 = (bf16[32,512]{1,0:T(8,128)(2,1)S(1)}, bf16[32,512]{1,0:T(8,128)(2,1)}, u32[]{:S(2)}) copy-start(bf16[32,512]{1,0:T(8,128)(2,1)} %copy-done.32) | copy-start | bytes 98308
  1508.1 14.6 collective-permute-start.7
  1517.6 56.5 %copy-start.269 = (f32[32]{0:T(128)S(1)}, f32[32]{0:T(128)}, u32[]{:S(2)}) copy-start(f32[32]{0:T(128)} %broadcast_multiply_fusion.2) | copy-start | bytes 388
  1521.4 56.1 %copy-start.126 = (pred[2,32,32]{1,2,0:T(32,128)(4,1)S(1)}, pred[2,32,32]{1,2,0:T(32,128)(4,1)}, u32[]{:S(2)}) copy-start(pred[2,32,32]{1,2,0:T(32,128)(4,1)} %copy-done.119) | copy-start | bytes 6148
  1526.0 49.4 %copy-start.95 = (f32[32,512]{1,0:T(8,128)}, f32[32,512]{1,0:T(8,128)S(1)}, u32[]{:S(2)}) copy-start(f32[32,512]{1,0:T(8,128)S(1)} %get-tuple-element.276) | copy-start | bytes 196612
  1526.1 49.4 %copy-start.327 = (f32[32]{0:T(128)}, f32[32]{0:T(128)S(1)}, u32[]{:S(2)}) copy-start(f32[32]{0:T(128)S(1)} %negate_multiply_fusion.4) | copy-start | bytes 388
  (337 other events, 3378.0 us)
Sparse Core Ops, SparseCore 0:
  1671.4 124.5 all-reduce.28
where the time goes:
time: 1840 us; the launch traced here: 1810 us
  blocking collectives  570 us (31%)
  local copies, waits for them, and re-layouts  563 us (31%)
  other arithmetic  280 us (15%)
  matrix products  277 us (15%)
  waiting for transfers between devices  85.5 us (5%)
  between operations  19.3 us (1%)
  starting transfers between devices  18.9 us (1%)
    psum x20, blocking collectives, finish(): lax.psum(partial_sum.astype(jnp.bfloat16), 'tensor').astype(jnp.float32)  226 us
    gather x11, local copies, waits for them, and re-layouts, attention_backward(): jnp.take_along_axis(padded, jnp.broadcast_to(back_index[None], (padded.sh...  225 us
    psum x20, blocking collectives, back_total(): lax.psum(partial_sum.astype(jnp.bfloat16), 'tensor').astype(jnp.float32)  225 us
    gather x32, local copies, waits for them, and re-layouts, attend_local(): jnp.take_along_axis(complete_relative, jnp.broadcast_to(offsets(frames)[N...  192 us
    dot_general x55, matrix products, over_rows(): lax.dot_general(left_side, right_side, (((0,), (0,)), ((), ())), preferre...  88.6 us
    psum x1, waiting for transfers between devices, on_device(): lax.psum(totals[7].astype(jnp.bfloat16), 'dp').astype(jnp.float32)  85.2 us
    dot_general x71, matrix products, matmul(): return jnp.dot(left_side, right_side, preferred_element_type=jnp.float32)  68.9 us
    reduce_sum x41, other arithmetic, layer_norm(): return centre * lax.rsqrt(spread + epsilon) * norm_gain + norm_bias  55 us
  transfers between devices with their start and end apart: 9, of which 4 were waited for; matrix products, arithmetic and copies ran while one was open for 11% of the time, Pallas kernels for 0%

commit v1 on v0

v1 whole, which is shorter than its diff:
```python
import math

import jax
import jax.numpy as jnp
import numpy as np
from jax import lax
from jax.experimental import pallas as pl
from jax.experimental.pallas import tpu as pltpu
from jax.sharding import PartitionSpec as P

HEAD = 64
EPSILON = 1e-05
MESH = pl.DeviceIdType.MESH
PLACE = (0, 2, 1, 3)
SMALL_ROWS = 40
bf16, f32 = jnp.bfloat16, jnp.float32


def dot(left, right, left_dim=1, right_dim=0):
    return lax.dot_general(
        left, right, (((left_dim,), (right_dim,)), ((), ())), preferred_element_type=f32
    )


def position_rows(frames, width):
    offset = np.arange(2 * frames - 1, dtype=np.float32) - np.float32(frames - 1)
    rates = np.exp(
        np.arange(width // 2, dtype=np.float32) * np.float32(-2.0 * math.log(10000.0) / width)
    )
    angles = (offset[:, None] * rates[None, :]).astype(np.float32)
    table = np.stack([np.sin(angles), np.cos(angles)], -1).reshape(2 * frames - 1, width)
    blank = np.zeros((1, width), np.float32)
    return jnp.asarray(np.concatenate([table[::-1], blank, table, blank]), bf16)


def layer_kernel(dims, *refs):
    frames, width, dp, groups = dims
    T = frames
    C = width // 4
    (lengths, inputs, cot, ng, nb, fin, fout, ain, aout, cin, cout, pos, bng, bns, dw, e2) = refs[:16]
    (Nall, Ball, Sf, Sb, LO, IG, PA, PB) = refs[16:24]
    (Win, Wout, Wqkv, Wr, Wo, Wci, Wco, R2, SM) = refs[24:33]
    (H, XH, RS, X, ARR, HOP, QKV, PRB, GVG, CT, UP, DP, SfSt, SbSt, PAst, PAin, PBin, STF, STB) = refs[33:52]
    ss, rs, ls = refs[52:55]

    s, t, d = lax.axis_index("section"), lax.axis_index("tensor"), lax.axis_index("dp")
    taps = dw.shape[0]
    peers = [(s, t ^ k, d) for k in range(4)]
    sib, yp = peers[1], peers[2]
    ahead = [lax.rem(d + r, dp) for r in range(dp)]
    behind = [lax.rem(d - r + dp, dp) for r in range(dp)]
    zpeers = [(s, t, ahead[r]) for r in range(dp)]
    zpair = (s, t, d ^ 1)
    partner = (1 - s, t, d)
    half = lax.rem(d, 2)
    other = 1 - half
    R4 = 4 * T
    base = pl.multiple_of(d * R4, R4) if groups > 1 else 0
    zbase = [pl.multiple_of(behind[r] * R4, R4) for r in range(dp)]
    zhigh = [pl.multiple_of(z + 2 * T, 2 * T) for z in zbase]
    trow = pl.multiple_of(t * T, T)

    index, pending = {}, []

    def copy_of(key, src, dst, dev):
        i = index.setdefault(key, len(index))
        return pltpu.make_async_remote_copy(
            src_ref=src, dst_ref=dst, send_sem=ss.at[i], recv_sem=rs.at[i],
            device_id=dev, device_id_type=MESH,
        )

    def start(key, src, dst, dev, cond=None):
        if cond is None:
            c = copy_of(key, src, dst, dev)
            c.start()
            pending.append((None, lambda: c))
        else:
            again = lambda: copy_of(key, src(), dst(), dev)
            again().start()
            pending.append((cond, again))

    def arrived(key, dst):
        copy_of(key, dst, dst, partner).wait_recv()

    def rows_of(ref_rows, part):
        if part is None:
            return pl.ds(0, ref_rows)
        n = ref_rows // 2
        return pl.ds(pl.multiple_of(part * n, n), n)

    halves = {}
    for n in (width, C):
        m = n // 2
        halves[n] = {"own": pl.multiple_of(half * m, m), "other": pl.multiple_of(other * m, m)}
    slot_rows = {
        (k, w): pl.multiple_of(C * k + halves[C][w], C // 2) for k in range(4) for w in ("own", "other")
    }

    def lines(n, which):
        return pl.ds(0, n) if which is None else pl.ds(halves[n][which], n // 2)

    def slot_lines(k, which):
        return pl.ds(C * k, C) if which is None else pl.ds(slot_rows[k, which], C // 2)

    def cols(k):
        return pl.ds(C * k, C)

    chunks = [
        (lambda w: fin.at[0, lines(width, w)], lambda k, w: Win.at[0, k, lines(width, w)]),
        (lambda w: fout.at[0, lines(width, w)], lambda k, w: Wout.at[0, k, lines(width, w)]),
        (lambda w: ain.at[pl.ds(0, 3), lines(width, w)], lambda k, w: Wqkv.at[:, lines(width, w), cols(k)]),
        (lambda w: aout.at[lines(C, w)], lambda k, w: Wo.at[slot_lines(k, w)]),
        (lambda w: cin.at[:, lines(width, w)], lambda k, w: Wci.at[:, lines(width, w), cols(k)]),
        (lambda w: cout.at[lines(C, w)], lambda k, w: Wco.at[slot_lines(k, w)]),
        (lambda w: fin.at[1, lines(width, w)], lambda k, w: Win.at[1, k, lines(width, w)]),
        (lambda w: fout.at[1, lines(width, w)], lambda k, w: Wout.at[1, k, lines(width, w)]),
    ]
    local = [pltpu.make_async_copy(ain.at[3], Wr, ls.at[8])] + [
        pltpu.make_async_copy(src(None), dst(0, None), ls.at[i]) for i, (src, dst) in enumerate(chunks)
    ]
    for c in local:
        c.start()

    barrier = pltpu.get_barrier_semaphore()
    greet = peers[1:] + zpeers[1:] + [partner]
    for dev in greet:
        pl.semaphore_signal(barrier, inc=1, device_id=dev, device_id_type=MESH)
    pl.semaphore_wait(barrier, len(greet))

    def send_chunk(i):
        src, dst = chunks[i]
        start(("sib", i), src(None), dst(1, None), sib)
        start(("y", i), src("own"), dst(2, "own"), yp)

    def step_a(i, cond):
        dst = chunks[i][1]
        arrived(("y", i), dst(2, "own"))
        start(("z", i), lambda: dst(2, "own"), lambda: dst(2, "own"), zpair, cond)
        start(("sib2", i), lambda: dst(2, "own"), lambda: dst(3, "own"), sib, cond)

    def step_b(i, cond):
        dst = chunks[i][1]
        arrived(("z", i), dst(2, "other"))
        start(("sib3", i), lambda: dst(2, "other"), lambda: dst(3, "other"), sib, cond)

    def step_c(i):
        dst = chunks[i][1]
        arrived(("sib", i), dst(1, None))
        arrived(("sib2", i), dst(3, "own"))
        arrived(("sib3", i), dst(3, "other"))

    def gather(i, cond):
        if i == 0:
            step_a(0, cond)
        if i + 1 < len(chunks):
            step_a(i + 1, cond)
        step_b(i, cond)
        step_c(i)

    def first_only(i):
        @pl.when(s == 0)
        def _():
            gather(i, 0)

    send_chunk(0)
    send_chunk(1)
    SM[:, 0:C] = jnp.zeros((SMALL_ROWS, C), f32)
    SM[0:2, 0:C] = pos[...]
    SM[2:3, 0:C] = bng[...]
    SM[3:4, 0:C] = bns[...]
    SM[4 : 4 + taps, 0:C] = dw[...]
    for k in (1, 2, 3):
        start(("small", k), SM.at[:, cols(0)], SM.at[:, cols(k)], peers[k])
    local[0].wait()
    R2[:, 0:C] = dot(e2[...], Wr[...]).astype(bf16)
    for k in (1, 2, 3):
        start(("rel", k), R2.at[:, cols(0)], R2.at[:, cols(k)], peers[k])
    for i in range(2, len(chunks)):
        send_chunk(i)
    for c in local[1:]:
        c.wait()

    margin = 16
    UP[...] = jnp.zeros(UP.shape, f32)
    DP[...] = jnp.zeros(DP.shape, f32)
    PAst[...] = jnp.zeros(PAst.shape, f32)
    PBin[t] = jnp.zeros(PBin.shape[1:], f32)

    length = lengths[t]
    row_mask = (lax.broadcasted_iota(jnp.int32, (T, 1), 0) < length).astype(f32)
    key_mask = lax.broadcasted_iota(jnp.int32, (2 * T, T), 1) < length
    first_head = lax.broadcasted_iota(jnp.int32, (T, 2 * HEAD), 1) < HEAD
    flip = (
        lax.broadcasted_iota(jnp.int32, (T, 4 * T), 0) + lax.broadcasted_iota(jnp.int32, (T, 4 * T), 1)
        == T - 1
    ).astype(f32).astype(bf16)

    def norm(i, x):
        centre = x - jnp.mean(x, -1, keepdims=True)
        rate = lax.rsqrt(jnp.mean(centre * centre, -1, keepdims=True) + EPSILON)
        hat = centre * rate
        XH[i] = hat
        RS[i] = jnp.broadcast_to(rate, RS.shape[1:])
        return hat * ng[i : i + 1] + nb[i : i + 1]

    def norm_back(i, grad):
        hat = XH[i]
        PBin[t, i : i + 1] = jnp.sum(grad * hat, 0, keepdims=True)
        PBin[t, 8 + i : 9 + i] = jnp.sum(grad, 0, keepdims=True)
        g = grad * ng[i : i + 1]
        return RS[i][:, 0:1] * (
            g - jnp.mean(g, -1, keepdims=True) - hat * jnp.mean(g * hat, -1, keepdims=True)
        )

    def pair_rows(v):
        return jnp.concatenate([jnp.where(first_head, v, 0.0), jnp.where(first_head, 0.0, v)], 0)

    def unpair(v):
        return jnp.where(first_head, v[:T], v[T:])

    own = pl.ds(base, T)

    @pl.when(s == 1)
    def _():
        for i in range(len(chunks)):
            gather(i, 1)
        arrived("hop", ARR)
        X[0] = ARR[...].astype(f32)

    @pl.when(s == 0)
    def _():
        X[0] = inputs[t]

    def feed(j, i, before, after):
        x = X[before]
        a = norm(i, x).astype(bf16)
        Nall[own, i * width : (i + 1) * width] = a
        first_only(6 * j)
        active = []
        for k in range(4):
            h = dot(a, Win[j, k])
            H[j, k] = h
            active.append((h * jax.nn.sigmoid(h)).astype(bf16))
        first_only(6 * j + 1)
        total = dot(active[0], Wout[j, 0])
        for k in range(1, 4):
            total += dot(active[k], Wout[j, k])
        X[after] = x + 0.5 * total

    feed(0, 0, 0, 1)

    x = X[1]
    a = norm(1, x).astype(bf16)
    Nall[own, width : 2 * width] = a
    for k in (1, 2, 3):
        arrived(("small", k), SM.at[:, cols(k)])
        arrived(("rel", k), R2.at[:, cols(k)])
    first_only(2)
    q = dot(a, Wqkv[0])
    QKV[0] = q + SM[0:1]
    QKV[1] = q + SM[1:2]
    QKV[2] = dot(a, Wqkv[1])
    QKV[3] = dot(a, Wqkv[2])
    mixed = []
    for p in range(4):
        c = pl.ds(2 * HEAD * p, 2 * HEAD)
        qu = pair_rows(QKV[0, :, c]).astype(bf16)
        qv = pair_rows(QKV[1, :, c]).astype(bf16)
        content = dot(qu, QKV[2, :, c].astype(bf16), 1, 1)
        whole = dot(qv, R2[:, c], 1, 1)
        placed = jnp.concatenate(
            [
                pltpu.roll(whole[e * T : (e + 1) * T], 4 * T - (T - 1), 1, stride=1, stride_axis=0)[:, :T]
                for e in range(2)
            ],
            0,
        )
        scores = jnp.where(key_mask, (content + placed) * HEAD ** (-0.5), -1e30)
        e = jnp.exp(scores - jnp.max(scores, -1, keepdims=True))
        probs = e / jnp.sum(e, -1, keepdims=True)
        PRB[p] = probs
        mixed.append(unpair(dot(probs.astype(bf16), QKV[3, :, c].astype(bf16))).astype(bf16))
    for k in range(4):
        SfSt[k, :, 0:C] = mixed[k]
    first_only(3)
    total = dot(mixed[0], Wo[0:C])
    for k in range(1, 4):
        total += dot(mixed[k], Wo[C * k : C * (k + 1)])
    x = x + total
    X[2] = x

    a = norm(2, x).astype(bf16)
    Nall[own, 2 * width : 3 * width] = a
    first_only(4)
    GVG[0] = dot(a, Wci[0])
    GVG[1] = dot(a, Wci[1])
    UP[margin : margin + T] = GVG[0] * jax.nn.sigmoid(GVG[1]) * row_mask
    for p in range(4):
        c = pl.ds(C * p, C)
        acc = SM[4:5, c] * UP[margin - taps // 2 : margin - taps // 2 + T, c]
        for k in range(1, taps):
            o = margin - taps // 2 + k
            acc += SM[4 + k : 5 + k, c] * UP[o : o + T, c]
        CT[:, c] = acc
    conv = CT[...]
    masked = conv * row_mask
    STF[d] = jnp.concatenate(
        [
            jnp.sum(masked, 0, keepdims=True),
            jnp.sum(masked * conv, 0, keepdims=True),
            jnp.broadcast_to(jnp.sum(row_mask, 0, keepdims=True), (1, width)),
            jnp.zeros((5, width), f32),
        ],
        0,
    )
    for r in range(1, dp):
        start(("bnf", r), STF.at[d], STF.at[d], zpeers[r])
    first_only(5)
    for r in range(1, dp):
        arrived(("bnf", r), STF.at[behind[r]])
    sums = STF[0]
    for r in range(1, dp):
        sums += STF[r]
    count = sums[2:3]
    bn_mean = sums[0:1] / count
    inv_std = lax.rsqrt(sums[1:2] / count - bn_mean * bn_mean + EPSILON)
    hat = (conv - bn_mean) * inv_std
    CT[...] = hat
    y = hat * SM[2:3] + SM[3:4]
    active = (y * jax.nn.sigmoid(y)).astype(bf16)
    for k in range(4):
        SfSt[k, :, C : 2 * C] = active[:, C * k : C * (k + 1)]
    x = X[2] + dot(active, Wco[...])
    X[3] = x

    feed(1, 3, 3, 4)

    out = (norm(4, X[4]) * row_mask).astype(bf16)
    HOP[...] = out

    @pl.when(s == 0)
    def _():
        start("hop", lambda: HOP, lambda: ARR, partner, 0)

    LO[pl.ds(trow, T)] = out
    for k in (1, 2, 3):
        mine = pl.ds(trow, T)
        start(("out", k), LO.at[mine], LO.at[mine], peers[k])

    def place(k):
        return pl.ds(base + T * PLACE[k], T)

    def to_tensor(name, ref, c):
        for k in (1, 2, 3):
            start((name, k), ref.at[own, c], ref.at[place(k), c], peers[k])

    def from_tensor(name, ref, c, which=(1, 2, 3)):
        for k in which:
            arrived((name, k), ref.at[place(k), c])

    def to_dp(name, ref, n, c, cond=None):
        for r in range(1, groups):
            there = lambda: ref.at[pl.ds(base, n), c]
            if cond is None:
                start((name, "z", r), there(), there(), zpeers[r])
            else:
                start((name, "z", r), there, there, zpeers[r], cond)

    def from_dp(name, ref, n, c):
        for r in range(1, groups):
            arrived((name, "z", r), ref.at[pl.ds(zbase[r], n), c])

    def to_core(name, ref, c, cond=None):
        for r in range(1, groups):
            src = lambda r=r: ref.at[pl.ds(zbase[r], 2 * T), c]
            dst = lambda r=r: ref.at[pl.ds(zhigh[r], 2 * T), c]
            if cond is None:
                start((name, "c", r), src(), dst(), sib)
            else:
                start((name, "c", r), src, dst, sib, cond)

    def from_core(name, ref, c):
        for r in range(1, groups):
            arrived((name, "c", r), ref.at[pl.ds(zhigh[r], 2 * T), c])

    def block(i):
        return pl.ds(i * width, width)

    every = pl.ds(0, 4 * width)
    sf_cols, sb_cols = pl.ds(0, 2 * C), pl.ds(0, 5 * C)
    to_tensor("n", Nall, every)
    Sf[own] = SfSt[0]
    for k in (1, 2, 3):
        start(("sf", k), SfSt.at[k], Sf.at[place(k)], peers[k])

    def spread_forward(cond):
        from_tensor("n", Nall, every)
        to_dp("n", Nall, 2 * T, every, cond)
        from_tensor("sf", Sf, sf_cols)
        to_dp("sf", Sf, R4, sf_cols, cond)

    @pl.when(s == 0)
    def _():
        spread_forward(0)
        from_dp("n", Nall, 2 * T, every)
        to_core("n", Nall, every, 0)
        arrived("back", ARR)
        X[0] = ARR[...].astype(f32)

    @pl.when(s == 1)
    def _():
        X[0] = cot[t]

    def feed_back(j, i, g):
        b = (0.5 * g).astype(bf16)
        Ball[own, i * width : (i + 1) * width] = b
        to_tensor(("b", i), Ball, block(i))
        grad = None
        for k in range(4):
            h = H[j, k]
            sig = jax.nn.sigmoid(h)
            hg = (dot(b, Wout[j, k], 1, 1) * (sig * (1.0 + h * (1.0 - sig)))).astype(bf16)
            part = dot(hg, Win[j, k], 1, 1)
            grad = part if grad is None else grad + part
        return g + norm_back(i, grad)

    g = norm_back(4, X[0] * row_mask)
    g = feed_back(1, 3, g)

    @pl.when(s == 1)
    def _():
        spread_forward(1)

    b = g.astype(bf16)
    Ball[own, 2 * width : 3 * width] = b
    to_tensor(("b", 2), Ball, block(2))
    hat = CT[...]
    y = hat * SM[2:3] + SM[3:4]
    sig = jax.nn.sigmoid(y)
    dy = dot(b, Wco[...], 1, 1) * (sig * (1.0 + y * (1.0 - sig)))
    PAst[2:3] = jnp.sum(dy * hat, 0, keepdims=True)
    PAst[3:4] = jnp.sum(dy, 0, keepdims=True)
    dhat = dy * SM[2:3]
    masked = dhat * row_mask
    STB[d] = jnp.concatenate(
        [
            jnp.sum(masked, 0, keepdims=True),
            jnp.sum(masked * hat, 0, keepdims=True),
            jnp.zeros((6, width), f32),
        ],
        0,
    )
    for r in range(1, dp):
        start(("bnb", r), STB.at[d], STB.at[d], zpeers[r])
    for r in range(1, dp):
        arrived(("bnb", r), STB.at[behind[r]])
    sums = STB[0]
    for r in range(1, dp):
        sums += STB[r]
    dc = inv_std * (dhat - (sums[0:1] + hat * sums[1:2]) / count) * row_mask
    DP[margin : margin + T] = dc
    from_tensor(("b", 3), Ball, block(3))
    to_dp(("b", 3), Ball, 2 * T, block(3))
    for p in range(4):
        c = pl.ds(C * p, C)
        here = DP[margin : margin + T, c]
        acc = None
        for k in range(taps):
            o = margin + taps // 2 - k
            term = SM[4 + k : 5 + k, c] * DP[o : o + T, c]
            acc = term if acc is None else acc + term
            o = margin - taps // 2 + k
            PAst[4 + k : 5 + k, c] = jnp.sum(here * UP[o : o + T, c], 0, keepdims=True)
        CT[:, c] = acc
    du = CT[...] * row_mask
    sig = jax.nn.sigmoid(GVG[1])
    dvalue = (du * sig).astype(bf16)
    dgate = (du * GVG[0] * (sig * (1.0 - sig))).astype(bf16)
    for k in range(4):
        SbSt[k, :, 3 * C : 4 * C] = dvalue[:, C * k : C * (k + 1)]
        SbSt[k, :, 4 * C : 5 * C] = dgate[:, C * k : C * (k + 1)]
    g = g + norm_back(2, dot(dvalue, Wci[0], 1, 1) + dot(dgate, Wci[1], 1, 1))

    b = g.astype(bf16)
    Ball[own, width : 2 * width] = b
    to_tensor(("b", 1), Ball, block(1))
    dmix = dot(b, Wo[...], 1, 1).astype(bf16).astype(f32)
    scale = HEAD ** (-0.5)
    dq, dk, dv = [], [], []
    for p in range(4):
        c = pl.ds(2 * HEAD * p, 2 * HEAD)
        qu = pair_rows(QKV[0, :, c]).astype(bf16)
        qv = pair_rows(QKV[1, :, c]).astype(bf16)
        key = QKV[2, :, c].astype(bf16)
        val = QKV[3, :, c].astype(bf16)
        do = pair_rows(dmix[:, 2 * HEAD * p : 2 * HEAD * (p + 1)]).astype(bf16)
        probs = PRB[p]
        dprob = dot(do, val, 1, 1)
        ds = (probs * (dprob - jnp.sum(probs * dprob, -1, keepdims=True))).astype(bf16)
        du_rows = unpair(dot(ds, key)) * scale
        turned = dot(ds, flip)
        whole = jnp.concatenate(
            [
                pltpu.roll(turned[e * T : (e + 1) * T], 0, 1, stride=1, stride_axis=0)[:, : 2 * T]
                for e in range(2)
            ],
            0,
        ).astype(bf16)
        dv_rows = unpair(dot(whole, R2[2 * T : 4 * T, c])) * scale
        dk.append((dot(ds, qu, 0, 0) * scale).astype(bf16))
        dv.append(dot(probs.astype(bf16), do, 0, 0).astype(bf16))
        dq.append((du_rows + dv_rows).astype(bf16))
        PAst[0:1, c] = jnp.sum(du_rows, 0, keepdims=True)
        PAst[1:2, c] = jnp.sum(dv_rows, 0, keepdims=True)
        drel = dot(whole, qv, 0, 0) * scale
        PAst[SMALL_ROWS : SMALL_ROWS + 2 * T, c] = drel.astype(bf16).astype(f32)
    for k in range(4):
        SbSt[k, :, 0:C] = dq[k]
        SbSt[k, :, C : 2 * C] = dk[k]
        SbSt[k, :, 2 * C : 3 * C] = dv[k]
    Sb[own] = SbSt[0]
    grad = dot(jnp.concatenate(dq, 1), Wqkv[0], 1, 1)
    grad += dot(jnp.concatenate(dk, 1), Wqkv[1], 1, 1)
    grad += dot(jnp.concatenate(dv, 1), Wqkv[2], 1, 1)
    g = g + norm_back(1, grad)

    g = feed_back(0, 0, g)
    low = g.astype(bf16)
    back_rows = lambda: IG.at[pl.ds(trow, T)]
    IG[pl.ds(trow, T)] = low

    @pl.when(s == 1)
    def _():
        start("back", back_rows, lambda: ARR, partner, 1)

    for k in (1, 2, 3):
        start(("grad", k), back_rows(), back_rows(), peers[k])
    for k in (1, 2, 3):
        start(("sb", k), SbSt.at[k], Sb.at[place(k)], peers[k])
        start(("pa", k), PAst.at[:, cols(k)], PAin.at[k], peers[k])
        start(("pb", k), PBin.at[t], PBin.at[t], peers[k])

    for i in (2, 1, 0):
        from_tensor(("b", i), Ball, block(i))
        to_dp(("b", i), Ball, 2 * T, block(i))
    from_tensor("sb", Sb, sb_cols)
    to_dp("sb", Sb, R4, sb_cols)
    PAin[0] = PAst[:, 0:C]
    for k in (1, 2, 3):
        arrived(("pa", k), PAin.at[k])
    mine = d if groups > 1 else 0
    PA[mine] = PAin[0] + PAin[1] + PAin[2] + PAin[3]
    for r in range(1, groups):
        start(("pa", "z", r), PA.at[d], PA.at[d], zpeers[r])
    for k in (1, 2, 3):
        arrived(("pb", k), PBin.at[t ^ k])
    PB[mine] = PBin[0] + PBin[1] + PBin[2] + PBin[3]
    for r in range(1, groups):
        start(("pb", "z", r), PB.at[d], PB.at[d], zpeers[r])

    @pl.when(s == 1)
    def _():
        from_dp("n", Nall, 2 * T, every)
        to_core("n", Nall, every, 1)

    for i in (3, 2, 1, 0):
        from_dp(("b", i), Ball, 2 * T, block(i))
        to_core(("b", i), Ball, block(i))
    from_dp("sf", Sf, R4, sf_cols)
    from_dp("sb", Sb, R4, sb_cols)
    for r in range(1, groups):
        arrived(("pa", "z", r), PA.at[behind[r]])
        arrived(("pb", "z", r), PB.at[behind[r]])
    for k in (1, 2, 3):
        theirs = pl.ds(pl.multiple_of((t ^ k) * T, T), T)
        arrived(("out", k), LO.at[theirs])
        arrived(("grad", k), IG.at[theirs])
    from_core("n", Nall, every)
    for i in (3, 2, 1, 0):
        from_core(("b", i), Ball, block(i))

    for cond, c in pending:
        if cond is None:
            c().wait_send()
    for which in (0, 1):

        @pl.when(s == which)
        def _():
            for cond, c in pending:
                if cond == which:
                    c().wait_send()


def on_device(
    inputs, lengths, cotangent, norm_gain, norm_bias, ffn_in, ffn_out, attn_in, pos_bias, attn_out,
    conv_in, depthwise, bn_gain, bn_shift, conv_out,
):
    dp = lax.axis_size("dp")
    group, frames, width = inputs.shape
    C = width // 4
    taps = depthwise.shape[1]
    groups = dp if dp <= 4 else 1
    R = groups * group * frames
    table = position_rows(frames, width)
    vm = pl.BlockSpec(memory_space=pltpu.VMEM)
    hbm = pl.BlockSpec(memory_space=pl.ANY)
    sm = pl.BlockSpec(memory_space=pltpu.SMEM)
    sums_rows = SMALL_ROWS + 2 * frames

    def shape(dims, dtype=bf16):
        return jax.ShapeDtypeStruct(dims, dtype)

    n_copies = 150 + 6 * (groups - 1) + 2 * dp
    operands = (
        lengths, inputs, cotangent, norm_gain[0], norm_bias[0], ffn_in[0], ffn_out[0], attn_in[0],
        attn_out[0], conv_in[0].transpose(1, 0, 2), conv_out[0], pos_bias[0], bn_gain, bn_shift,
        depthwise[0], table,
    )
    nall, ball, sf, sb, lo, ig, pa, pb = pl.pallas_call(
        lambda *refs: layer_kernel((frames, width, dp, groups), *refs),
        out_shape=[
            shape((R, 4 * width)), shape((R, 4 * width)), shape((R, 2 * C)), shape((R, 5 * C)),
            shape((group * frames, width)), shape((group * frames, width)),
            shape((groups, sums_rows, C), f32), shape((groups, 16, width), f32),
        ],
        in_specs=[sm, vm, vm, vm, vm, hbm, hbm, hbm, hbm, hbm, hbm, vm, vm, vm, vm, vm],
        out_specs=[vm] * 8,
        scratch_shapes=[
            pltpu.VMEM((2, 4, width, width), bf16),
            pltpu.VMEM((2, 4, width, width), bf16),
            pltpu.VMEM((3, width, width), bf16),
            pltpu.VMEM((width, C), bf16),
            pltpu.VMEM((width, width), bf16),
            pltpu.VMEM((2, width, width), bf16),
            pltpu.VMEM((width, width), bf16),
            pltpu.VMEM((4 * frames, width), bf16),
            pltpu.VMEM((SMALL_ROWS, width), f32),
            pltpu.VMEM((2, 4, frames, width), f32),
            pltpu.VMEM((5, frames, width), f32),
            pltpu.VMEM((5, frames, 128), f32),
            pltpu.VMEM((5, frames, width), f32),
            pltpu.VMEM((frames, width), bf16),
            pltpu.VMEM((frames, width), bf16),
            pltpu.VMEM((4, frames, width), f32),
            pltpu.VMEM((4, 2 * frames, frames), f32),
            pltpu.VMEM((2, frames, width), f32),
            pltpu.VMEM((frames, width), f32),
            pltpu.VMEM((frames + 32, width), f32),
            pltpu.VMEM((frames + 32, width), f32),
            pltpu.VMEM((4, frames, 2 * C), bf16),
            pltpu.VMEM((4, frames, 5 * C), bf16),
            pltpu.VMEM((sums_rows, width), f32),
            pltpu.VMEM((4, sums_rows, C), f32),
            pltpu.VMEM((4, 16, width), f32),
            pltpu.VMEM((dp, 8, width), f32),
            pltpu.VMEM((dp, 8, width), f32),
            pltpu.SemaphoreType.DMA((n_copies,)),
            pltpu.SemaphoreType.DMA((n_copies,)),
            pltpu.SemaphoreType.DMA((9,)),
        ],
        compiler_params=pltpu.CompilerParams(
            collective_id=0, has_side_effects=True, vmem_limit_bytes=48 * 2**20
        ),
    )(*operands)

    def part(ref, i, n):
        return ref[:, i * n : (i + 1) * n]

    def feed_grads(j, i):
        n, b = part(nall, i, width), part(ball, i, width)
        h = dot(n, ffn_in[0, j])
        sig = jax.nn.sigmoid(h)
        active = (h * sig).astype(bf16)
        hg = (dot(b, ffn_out[0, j], 1, 1) * (sig * (1.0 + h * (1.0 - sig)))).astype(bf16)
        return dot(n, hg, 0, 0), dot(active, b, 0, 0)

    in0, out0 = feed_grads(0, 0)
    in1, out1 = feed_grads(1, 3)
    pa, pb = jnp.sum(pa, 0), jnp.sum(pb, 0)
    n1, n2 = part(nall, 1, width), part(nall, 2, width)
    qkv = [dot(n1, part(sb, i, C), 0, 0) for i in range(3)]
    rel = dot(table[2 * frames :], pa[SMALL_ROWS:].astype(bf16), 0, 0)
    gates = [dot(n2, part(sb, i, C), 0, 0) for i in (3, 4)]
    grads = [
        pb[0:5], pb[8:13], jnp.stack([in0, in1]), jnp.stack([out0, out1]), jnp.stack(qkv + [rel]),
        pa[0:2], dot(part(sf, 0, C), part(ball, 1, width), 0, 0), jnp.stack(gates, 1),
        pa[4 : 4 + taps], pa[2], pa[3], dot(part(sf, 1, C), part(ball, 2, width), 0, 0),
    ]
    if groups == 1:
        grads = [lax.psum(m.astype(bf16), "dp").astype(f32) for m in grads]
    rows = (group, frames, width)
    outs = [lo.reshape(rows).astype(f32), ig.reshape(rows).astype(f32)] + grads
    return tuple(m[None] for m in outs)


def solution(mesh):
    placed = (
        P("dp", None, None),
        P("dp"),
        P("dp", None, None),
        P("section", None, None),
        P("section", None, None),
        P("section", None, None, "tensor"),
        P("section", None, "tensor", None),
        P("section", None, None, "tensor"),
        P("section", None, "tensor"),
        P("section", "tensor", None),
        P("section", None, None, "tensor"),
        P("section", None, "tensor"),
        P("section", "tensor"),
        P("section", "tensor"),
        P("section", "tensor", None),
    )
    return jax.shard_map(
        on_device,
        mesh=mesh,
        in_specs=placed,
        out_specs=(
            P("section", "dp", None, None),
            P("section", "dp", None, None),
            P("section", None, None),
            P("section", None, None),
            P("section", None, None, "tensor"),
            P("section", None, "tensor", None),
            P("section", None, None, "tensor"),
            P("section", None, "tensor"),
            P("section", "tensor", None),
            P("section", None, None, "tensor"),
            P("section", None, "tensor"),
            P("section", "tensor"),
            P("section", "tensor"),
            P("section", "tensor", None),
        ),
        check_vma=False,
    )
```

time: 1840 us -> 217 us (0.12); the launches traced: 1810 us -> 216 us
  blocking collectives: 570 us -> 0 us
  local copies, waits for them, and re-layouts: 563 us -> 19.8 us
  other arithmetic: 280 us -> 6.2 us
  matrix products: 277 us -> 16.8 us
  Pallas kernels: 0 us -> 172 us
  waiting for transfers between devices: 85.5 us -> 0 us
  starting transfers between devices: 18.9 us -> 0 us
  between operations: 19.3 us -> 0.77 us
    psum x51 -> x0, blocking collectives: 570 us -> none  [the longest x20 226 us: finish(): lax.psum(partial_sum.astype(jnp.bfloat16), 'tensor').astype(jnp.float32)]
    gather x43 -> x0, local copies, waits for them, and re-layouts: 417 us -> none  [the longest x11 225 us: attention_backward(): jnp.take_along_axis(padded, jnp.broadcast_to(back_index[None], (padded.sh...]
    dot_general x236 -> x14, matrix products: 258 us -> 16.8 us  [dot(): lax.dot_general(left, right, (((left_dim,), (right_dim,)), ((), ())), pre...]
    pallas_call x0 -> x1, Pallas kernels: none -> 172 us  [on_device(): pl.pallas_call(lambda *refs: layer_kernel((frames, width, dp, groups), *r...]
    reduce_sum x122 -> x2, other arithmetic: 108 us -> 0.64 us  [on_device(): pa, pb = (jnp.sum(pa, 0), jnp.sum(pb, 0))]
    psum x1 -> x0, waiting for transfers between devices: 85.2 us -> none  [on_device(): lax.psum(totals[7].astype(jnp.bfloat16), 'dp').astype(jnp.float32)]
    reshape x46 -> x0, local copies, waits for them, and re-layouts: 49.8 us -> none  [split_heads(): return member.reshape(member.shape[0], -1, HEAD).transpose(1, 0, 2)]
    div x100 -> x0, other arithmetic: 32.8 us -> none  [the longest x75 18 us: layer_norm(): centre = states - jnp.mean(states, -1, keepdims=True)]
  transfers between devices with their start and end apart: 9 -> 0, of which waited for: 4 -> 0; matrix products, arithmetic and copies ran while one was open for 11% -> 0% of each run, Pallas kernels for 0% -> 0%
where the time goes in v1:
time: 217 us; the launch traced here: 216 us
  Pallas kernels  172 us (79%)
  local copies, waits for them, and re-layouts  19.8 us (9%)
  matrix products  16.8 us (8%)
  other arithmetic  6.2 us (3%)
    pallas_call x1, Pallas kernels, on_device(): pl.pallas_call(lambda *refs: layer_kernel((frames, width, dp, groups), *r...  172 us
    dot_general x14, matrix products, dot(): lax.dot_general(left, right, (((left_dim,), (right_dim,)), ((), ())), pre...  16.8 us
    unnamed x40, local copies, waits for them, and re-layouts  16 us

profile of v1, /device:TPU:0, one launch (start us, length us, event | category | flops | bytes accessed | tf_op | source)
XLA Modules:
  0.0 215.7 jit_solution(10010419563890694358)
XLA Ops:
  0.6 0.7 copy.40
  1.4 0.7 copy_bitcast_fusion.2
  2.1 1.0 copy.39
  3.1 0.0 copy-start
  3.1 1.2 copy-done
  4.3 1.2 copy-done.2
  5.5 1.0 copy-done.4
  6.6 0.9 copy-done.5
  7.5 0.9 copy-done.6
  8.5 0.9 copy-done.7
  9.4 0.9 copy-done.8
  10.3 0.9 copy-done.9
  11.2 0.7 copy-done.10
  11.9 0.7 copy-done.11
  12.5 0.7 copy-done.12
  13.2 0.7 copy-done.13
  13.8 172.0 %shard_map.263 = (bf16[512,2048]{1,0:T(8,128)(2,1)}, bf16[512,2048]{1,0:T(8,128)(2,1)}, bf16[512,256]{1,0:T(8,128)(2,1)S(1)}, bf16[512,640]{1,0:T(8,128)(2,1)S(1...) custom-call(s32[4]{0:T(128)S(1)} %copy-done.11, ...), custom_call_target="tpu_custom_call" | custom-call | tf_op jit(solution)/shard_map/pallas_call | solution.py:619
  185.9 0.6 reduce_sum.18
  186.5 0.9 fusion.57
  187.4 0.6 broadcast_in_dim.33
  188.0 0.6 slice_bitcast_fusion
  188.6 0.5 fusion.56
  189.1 0.6 broadcast_in_dim.32
  189.7 0.6 broadcast_in_dim.40
  190.3 0.7 convert.7
  191.1 0.7 convert.6
  191.8 1.0 convolution_bitcast_fusion.11
  192.8 2.0 convolution_bitcast_fusion.4
  194.8 2.0 convolution_bitcast_fusion.7
  196.8 0.3 convolution_bitcast_fusion.5
  197.2 0.3 convolution_bitcast_fusion.6
  197.5 1.2 copy.31
  198.7 0.3 convolution_bitcast_fusion.8
  199.1 0.0 copy-start.1
  199.1 0.3 convolution_bitcast_fusion.9
  199.4 0.3 convolution_bitcast_fusion.10
  199.8 1.0 maximum_bitcast_fusion.2
  200.8 0.6 copy-done.17
  201.4 0.4 fusion.10
  201.8 0.4 fusion.14
  202.3 0.3 copy-done.3
  202.6 3.1 %convolution_bitcast_fusion.3 = f32[1,512,512]{2,1,0:T(8,128)} fusion(f32[512,512]{1,0:T(8,128)S(1)} %fusion.14, bf16[1,2,512,512]{3,2,1,0:T(8,128)(2,1)S(1)} %copy-done.3, bf16[512,2048]{1,0:T(8,128)(2,1)} %get-tuple-element.26, bf16[512,2048]{1,0:T(8,128)(2,1)} %get-tuple-element.25), kind=kOutput, calls=%fused_computation.6 | convolution fusion | flops 539230208 | bytes 3670016 | tf_op jit(solution)/shard_map/dot_general | solution.py:20
  205.7 3.1 %convolution_bitcast_fusion.2 = f32[1,512,512]{2,1,0:T(8,128)} fusion(f32[512,512]{1,0:T(8,128)S(1)} %fusion.10, bf16[1,2,512,512]{3,2,1,0:T(8,128)(2,1)S(1)} %copy-done.3, bf16[512,2048]{1,0:T(8,128)(2,1)} %get-tuple-element.26, bf16[512,2048]{1,0:T(8,128)(2,1)} %get-tuple-element.25), kind=kOutput, calls=%fused_computation.4 | convolution fusion | flops 539230208 | bytes 3670016 | tf_op jit(solution)/shard_map/dot_general | solution.py:20
  208.8 1.5 convolution_bitcast_fusion
  210.3 1.5 convolution_bitcast_fusion.1
  211.9 1.5 maximum_bitcast_fusion.1
  213.4 0.7 copy-done.15
  214.2 1.5 maximum_bitcast_fusion
  (22 shorter events, 0.1 us)
Async XLA Ops:
  3.1 1.2 copy-start
  4.3 1.2 copy-start.2
  5.5 1.0 copy-start.4
  6.6 0.9 copy-start.5
  7.5 0.9 copy-start.6
  8.5 0.9 copy-start.7
  9.4 0.9 copy-start.8
  10.3 0.9 copy-start.9
  11.2 0.7 copy-start.10
  11.9 0.7 copy-start.11
  12.5 0.7 copy-start.12
  13.2 0.7 copy-start.13
  186.5 10.3 %copy-start.16 = (bf16[512,2048]{1,0:T(8,128)(2,1)S(1)}, bf16[512,2048]{1,0:T(8,128)(2,1)}, u32[]{:S(2)}) copy-start(bf16[512,2048]{1,0:T(8,128)(2,1)} %get-tuple-element.25) | copy-start | bytes 6291460
  199.1 1.7 copy-start.1
  199.1 2.3 %copy-start.17 = (bf16[512,2048]{1,0:T(8,128)(2,1)S(1)}, bf16[512,2048]{1,0:T(8,128)(2,1)}, u32[]{:S(2)}) copy-start(bf16[512,2048]{1,0:T(8,128)(2,1)} %get-tuple-element.25) | copy-start | bytes 6291460
  201.4 1.2 copy-start.3
  211.9 1.6 copy-start.14
  211.9 2.3 %copy-start.15 = (f32[1,512,512]{2,1,0:T(8,128)S(1)}, f32[1,512,512]{2,1,0:T(8,128)}, u32[]{:S(2)}) copy-start(f32[1,512,512]{2,1,0:T(8,128)} %convolution_bitcast_fusion.2) | copy-start | bytes 3145732

commit v2 on v1

v2 whole, which is shorter than its diff:
```python
import math

import jax
import jax.numpy as jnp
import numpy as np
from jax import lax
from jax.experimental import pallas as pl
from jax.experimental.pallas import tpu as pltpu
from jax.sharding import PartitionSpec as P

HEAD = 64
EPSILON = 1e-05
MESH = pl.DeviceIdType.MESH
SECTION, TENSOR, DATA = "section", "tensor", "dp"
PLACE = (0, 2, 1, 3)
SMALL_ROWS = 48
bf16, f32 = jnp.bfloat16, jnp.float32


def dot(left, right, left_dim=1, right_dim=0):
    return lax.dot_general(
        left, right, (((left_dim,), (right_dim,)), ((), ())), preferred_element_type=f32
    )


def position_rows(frames, width):
    offset = np.arange(2 * frames - 1, dtype=np.float32) - np.float32(frames - 1)
    rates = np.exp(
        np.arange(width // 2, dtype=np.float32) * np.float32(-2.0 * math.log(10000.0) / width)
    )
    angles = (offset[:, None] * rates[None, :]).astype(np.float32)
    table = np.stack([np.sin(angles), np.cos(angles)], -1).reshape(2 * frames - 1, width)
    blank = np.zeros((1, width), np.float32)
    return jnp.asarray(np.concatenate([table[::-1], blank, table, blank]), bf16)


def layer_kernel(dims, *refs):
    T, width, dp, groups = dims
    C = width // 4
    (lengths, inputs, cot, ng_in, nb_in, fin, fout, ain, aout, cin, cout, pos_in, bng_in, bns_in, dw_in, e2_in) = refs[:16]
    (Nall, Ball, Sf, Sb, LO, IG, PA, PB) = refs[16:24]
    (Win, Wout, Wqkv, Wr, Wo, Wci, Wco, R2, SM) = refs[24:33]
    (H, XH, RS, X, G, ARR, HOP, QKV, PRB, GVG, CT, UP, DP) = refs[33:46]
    (SfSt, SbSt, PAst, PAb, PAin, PBst, PBin, STF, STB, RSst, RSin) = refs[46:57]
    (ng, nb, pos, bng, bns, dw, e2, lens, pairs, spread) = refs[57:67]
    ss, rs, ls = refs[67:70]

    s, t, d = lax.axis_index(SECTION), lax.axis_index(TENSOR), lax.axis_index(DATA)
    first, second = s == 0, s == 1
    taps = dw.shape[0]
    peers = [(s, t ^ k, d) for k in range(4)]
    sib, yp = peers[1], peers[2]
    around = {j: lax.rem(d + j + dp, dp) for j in range(1 - dp, dp)}
    zpeers = [(s, t, around[r]) for r in range(dp)]
    zpair = (s, t, d ^ 1)
    partner = (1 - s, t, d)
    half = lax.rem(d, 2)
    R4 = 4 * T
    reach = range(1 - groups, groups)
    base_of = {j: pl.multiple_of(around[j] * R4, R4) if groups > 1 else 0 for j in reach}
    second_of, high_of, last_of = (
        {j: pl.multiple_of(around[j] * R4 + n * T, T) if groups > 1 else n * T for j in reach} for n in (1, 2, 3)
    )
    there = {j: d + j >= 0 if j < 0 else d + j <= dp - 1 for j in reach}
    through = {
        (j, to): there[j] & there[to] for j in reach for to in (1, -1) if j * to < 0 and groups > 1
    }
    base = base_of[0]
    trow = pl.multiple_of(t * T, T)
    mine = d if groups > 1 else 0

    index, pending = {}, {}

    def copy_of(key, src, dst, dev):
        i = index.setdefault(key, len(index))
        return pltpu.make_async_remote_copy(
            src_ref=src, dst_ref=dst, send_sem=ss.at[i], recv_sem=rs.at[i],
            device_id=dev, device_id_type=MESH,
        )

    def start(key, src, dst, dev, cond=None):
        again = lambda: copy_of(key, src(), dst(), dev)
        again().start()
        pending[key] = (cond, again)

    def arrived(key, dst):
        copy_of(key, dst, dst, partner).wait_recv()

    locals_ = {}

    def fetch(name, src, dst):
        locals_[name] = lambda: pltpu.make_async_copy(src(), dst(), ls.at[list(locals_).index(name)])
        locals_[name]().start()

    def fetched(*names):
        for name in names:
            locals_[name]().wait()

    @pl.when(first)
    def _():
        pltpu.make_async_copy(inputs.at[t], X.at[0], ls.at[20]).start()

    @pl.when(second)
    def _():
        pltpu.make_async_copy(cot.at[t], G, ls.at[20]).start()

    fetch("ng", lambda: ng_in, lambda: ng)
    fetch("nb", lambda: nb_in, lambda: nb)
    fetch("in0", lambda: fin.at[0], lambda: Win.at[0, 0])
    fetch("out0", lambda: fout.at[0], lambda: Wout.at[0, 0])
    fetch("wr", lambda: ain.at[3], lambda: Wr)
    fetch("e2", lambda: e2_in, lambda: e2)
    fetch("pos", lambda: pos_in, lambda: pos)
    fetch("bng", lambda: bng_in, lambda: bng)
    fetch("bns", lambda: bns_in, lambda: bns)
    fetch("dw", lambda: dw_in, lambda: dw)
    fetch("len", lambda: lengths, lambda: lens)
    fetch("qkv", lambda: ain.at[pl.ds(0, 3)], lambda: Wqkv.at[:, :, pl.ds(0, C)])
    fetch("o", lambda: aout, lambda: Wo.at[pl.ds(0, C)])
    fetch("ci", lambda: cin, lambda: pairs)
    fetch("co", lambda: cout, lambda: Wco.at[pl.ds(0, C)])
    fetch("in1", lambda: fin.at[1], lambda: Win.at[1, 0])
    fetch("out1", lambda: fout.at[1], lambda: Wout.at[1, 0])

    barrier = pltpu.get_barrier_semaphore()
    greet = peers[1:] + zpeers[1:] + [partner]
    for dev in greet:
        pl.semaphore_signal(barrier, inc=1, device_id=dev, device_id_type=MESH)
    pl.semaphore_wait(barrier, len(greet))

    starts = {}

    def lines(first_row, n, which):
        if which is None:
            return pl.ds(first_row, n)
        at = (first_row, n, which)
        if at not in starts:
            starts[at] = pl.multiple_of(first_row + n // 2 * (half if which == "own" else 1 - half), n // 2)
        return pl.ds(starts[at], n // 2)

    def cols(k):
        return pl.ds(C * k, C)

    def feed_chunks(j):
        Q = width // 2
        return [
            (
                lambda w, src=src, q=q: src.at[j, lines(Q * q, Q, w)],
                lambda k, w, dst=dst, q=q: dst.at[j, k, lines(Q * q, Q, w)],
            )
            for src, dst in ((fin, Win), (fout, Wout))
            for q in range(2)
        ]

    def row_chunk(src, dst):
        return [(lambda w: src.at[lines(0, C, w)], lambda k, w: dst.at[lines(C * k, C, w)])]

    def column_chunks(src, dst, n):
        return [
            (lambda w, i=i: src(i, lines(0, width, w)), lambda k, w, i=i: dst.at[i, lines(0, width, w), cols(k)])
            for i in range(n)
        ]

    chunks = (
        feed_chunks(0)
        + column_chunks(lambda i, rows: ain.at[i, rows], Wqkv, 3)
        + row_chunk(aout, Wo)
        + column_chunks(lambda i, rows: Wci.at[i, rows, cols(0)], Wci, 2)
        + row_chunk(cout, Wco)
        + feed_chunks(1)
    )
    for n, at in ((width // 2, 0), (width // 2, width // 2), (width, 0)) + tuple((C, C * k) for k in range(4)):
        for w in ("own", "other"):
            lines(at, n, w)
    only = {i: second for i in range(4)}

    def send_chunks(names):
        for i in names:
            src, dst = chunks[i]
            start(("sib", i), lambda src=src: src(None), lambda dst=dst: dst(1, None), sib, only.get(i))
            start(("y", i), lambda src=src: src("own"), lambda dst=dst: dst(2, "own"), yp, only.get(i))

    def step_a(i):
        dst = chunks[i][1]
        arrived(("y", i), dst(2, "own"))
        start(("z", i), lambda: dst(2, "own"), lambda: dst(2, "own"), zpair, only.get(i))
        start(("sib2", i), lambda: dst(2, "own"), lambda: dst(3, "own"), sib, only.get(i))

    def step_b(i):
        dst = chunks[i][1]
        arrived(("z", i), dst(2, "other"))
        start(("sib3", i), lambda: dst(2, "other"), lambda: dst(3, "other"), sib, only.get(i))

    def step_c(i):
        dst = chunks[i][1]
        arrived(("sib", i), dst(1, None))
        arrived(("sib2", i), dst(3, "own"))
        arrived(("sib3", i), dst(3, "other"))

    def steps(cond, *plan):
        @pl.when(cond)
        def _():
            for step, i in plan:
                step(i)

    A, B, W = step_a, step_b, step_c

    def norm(i, x):
        centre = x - jnp.mean(x, -1, keepdims=True)
        rate = lax.rsqrt(jnp.mean(centre * centre, -1, keepdims=True) + EPSILON)
        hat = centre * rate
        XH[i] = hat
        RS[i] = jnp.broadcast_to(rate, RS.shape[1:])
        return hat * ng[i] + nb[i]

    def norm_back(i, grad):
        hat = XH[i]
        PBst[i : i + 1] = jnp.sum(grad * hat, 0, keepdims=True)
        PBst[8 + i : 9 + i] = jnp.sum(grad, 0, keepdims=True)
        g = grad * ng[i]
        return RS[i][:, 0:1] * (
            g - jnp.mean(g, -1, keepdims=True) - hat * jnp.mean(g * hat, -1, keepdims=True)
        )

    def silu(h):
        return h * jax.nn.sigmoid(h)

    def place(k):
        return pl.ds(base + T * PLACE[k], T)

    own, four = pl.ds(base, T), pl.ds(base, R4)

    def block(i, n=1):
        return pl.ds(i * width, n * width)

    def to_tensor(name, ref, c):
        for k in (1, 2, 3):
            start((name, k), lambda: ref.at[own, c], lambda k=k: ref.at[place(k), c], peers[k])

    def from_tensor(name, ref, c, which=(1, 2, 3)):
        for k in which:
            arrived((name, k), ref.at[place(k), c])

    def feed(j, i, before, after):
        x = X[before]
        a = norm(i, x).astype(bf16)
        Nall[own, i * width : (i + 1) * width] = a
        to_tensor(("n", i), Nall, block(i))
        active = []
        for k in range(4):
            h = dot(a, Win[j, k])
            H[j, k] = h
            active.append(silu(h).astype(bf16))
        total = dot(active[0], Wout[j, 0])
        for k in range(1, 4):
            total += dot(active[k], Wout[j, k])
        X[after] = x + 0.5 * total

    def sum_to_owner(name, slot, total):
        for k in (1, 2, 3):
            RSst[slot, k - 1] = total[T * PLACE[k] : T * (PLACE[k] + 1)].astype(bf16)
        for k in (1, 2, 3):
            start(
                (name, k), lambda k=k: RSst.at[slot, k - 1], lambda k=k: RSin.at[slot, k - 1], peers[k], first
            )
        return total[0:T]

    def summed_here(name, slot, total):
        for k in (1, 2, 3):
            arrived((name, k), RSin.at[slot, k - 1])
            total += RSin[slot, k - 1].astype(f32)
        return total

    def shared_feed(j, i):
        from_tensor(("n", i), Nall, block(i))
        active = silu(dot(Nall[four, i * width : (i + 1) * width], Win[j, 0])).astype(bf16)
        return sum_to_owner(("s", j), j, dot(active, Wout[j, 0]))

    fetched("ng", "nb")

    @pl.when(first)
    def _():
        send_chunks((4,))
        pltpu.make_async_copy(inputs.at[t], X.at[0], ls.at[20]).wait()
        Nall[own, 0:width] = norm(0, X[0]).astype(bf16)
        to_tensor(("n", 0), Nall, block(0))
        send_chunks((5,))

    @pl.when(second)
    def _():
        send_chunks(range(4))
        pltpu.make_async_copy(cot.at[t], G, ls.at[20]).wait()

    fetched("in0", "out0")

    @pl.when(first)
    def _():
        X[1] = shared_feed(0, 0)
        send_chunks((6,))
        step_a(4)

    fetched("pos", "bng", "bns", "dw", "wr", "e2", "len", "ci")
    spread[...] = pairs[...].astype(f32)
    for i in range(2):
        Wci[i, :, 0:C] = spread[pl.ds(i, width, stride=2), :].astype(bf16)
    SM[:, 0:C] = jnp.zeros((SMALL_ROWS, C), f32)
    SM[0:2, 0:C] = pos[...]
    SM[2:3, 0:C] = bng[...]
    SM[3:4, 0:C] = bns[...]
    for k in range(taps):
        SM[4 + k : 5 + k, 0:C] = dw[k]
    R2[:, 0:C] = dot(e2[...], Wr[...]).astype(bf16)
    for k in (1, 2, 3):
        start(("small", k), lambda: SM.at[:, cols(0)], lambda k=k: SM.at[:, cols(k)], peers[k])
        start(("rel", k), lambda: R2.at[:, cols(0)], lambda k=k: R2.at[:, cols(k)], peers[k])
    @pl.when(first)
    def _():
        send_chunks(range(7, 13))
        step_a(5)
        X[1] = X[0] + 0.5 * summed_here(("s", 0), 0, X[1])
        step_a(6)
        step_b(4)
        step_b(5)

    @pl.when(second)
    def _():
        send_chunks(range(4, 15))

    fetched("qkv", "o", "co", "in1", "out1")
    margin = 16
    UP[...] = jnp.zeros(UP.shape, f32)
    DP[...] = jnp.zeros(DP.shape, f32)
    PAst[...] = jnp.zeros(PAst.shape, f32)
    PBst[...] = jnp.zeros(PBst.shape, f32)

    length = lens[t]
    row_mask = (lax.broadcasted_iota(jnp.int32, (T, 1), 0) < length).astype(f32)
    key_mask = lax.broadcasted_iota(jnp.int32, (2 * T, T), 1) < length
    first_head = lax.broadcasted_iota(jnp.int32, (T, 2 * HEAD), 1) < HEAD
    flip = (
        lax.broadcasted_iota(jnp.int32, (T, 4 * T), 0) + lax.broadcasted_iota(jnp.int32, (T, 4 * T), 1)
        == T - 1
    ).astype(f32).astype(bf16)

    def pair_rows(v):
        return jnp.concatenate([jnp.where(first_head, v, 0.0), jnp.where(first_head, 0.0, v)], 0)

    def unpair(v):
        return jnp.where(first_head, v[:T], v[T:])

    @pl.when(second)
    def _():
        for i in range(14):
            step_a(i)
            if i > 1:
                step_b(i - 2)
        for i in range(7):
            step_c(i)
        arrived("hop", ARR)
        X[0] = ARR[...].astype(f32)
        feed(0, 0, 0, 1)

    def send_rows_second(i):
        @pl.when(second)
        def _():
            to_tensor(("n", i), Nall, block(i))

    x = X[1]
    a = norm(1, x).astype(bf16)
    Nall[own, width : 2 * width] = a
    send_rows_second(1)
    steps(first, (W, 4), (W, 5))
    for k in (1, 2, 3):
        arrived(("small", k), SM.at[:, cols(k)])
        arrived(("rel", k), R2.at[:, cols(k)])
    steps(first, (A, 7), (B, 6), (W, 6))
    q = dot(a, Wqkv[0])
    QKV[0] = q + SM[0:1]
    QKV[1] = q + SM[1:2]
    QKV[2] = dot(a, Wqkv[1])
    QKV[3] = dot(a, Wqkv[2])
    mixed = []
    for p in range(4):
        c = pl.ds(2 * HEAD * p, 2 * HEAD)
        qu = pair_rows(QKV[0, :, c]).astype(bf16)
        qv = pair_rows(QKV[1, :, c]).astype(bf16)
        content = dot(qu, QKV[2, :, c].astype(bf16), 1, 1)
        whole = dot(qv, R2[:, c], 1, 1)
        placed = jnp.concatenate(
            [
                pltpu.roll(whole[e * T : (e + 1) * T], 4 * T - (T - 1), 1, stride=1, stride_axis=0)[:, :T]
                for e in range(2)
            ],
            0,
        )
        scores = jnp.where(key_mask, (content + placed) * HEAD ** (-0.5), -1e30)
        e = jnp.exp(scores - jnp.max(scores, -1, keepdims=True))
        probs = e / jnp.sum(e, -1, keepdims=True)
        PRB[p] = probs
        mixed.append(unpair(dot(probs.astype(bf16), QKV[3, :, c].astype(bf16))).astype(bf16))
    for k in range(4):
        SfSt[k, :, 0:C] = mixed[k]
    steps(first, (A, 8), (B, 7), (A, 9))
    step_c(7)
    steps(second, (A, 14), (B, 12))
    total = dot(mixed[0], Wo[0:C])
    for k in range(1, 4):
        total += dot(mixed[k], Wo[C * k : C * (k + 1)])
    x = x + total
    X[2] = x

    a = norm(2, x).astype(bf16)
    Nall[own, 2 * width : 3 * width] = a
    send_rows_second(2)
    steps(first, (B, 8), (A, 10), (B, 9))
    step_c(8)
    step_c(9)
    GVG[0] = dot(a, Wci[0])
    GVG[1] = dot(a, Wci[1])
    UP[margin : margin + T] = GVG[0] * jax.nn.sigmoid(GVG[1]) * row_mask
    for p in range(4):
        c = pl.ds(C * p, C)
        acc = SM[4:5, c] * UP[margin - taps // 2 : margin - taps // 2 + T, c]
        for k in range(1, taps):
            o = margin - taps // 2 + k
            acc += SM[4 + k : 5 + k, c] * UP[o : o + T, c]
        CT[:, c] = acc
    conv = CT[...]

    def dp_sums(name, ref, rows):
        n = len(rows)
        ref[d] = jnp.concatenate(rows + [jnp.zeros((8 - n, width), f32)], 0)
        for r in range(1, dp):
            start((name, r), lambda: ref.at[d], lambda: ref.at[d], zpeers[r])

    def summed(name, ref):
        for r in range(1, dp):
            arrived((name, r), ref.at[around[-r]])
        total = ref[0]
        for r in range(1, dp):
            total += ref[r]
        return total

    def total_of(v):
        return jnp.sum(v, 0, keepdims=True)

    masked = conv * row_mask
    frames_row = jnp.broadcast_to(total_of(row_mask), (1, width))
    dp_sums("bnf", STF, [total_of(masked), total_of(masked * conv), frames_row])
    steps(first, (B, 10))
    step_c(10)
    sums = summed("bnf", STF)
    count = sums[2:3]
    bn_mean = sums[0:1] / count
    inv_std = lax.rsqrt(sums[1:2] / count - bn_mean * bn_mean + EPSILON)
    hat = (conv - bn_mean) * inv_std
    CT[...] = hat
    active = silu(hat * SM[2:3] + SM[3:4]).astype(bf16)
    for k in range(4):
        SfSt[k, :, C : 2 * C] = active[:, C * k : C * (k + 1)]
    X[3] = X[2] + dot(active, Wco[...])

    @pl.when(first)
    def _():
        Nall[own, 3 * width : 4 * width] = norm(3, X[3]).astype(bf16)
        to_tensor(("n", 3), Nall, block(3))
        total = shared_feed(1, 3)
        send_chunks((13, 14))
        step_a(11)
        step_a(12)
        X[4] = X[3] + 0.5 * summed_here(("s", 1), 1, total)

    @pl.when(second)
    def _():
        for i in (13, 14):
            step_b(i)
        for i in range(11, 15):
            step_c(i)
        feed(1, 3, 3, 4)
    out = (norm(4, X[4]) * row_mask).astype(bf16)
    HOP[...] = out

    @pl.when(first)
    def _():
        start("hop", lambda: HOP, lambda: ARR, partner, first)

    LO[pl.ds(trow, T)] = out
    out_rows = lambda: LO.at[pl.ds(trow, T)]
    for k in (1, 2, 3):
        start(("out", k), out_rows, out_rows, peers[k])

    def line_start(name, region):
        for way, to, back in (("up", 1, -1), ("down", -1, 1)):
            if groups > 1:

                @pl.when(there[to])
                def _():
                    start((name, way, 1), lambda: region(0), lambda: region(0), (s, t, around[to]), there[to])

    def line_hop(name, region, n, after=None):
        for way, to, back in (("up", 1, -1), ("down", -1, 1)):
            if n < groups:

                @pl.when(there[back * n])
                def _():
                    j = back * n
                    arrived((name, way, n), region(j))
                    if n + 1 < groups:

                        @pl.when(there[to])
                        def _():
                            start(
                                (name, way, n + 1), lambda: region(j), lambda: region(j),
                                (s, t, around[to]), through[j, to],
                            )

                    if after is not None:
                        after(name, j)

    def rows_region(ref, n, c):
        return lambda j: ref.at[pl.ds(base_of[j], n), c]

    def share(ref, c):
        def go(name, j):
            rows = lambda: ref.at[pl.ds(base_of[j], T), c]
            start((name, "y", j), rows, lambda: ref.at[pl.ds(second_of[j], T), c], yp, there[j])
            start((name, "core", j), rows, lambda: ref.at[pl.ds(high_of[j], T), c], sib, there[j])

        return go

    def share_on(name, ref, c, n):
        for j in (n, -n):
            if n < groups:

                @pl.when(there[j])
                def _():
                    rows = lambda: ref.at[pl.ds(second_of[j], T), c]
                    arrived((name, "y", j), rows())
                    start((name, "core2", j), rows, lambda: ref.at[pl.ds(last_of[j], T), c], sib, there[j])

    def shared(name, ref, c):
        for j in reach:
            if j:

                @pl.when(there[j])
                def _():
                    arrived((name, "core", j), ref.at[pl.ds(high_of[j], T), c])
                    arrived((name, "core2", j), ref.at[pl.ds(last_of[j], T), c])

    every = block(0, 4)
    sf_cols = pl.ds(0, 2 * C)
    qkv_cols, gate_cols = pl.ds(0, 3 * C), pl.ds(3 * C, 2 * C)
    lines_of = {
        "n": (rows_region(Nall, T, every), share(Nall, every)),
        "sf": (rows_region(Sf, R4, sf_cols), None),
        "gates": (rows_region(Sb, R4, gate_cols), None),
        "qkv": (rows_region(Sb, R4, qkv_cols), None),
        "pa": (lambda j: PA.at[around[j] if groups > 1 else 0], None),
        "pb": (lambda j: PB.at[around[j] if groups > 1 else 0], None),
    }
    for i in range(4):
        lines_of["b", i] = (rows_region(Ball, T, block(i)), share(Ball, block(i)))

    def set_off(*names):
        for name in names:
            line_start(name, lines_of[name][0])

    def hop(n, *names):
        for name in names:
            line_hop(name, lines_of[name][0], n, lines_of[name][1])

    def hand_on(n, *names):
        for name in names:
            ref, c = (Nall, every) if name == "n" else (Ball, block(name[1]))
            share_on(name, ref, c, n)

    Sf[own] = SfSt[0]
    for k in (1, 2, 3):
        start(("sf", k), lambda k=k: SfSt.at[k], lambda k=k: Sf.at[place(k)], peers[k])

    @pl.when(first)
    def _():
        set_off("n")
        for i in (1, 2):
            to_tensor(("n", i), Nall, block(i))
        step_b(11)
        step_b(12)
        from_tensor("sf", Sf, sf_cols)
        set_off("sf")
        step_a(13)
        hop(1, "n", "sf")
        step_a(14)
        step_b(13)
        hop(2, "n", "sf")
        step_b(14)
        for i in range(11, 15):
            step_c(i)
        for k in range(4):
            H[1, k] = dot(Nall[own, 3 * width : 4 * width], Win[1, k])
        hand_on(1, "n")
        hop(3, "n", "sf")
        for i in (1, 2):
            from_tensor(("n", i), Nall, block(i))
        hand_on(2, "n")
        hand_on(3, "n")

    @pl.when(first)
    def _():
        arrived("back", ARR)
        G[...] = ARR[...].astype(f32)

    back_rows = lambda: IG.at[pl.ds(trow, T)]

    def feed_back(j, i, g):
        b = (0.5 * g).astype(bf16)
        Ball[own, i * width : (i + 1) * width] = b
        to_tensor(("b", i), Ball, block(i))
        grad = None
        for k in range(4):
            h = H[j, k]
            sig = jax.nn.sigmoid(h)
            hg = (dot(b, Wout[j, k], 1, 1) * (sig * (1.0 + h * (1.0 - sig)))).astype(bf16)
            part = dot(hg, Win[j, k], 1, 1)
            grad = part if grad is None else grad + part
        return g + norm_back(i, grad)
    g = norm_back(4, G[...] * row_mask)
    g = feed_back(1, 3, g)
    b = g.astype(bf16)
    Ball[own, 2 * width : 3 * width] = b
    to_tensor(("b", 2), Ball, block(2))
    hat = CT[...]
    y = hat * SM[2:3] + SM[3:4]
    sig = jax.nn.sigmoid(y)
    dy = dot(b, Wco[...], 1, 1) * (sig * (1.0 + y * (1.0 - sig)))
    PAst[2:3] = total_of(dy * hat)
    PAst[3:4] = total_of(dy)
    dhat = dy * SM[2:3]
    masked = dhat * row_mask
    dp_sums("bnb", STB, [total_of(masked), total_of(masked * hat)])
    sums = summed("bnb", STB)

    @pl.when(second)
    def _():
        set_off("n")
        from_tensor("sf", Sf, sf_cols)
        set_off("sf")

    set_off(("b", 3), ("b", 2))
    dc = inv_std * (dhat - (sums[0:1] + hat * sums[1:2]) / count) * row_mask
    DP[margin : margin + T] = dc
    for p in range(4):
        c = pl.ds(C * p, C)
        here = DP[margin : margin + T, c]
        acc = None
        for k in range(taps):
            o = margin + taps // 2 - k
            term = SM[4 + k : 5 + k, c] * DP[o : o + T, c]
            acc = term if acc is None else acc + term
            o = margin - taps // 2 + k
            PAst[4 + k : 5 + k, c] = total_of(here * UP[o : o + T, c])
        CT[:, c] = acc
    du = CT[...] * row_mask
    sig = jax.nn.sigmoid(GVG[1])
    dvalue = (du * sig).astype(bf16)
    dgate = (du * GVG[0] * (sig * (1.0 - sig))).astype(bf16)
    for k in range(4):
        SbSt[k, :, 3 * C : 4 * C] = dvalue[:, C * k : C * (k + 1)]
        SbSt[k, :, 4 * C : 5 * C] = dgate[:, C * k : C * (k + 1)]
    Sb[own, 3 * C : 5 * C] = SbSt[0, :, 3 * C : 5 * C]

    def sb_to_tensor(name, c):
        for k in (1, 2, 3):
            start((name, k), lambda k=k: SbSt.at[k, :, c], lambda k=k: Sb.at[place(k), c], peers[k])

    sb_to_tensor("gates", gate_cols)
    g = g + norm_back(2, dot(dvalue, Wci[0], 1, 1) + dot(dgate, Wci[1], 1, 1))
    b = g.astype(bf16)
    Ball[own, width : 2 * width] = b
    to_tensor(("b", 1), Ball, block(1))
    dmix = dot(b, Wo[...], 1, 1).astype(bf16).astype(f32)
    scale = HEAD ** (-0.5)
    dq, dk, dv = [], [], []
    for p in range(4):
        c = pl.ds(2 * HEAD * p, 2 * HEAD)
        qu = pair_rows(QKV[0, :, c]).astype(bf16)
        qv = pair_rows(QKV[1, :, c]).astype(bf16)
        key = QKV[2, :, c].astype(bf16)
        val = QKV[3, :, c].astype(bf16)
        do = pair_rows(dmix[:, 2 * HEAD * p : 2 * HEAD * (p + 1)]).astype(bf16)
        probs = PRB[p]
        dprob = dot(do, val, 1, 1)
        ds = (probs * (dprob - jnp.sum(probs * dprob, -1, keepdims=True))).astype(bf16)
        du_rows = unpair(dot(ds, key)) * scale
        turned = dot(ds, flip)
        whole = jnp.concatenate(
            [
                pltpu.roll(turned[e * T : (e + 1) * T], 0, 1, stride=1, stride_axis=0)[:, : 2 * T]
                for e in range(2)
            ],
            0,
        ).astype(bf16)
        dv_rows = unpair(dot(whole, R2[2 * T : 4 * T, c])) * scale
        dk.append((dot(ds, qu, 0, 0) * scale).astype(bf16))
        dv.append(dot(probs.astype(bf16), do, 0, 0).astype(bf16))
        dq.append((du_rows + dv_rows).astype(bf16))
        PAst[0:1, c] = total_of(du_rows)
        PAst[1:2, c] = total_of(dv_rows)
        PAst[SMALL_ROWS : SMALL_ROWS + 2 * T, c] = dot(whole, qv, 0, 0) * scale
    for k in range(4):
        SbSt[k, :, 0:C] = dq[k]
        SbSt[k, :, C : 2 * C] = dk[k]
        SbSt[k, :, 2 * C : 3 * C] = dv[k]
    Sb[own, 0 : 3 * C] = SbSt[0, :, 0 : 3 * C]
    sb_to_tensor("qkv", qkv_cols)
    set_off(("b", 1))

    @pl.when(first)
    def _():
        from_tensor("gates", Sb, gate_cols)
        set_off("gates")
        hop(1, ("b", 3), ("b", 2))
    grad = dot(jnp.concatenate(dq, 1), Wqkv[0], 1, 1)
    grad += dot(jnp.concatenate(dk, 1), Wqkv[1], 1, 1)
    grad += dot(jnp.concatenate(dv, 1), Wqkv[2], 1, 1)
    g = g + norm_back(1, grad)

    @pl.when(second)
    def _():
        IG[pl.ds(trow, T)] = feed_back(0, 0, g).astype(bf16)
        start("back", back_rows, lambda: ARR, partner, second)

    @pl.when(first)
    def _():
        Ball[own, 0:width] = (0.5 * g).astype(bf16)
        to_tensor(("b", 0), Ball, block(0))
        G[...] = g

    set_off(("b", 0))
    PAb[...] = PAst[...].astype(bf16)
    for k in (1, 2, 3):
        start(("pa", k), lambda k=k: PAb.at[:, cols(k)], lambda k=k: PAin.at[k], peers[k])


    @pl.when(second)
    def _():
        from_tensor("gates", Sb, gate_cols)
        set_off("gates")

    from_tensor("qkv", Sb, qkv_cols)
    set_off("qkv")

    @pl.when(first)
    def _():
        from_tensor(("b", 0), Ball, block(0))
        h = dot(Nall[four, 0:width], Win[0, 0])
        sig = jax.nn.sigmoid(h)
        hg = dot(Ball[four, 0:width], Wout[0, 0], 1, 1) * (sig * (1.0 + h * (1.0 - sig)))
        total = sum_to_owner("s2", 2, dot(hg.astype(bf16), Win[0, 0], 1, 1))
        hop(2, ("b", 3), ("b", 2))
        hop(1, "gates", ("b", 1))
        hand_on(1, ("b", 3), ("b", 2))
        g = G[...] + norm_back(0, summed_here("s2", 2, total))
        IG[pl.ds(trow, T)] = g.astype(bf16)

    PBin[t] = PBst[...].astype(bf16)
    for k in (1, 2, 3):
        start(("pb", k), lambda: PBin.at[t], lambda: PBin.at[t], peers[k])
        start(("grad", k), back_rows, back_rows, peers[k])
    PAin[0] = PAb[:, 0:C]
    for k in (1, 2, 3):
        arrived(("pa", k), PAin.at[k])
    PA[mine] = sum(PAin[k].astype(f32) for k in range(4)).astype(bf16)
    set_off("pa")

    @pl.when(second)
    def _():
        for n in (1, 2):
            hop(n, "n", "sf", ("b", 3), ("b", 2))
        hand_on(1, "n", ("b", 3), ("b", 2))
        hop(1, "gates", ("b", 1))
    hop(1, ("b", 0), "qkv")
    hop(3, ("b", 3), ("b", 2))
    hop(2, "gates", ("b", 1))
    for k in (1, 2, 3):
        arrived(("pb", k), PBin.at[t ^ k])
    PB[mine] = sum(PBin[k].astype(f32) for k in range(4)).astype(bf16)
    set_off("pb")
    hop(1, "pa")
    hand_on(1, ("b", 1), ("b", 0))
    hand_on(2, ("b", 3), ("b", 2))

    @pl.when(second)
    def _():
        hop(3, "n", "sf")
        hand_on(2, "n")
    hop(2, ("b", 0), "qkv")
    hop(3, "gates", ("b", 1))
    hop(1, "pb")
    hop(2, "pa")
    hand_on(2, ("b", 1), ("b", 0))
    hand_on(3, ("b", 3), ("b", 2))

    @pl.when(second)
    def _():
        hand_on(3, "n")
    hop(3, ("b", 0), "qkv")
    hop(2, "pb")
    hop(3, "pa")
    hand_on(3, ("b", 1), ("b", 0))
    hop(3, "pb")
    for k in (1, 2, 3):
        theirs = pl.ds(pl.multiple_of((t ^ k) * T, T), T)
        arrived(("out", k), LO.at[theirs])
        arrived(("grad", k), IG.at[theirs])
    for i in (3, 2, 1):
        from_tensor(("b", i), Ball, block(i))

    @pl.when(second)
    def _():
        from_tensor(("b", 0), Ball, block(0))
        for i in range(4):
            from_tensor(("n", i), Nall, block(i))

    shared("n", Nall, every)
    for i in (3, 2, 1, 0):
        shared(("b", i), Ball, block(i))
    conds = {}
    for cond, copy in pending.values():
        conds.setdefault(id(cond), (cond, []))[1].append(copy)
    for cond, copies in conds.values():
        if cond is None:
            for copy in copies:
                copy().wait_send()
        else:

            @pl.when(cond)
            def _():
                for copy in copies:
                    copy().wait_send()


def gradient_kernel(*refs):
    given, outs, held, made = refs[:11], refs[11:25], refs[25:36], refs[36:50]
    active, hidden, in_sems, out_sems = refs[50:]
    nall, ball, sf, sb, lo, ig, pa, pb, fin, fout, table = held
    (LO, IG, ng, nb, w_in, w_out, w_ain, pos, w_aout, w_cin, w_dw, bng, bns, w_cout) = made
    R, width, C = nall.shape[0], fin.shape[1], sf.shape[1] // 2
    loads = [pltpu.make_async_copy(given[i], held[i], in_sems.at[i]) for i in range(len(given))]
    for i in (8, 9, 0, 1, 2, 3, 4, 5, 6, 7, 10):
        loads[i].start()
    stores = []

    def store(src, dst, sem):
        copy = pltpu.make_async_copy(src, dst, out_sems.at[sem])
        copy.start()
        stores.append(copy)

    def block(ref, i, n):
        return ref[:, i * n : (i + 1) * n]

    for i in (8, 9, 0, 1):
        loads[i].wait()
    step = min(128, R)
    for j, i in ((0, 0), (1, 3)):
        c = slice(i * width, (i + 1) * width)
        for r in range(0, R, step):
            rows = slice(r, r + step)
            h = dot(nall[rows, c], fin[j])
            sig = jax.nn.sigmoid(h)
            active[rows] = (h * sig).astype(bf16)
            grad = dot(ball[rows, c], fout[j], 1, 1)
            hidden[rows] = (grad * (sig * (1.0 + h * (1.0 - sig)))).astype(bf16)
        w_in[j] = dot(nall[:, c], hidden[...], 0, 0)
        store(w_in.at[j], outs[4].at[j], 4 if j == 0 else 14)
        w_out[j] = dot(active[...], ball[:, c], 0, 0)
        store(w_out.at[j], outs[5].at[j], 5 if j == 0 else 15)
    for i in (2, 3, 4, 5, 6, 7, 10):
        loads[i].wait()
    qkv = dot(block(nall, 1, width), sb[:, 0 : 3 * C], 0, 0)
    for i in range(3):
        w_ain[i] = qkv[:, C * i : C * (i + 1)]
    sums = pa[0].astype(f32)
    for g in range(1, pa.shape[0]):
        sums += pa[g].astype(f32)
    w_ain[3] = dot(table[...], sums[SMALL_ROWS:].astype(bf16), 0, 0)
    store(w_ain, outs[6], 6)
    gates = dot(block(nall, 2, width), sb[:, 3 * C : 5 * C], 0, 0)
    for i in range(2):
        w_cin[pl.ds(i, width, stride=2), :] = gates[:, C * i : C * (i + 1)]
    store(w_cin, outs[9], 9)
    w_aout[...] = dot(sf[:, 0:C], block(ball, 1, width), 0, 0)
    store(w_aout, outs[8], 8)
    w_cout[...] = dot(sf[:, C : 2 * C], block(ball, 2, width), 0, 0)
    store(w_cout, outs[13], 13)
    LO[...] = lo[...].astype(f32)
    IG[...] = ig[...].astype(f32)
    norms = pb[0].astype(f32)
    for g in range(1, pb.shape[0]):
        norms += pb[g].astype(f32)
    for i in range(5):
        ng[i] = norms[i : i + 1]
        nb[i] = norms[8 + i : 9 + i]
    pos[...] = sums[0:2]
    bng[...] = sums[2:3]
    bns[...] = sums[3:4]
    for k in range(w_dw.shape[0]):
        w_dw[k] = sums[4 + k : 5 + k]
    for i in (0, 1, 2, 3, 7, 10, 11, 12):
        store(made[i], outs[i], i)
    for copy in stores:
        copy.wait()


def on_device(
    inputs, lengths, cotangent, norm_gain, norm_bias, ffn_in, ffn_out, attn_in, pos_bias, attn_out,
    conv_in, depthwise, bn_gain, bn_shift, conv_out,
):
    dp = lax.axis_size(DATA)
    group, frames, width = inputs.shape
    C = width // 4
    taps = depthwise.shape[1]
    groups = dp if dp <= 4 else 1
    R = groups * group * frames
    table = position_rows(frames, width)
    vm = pl.BlockSpec(memory_space=pltpu.VMEM)
    hbm = pl.BlockSpec(memory_space=pltpu.HBM)
    sums_rows = SMALL_ROWS + 2 * frames

    def shape(dims, dtype=bf16):
        return jax.ShapeDtypeStruct(dims, dtype)

    n_copies = 200 + 50 * (groups - 1) + 2 * dp
    operands = (
        lengths, inputs, cotangent, norm_gain.transpose(1, 0, 2), norm_bias.transpose(1, 0, 2), ffn_in[0],
        ffn_out[0], attn_in[0], attn_out[0], conv_in.reshape(2 * width, C), conv_out[0], pos_bias[0], bn_gain,
        bn_shift, depthwise.transpose(1, 0, 2), table,
    )
    nall, ball, sf, sb, lo, ig, pa, pb = pl.pallas_call(
        lambda *refs: layer_kernel((frames, width, dp, groups), *refs),
        out_shape=[
            shape((R, 4 * width)), shape((R, 4 * width)), shape((R, 2 * C)), shape((R, 5 * C)),
            shape((group * frames, width)), shape((group * frames, width)),
            shape((groups, sums_rows, C)), shape((groups, 16, width)),
        ],
        in_specs=[hbm] * 16,
        out_specs=[vm] * 8,
        scratch_shapes=[
            pltpu.VMEM((2, 4, width, width), bf16),
            pltpu.VMEM((2, 4, width, width), bf16),
            pltpu.VMEM((3, width, width), bf16),
            pltpu.VMEM((width, C), bf16),
            pltpu.VMEM((width, width), bf16),
            pltpu.VMEM((2, width, width), bf16),
            pltpu.VMEM((width, width), bf16),
            pltpu.VMEM((4 * frames, width), bf16),
            pltpu.VMEM((SMALL_ROWS, width), f32),
            pltpu.VMEM((2, 4, frames, width), f32),
            pltpu.VMEM((5, frames, width), f32),
            pltpu.VMEM((5, frames, 128), f32),
            pltpu.VMEM((5, frames, width), f32),
            pltpu.VMEM((frames, width), f32),
            pltpu.VMEM((frames, width), bf16),
            pltpu.VMEM((frames, width), bf16),
            pltpu.VMEM((4, frames, width), f32),
            pltpu.VMEM((4, 2 * frames, frames), f32),
            pltpu.VMEM((2, frames, width), f32),
            pltpu.VMEM((frames, width), f32),
            pltpu.VMEM((frames + 32, width), f32),
            pltpu.VMEM((frames + 32, width), f32),
            pltpu.VMEM((4, frames, 2 * C), bf16),
            pltpu.VMEM((4, frames, 5 * C), bf16),
            pltpu.VMEM((sums_rows, width), f32),
            pltpu.VMEM((sums_rows, width), bf16),
            pltpu.VMEM((4, sums_rows, C), bf16),
            pltpu.VMEM((16, width), f32),
            pltpu.VMEM((4, 16, width), bf16),
            pltpu.VMEM((dp, 8, width), f32),
            pltpu.VMEM((dp, 8, width), f32),
            pltpu.VMEM((3, 3, frames, width), bf16),
            pltpu.VMEM((3, 3, frames, width), bf16),
            pltpu.VMEM((5, 1, width), f32),
            pltpu.VMEM((5, 1, width), f32),
            pltpu.VMEM((2, C), f32),
            pltpu.VMEM((1, C), f32),
            pltpu.VMEM((1, C), f32),
            pltpu.VMEM((taps, 1, C), f32),
            pltpu.VMEM((4 * frames, width), bf16),
            pltpu.SMEM((group,), jnp.int32),
            pltpu.VMEM((2 * width, C), bf16),
            pltpu.VMEM((2 * width, C), f32),
            pltpu.SemaphoreType.DMA((n_copies,)),
            pltpu.SemaphoreType.DMA((n_copies,)),
            pltpu.SemaphoreType.DMA((21,)),
        ],
        compiler_params=pltpu.CompilerParams(
            collective_id=0, has_side_effects=True, vmem_limit_bytes=62 * 2**20
        ),
    )(*operands)

    gradients = [
        shape((group * frames, width), f32), shape((group * frames, width), f32), shape((5, 1, width), f32),
        shape((5, 1, width), f32), shape((2, width, width), f32), shape((2, width, width), f32),
        shape((4, width, C), f32), shape((2, C), f32), shape((C, width), f32), shape((2 * width, C), f32),
        shape((taps, 1, C), f32), shape((1, C), f32), shape((1, C), f32), shape((C, width), f32),
    ]
    given = (nall, ball, sf, sb, lo, ig, pa, pb, ffn_in[0], ffn_out[0], table[2 * frames :])
    outs = pl.pallas_call(
        gradient_kernel,
        out_shape=gradients,
        in_specs=[hbm] * len(given),
        out_specs=[hbm] * len(gradients),
        scratch_shapes=[pltpu.VMEM(m.shape, m.dtype) for m in given]
        + [pltpu.VMEM(m.shape, m.dtype) for m in gradients]
        + [
            pltpu.VMEM((R, width), bf16),
            pltpu.VMEM((R, width), bf16),
            pltpu.SemaphoreType.DMA((len(given),)),
            pltpu.SemaphoreType.DMA((len(gradients) + 2,)),
        ],
        compiler_params=pltpu.CompilerParams(vmem_limit_bytes=62 * 2**20),
    )(*given)
    if groups == 1:
        outs = list(outs[:2]) + [lax.psum(m.astype(bf16), DATA).astype(f32) for m in outs[2:]]
    (lo, ig, ng, nb, w_in, w_out, w_ain, pos, w_aout, w_cin, w_dw, bng, bns, w_cout) = outs
    rows = (1, group, frames, width)
    return (
        lo.reshape(rows), ig.reshape(rows), ng.transpose(1, 0, 2), nb.transpose(1, 0, 2), w_in[None], w_out[None],
        w_ain[None], pos[None], w_aout[None], w_cin.reshape(conv_in.shape), w_dw.transpose(1, 0, 2), bng, bns,
        w_cout[None],
    )


def solution(mesh):
    placed = (
        P(DATA, None, None),
        P(DATA),
        P(DATA, None, None),
        P(SECTION, None, None),
        P(SECTION, None, None),
        P(SECTION, None, None, TENSOR),
        P(SECTION, None, TENSOR, None),
        P(SECTION, None, None, TENSOR),
        P(SECTION, None, TENSOR),
        P(SECTION, TENSOR, None),
        P(SECTION, None, None, TENSOR),
        P(SECTION, None, TENSOR),
        P(SECTION, TENSOR),
        P(SECTION, TENSOR),
        P(SECTION, TENSOR, None),
    )
    return jax.shard_map(
        on_device,
        mesh=mesh,
        in_specs=placed,
        out_specs=(
            P(SECTION, DATA, None, None),
            P(SECTION, DATA, None, None),
            P(SECTION, None, None),
            P(SECTION, None, None),
            P(SECTION, None, None, TENSOR),
            P(SECTION, None, TENSOR, None),
            P(SECTION, None, None, TENSOR),
            P(SECTION, None, TENSOR),
            P(SECTION, TENSOR, None),
            P(SECTION, None, None, TENSOR),
            P(SECTION, None, TENSOR),
            P(SECTION, TENSOR),
            P(SECTION, TENSOR),
            P(SECTION, TENSOR, None),
        ),
        check_vma=False,
    )
```

time: 217 us -> 121 us (0.56)
  Pallas kernels: 172 us -> 120 us
  local copies, waits for them, and re-layouts: 19.8 us -> 0 us
  matrix products: 16.8 us -> 0 us
  other arithmetic: 6.2 us -> 0 us
    pallas_call x1, Pallas kernels: 172 us -> 112 us  [on_device(): pl.pallas_call(lambda *refs: layer_kernel((frames, width, dp, groups), *r...]
    dot_general x14 -> x0, matrix products: 16.8 us -> none  [dot(): lax.dot_general(left, right, (((left_dim,), (right_dim,)), ((), ())), pre...]
    unnamed x40 -> x0, local copies, waits for them, and re-layouts: 16 us -> none
    pallas_call x0 -> x1, Pallas kernels: none -> 8.35 us  [on_device(): pl.pallas_call(gradient_kernel, out_shape=gradients, in_specs=[hbm] * len...]
    broadcast_in_dim x4 -> x0, other arithmetic: 4.11 us -> none  [on_device(): return tuple((m[None] for m in outs))]
    broadcast_in_dim x4 -> x0, local copies, waits for them, and re-layouts: 2.39 us -> none  [on_device(): return tuple((m[None] for m in outs))]
where the time goes in v2:
time: 121 us
  Pallas kernels  120 us (99%)
    pallas_call x1, Pallas kernels, on_device(): pl.pallas_call(lambda *refs: layer_kernel((frames, width, dp, groups), *r...  112 us
    pallas_call x1, Pallas kernels, on_device(): pl.pallas_call(gradient_kernel, out_shape=gradients, in_specs=[hbm] * len...  8.35 us

profile of v2, /device:TPU:0, one launch (start us, length us, event | category | flops | bytes accessed | tf_op | source)
XLA Modules:
  0.0 120.7 jit_solution(2975870602386463412)
XLA Ops:
  0.7 111.6 %shard_map.263 = (bf16[512,2048]{1,0:T(8,128)(2,1)}, bf16[512,2048]{1,0:T(8,128)(2,1)}, bf16[512,256]{1,0:T(8,128)(2,1)}, bf16[512,640]{1,0:T(8,128)(2,1)}, bf16...) custom-call(s32[4]{0:T(128)} %refs_0_.1, ...), custom_call_target="tpu_custom_call" | custom-call | tf_op jit(solution)/shard_map/pallas_call | solution.py:938
  112.2 8.3 %shard_map.264 = (f32[128,512]{1,0:T(8,128)}, f32[128,512]{1,0:T(8,128)}, f32[5,1,512]{2,1,0:T(1,128)}, f32[5,1,512]{2,1,0:T(1,128)}, f32[2,512,512]{2,1,0:T(8,1...) custom-call(bf16[512,2048]{1,0:T(8,128)(2,1)} %get-tuple-element.36., ...), custom_call_target="tpu_custom_call" | custom-call | tf_op jit(solution)/shard_map/pallas_call | solution.py:1007

commit v3 on v2

--- a/solution.py
+++ b/solution.py
@@ -38,12 +38,14 @@
     T, width, dp, groups = dims
     C = width // 4
     (lengths, inputs, cot, ng_in, nb_in, fin, fout, ain, aout, cin, cout, pos_in, bng_in, bns_in, dw_in, e2_in) = refs[:16]
-    (Nall, Ball, Sf, Sb, LO, IG, PA, PB) = refs[16:24]
-    (Win, Wout, Wqkv, Wr, Wo, Wci, Wco, R2, SM) = refs[24:33]
-    (H, XH, RS, X, G, ARR, HOP, QKV, PRB, GVG, CT, UP, DP) = refs[33:46]
-    (SfSt, SbSt, PAst, PAb, PAin, PBst, PBin, STF, STB, RSst, RSin) = refs[46:57]
-    (ng, nb, pos, bng, bns, dw, e2, lens, pairs, spread) = refs[57:67]
-    ss, rs, ls = refs[67:70]
+    (LO, IG, PA, PB, n0_out, b0_out, act0_out, slope0_out, in1_out, out1_out, qkv_out, ao_out, ci_out, co_out) = refs[16:30]
+    refs = refs[30:]
+    (Win, Wout, Wqkv, Wr, Wo, Wci, Wco, R2, SM) = refs[:9]
+    (H, XH, RS, X, G, ARR, HOP, QKV, PRB, GVG, CT, UP, DP) = refs[9:22]
+    (SfSt, SbSt, PAst, PAb, PAin, PBst, PBin, STF, STB, RSst, RSin) = refs[22:33]
+    (ng, nb, pos, bng, bns, dw, e2, lens, pairs, spread) = refs[33:43]
+    (Nall, Ball, Sf, Sb, ACT, SLOPE, HG, gin1, gout1, gqkv, gao, gci, gco) = refs[43:56]
+    dummy, ss, rs, ls, os = refs[56:61]
 
     s, t, d = lax.axis_index(SECTION), lax.axis_index(TENSOR), lax.axis_index(DATA)
     first, second = s == 0, s == 1
@@ -69,22 +71,32 @@
     trow = pl.multiple_of(t * T, T)
     mine = d if groups > 1 else 0
 
-    index, pending = {}, {}
-
-    def copy_of(key, src, dst, dev):
-        i = index.setdefault(key, len(index))
+    recv_index, send_index, sent = {}, {}, {}
+
+    def size_of(view):
+        return math.prod(view.shape) * view.dtype.itemsize
+
+    def copy_of(key, src, dst, dev, group):
+        i = recv_index.setdefault(key, len(recv_index))
+        j = send_index.setdefault(id(group), len(send_index))
         return pltpu.make_async_remote_copy(
-            src_ref=src, dst_ref=dst, send_sem=ss.at[i], recv_sem=rs.at[i],
-            device_id=dev, device_id_type=MESH,
+            src_ref=src, dst_ref=dst, send_sem=ss.at[j], recv_sem=rs.at[i], device_id=dev, device_id_type=MESH,
         )
 
-    def start(key, src, dst, dev, cond=None):
-        again = lambda: copy_of(key, src(), dst(), dev)
-        again().start()
-        pending[key] = (cond, again)
+    def start(key, src, dst, dev, cond=None, part=0):
+        view = src()
+        copy_of(key, view, dst(), dev, cond).start()
+        sent.setdefault(id(cond), (cond, {}))[1][key, part] = size_of(view)
 
     def arrived(key, dst):
-        copy_of(key, dst, dst, partner).wait_recv()
+        copy_of(key, dst, dst, partner, None).wait_recv()
+
+    def room(size):
+        return dummy.at[pl.ds(0, size // (4 * dummy.shape[1]))]
+
+    def all_arrived(key, size):
+        if size:
+            arrived(key, room(size))
 
     locals_ = {}
 
@@ -184,18 +196,15 @@
         dst = chunks[i][1]
         arrived(("y", i), dst(2, "own"))
         start(("z", i), lambda: dst(2, "own"), lambda: dst(2, "own"), zpair, only.get(i))
-        start(("sib2", i), lambda: dst(2, "own"), lambda: dst(3, "own"), sib, only.get(i))
+        start(("sib", i), lambda: dst(2, "own"), lambda: dst(3, "own"), sib, only.get(i), 1)
 
     def step_b(i):
         dst = chunks[i][1]
         arrived(("z", i), dst(2, "other"))
-        start(("sib3", i), lambda: dst(2, "other"), lambda: dst(3, "other"), sib, only.get(i))
+        start(("sib", i), lambda: dst(2, "other"), lambda: dst(3, "other"), sib, only.get(i), 2)
 
     def step_c(i):
-        dst = chunks[i][1]
-        arrived(("sib", i), dst(1, None))
-        arrived(("sib2", i), dst(3, "own"))
-        arrived(("sib3", i), dst(3, "other"))
+        all_arrived(("sib", i), 2 * size_of(chunks[i][1](1, None)))
 
     def steps(cond, *plan):
         @pl.when(cond)
@@ -235,11 +244,10 @@
 
     def to_tensor(name, ref, c):
         for k in (1, 2, 3):
-            start((name, k), lambda: ref.at[own, c], lambda k=k: ref.at[place(k), c], peers[k])
-
-    def from_tensor(name, ref, c, which=(1, 2, 3)):
-        for k in which:
-            arrived((name, k), ref.at[place(k), c])
+            start(name, lambda: ref.at[own, c], lambda k=k: ref.at[place(k), c], peers[k], None, k)
+
+    def from_tensor(name, ref, c):
+        all_arrived(name, 3 * size_of(ref.at[own, c]))
 
     def feed(j, i, before, after):
         x = X[before]
@@ -260,14 +268,12 @@
         for k in (1, 2, 3):
             RSst[slot, k - 1] = total[T * PLACE[k] : T * (PLACE[k] + 1)].astype(bf16)
         for k in (1, 2, 3):
-            start(
-                (name, k), lambda k=k: RSst.at[slot, k - 1], lambda k=k: RSin.at[slot, k - 1], peers[k], first
-            )
+            start(name, lambda k=k: RSst.at[slot, k - 1], lambda k=k: RSin.at[slot, k - 1], peers[k], first, k)
         return total[0:T]
 
     def summed_here(name, slot, total):
+        all_arrived(name, size_of(RSin.at[slot]))
         for k in (1, 2, 3):
-            arrived((name, k), RSin.at[slot, k - 1])
             total += RSin[slot, k - 1].astype(f32)
         return total
 
@@ -311,8 +317,8 @@
         SM[4 + k : 5 + k, 0:C] = dw[k]
     R2[:, 0:C] = dot(e2[...], Wr[...]).astype(bf16)
     for k in (1, 2, 3):
-        start(("small", k), lambda: SM.at[:, cols(0)], lambda k=k: SM.at[:, cols(k)], peers[k])
-        start(("rel", k), lambda: R2.at[:, cols(0)], lambda k=k: R2.at[:, cols(k)], peers[k])
+        start("small", lambda: SM.at[:, cols(0)], lambda k=k: SM.at[:, cols(k)], peers[k], None, k)
+        start("small", lambda: R2.at[:, cols(0)], lambda k=k: R2.at[:, cols(k)], peers[k], None, 3 + k)
     @pl.when(first)
     def _():
         send_chunks(range(7, 13))
@@ -369,10 +375,9 @@
     a = norm(1, x).astype(bf16)
     Nall[own, width : 2 * width] = a
     send_rows_second(1)
+    steps(second, (A, 14), (B, 12))
     steps(first, (W, 4), (W, 5))
-    for k in (1, 2, 3):
-        arrived(("small", k), SM.at[:, cols(k)])
-        arrived(("rel", k), R2.at[:, cols(k)])
+    all_arrived("small", 3 * (size_of(SM.at[:, cols(0)]) + size_of(R2.at[:, cols(0)])))
     steps(first, (A, 7), (B, 6), (W, 6))
     q = dot(a, Wqkv[0])
     QKV[0] = q + SM[0:1]
@@ -402,7 +407,6 @@
         SfSt[k, :, 0:C] = mixed[k]
     steps(first, (A, 8), (B, 7), (A, 9))
     step_c(7)
-    steps(second, (A, 14), (B, 12))
     total = dot(mixed[0], Wo[0:C])
     for k in range(1, 4):
         total += dot(mixed[k], Wo[C * k : C * (k + 1)])
@@ -431,11 +435,10 @@
         n = len(rows)
         ref[d] = jnp.concatenate(rows + [jnp.zeros((8 - n, width), f32)], 0)
         for r in range(1, dp):
-            start((name, r), lambda: ref.at[d], lambda: ref.at[d], zpeers[r])
+            start(name, lambda: ref.at[d], lambda: ref.at[d], zpeers[r], None, r)
 
     def summed(name, ref):
-        for r in range(1, dp):
-            arrived((name, r), ref.at[around[-r]])
+        all_arrived(name, (dp - 1) * size_of(ref.at[0]))
         total = ref[0]
         for r in range(1, dp):
             total += ref[r]
@@ -487,7 +490,7 @@
     LO[pl.ds(trow, T)] = out
     out_rows = lambda: LO.at[pl.ds(trow, T)]
     for k in (1, 2, 3):
-        start(("out", k), out_rows, out_rows, peers[k])
+        start("out", out_rows, out_rows, peers[k], None, k)
 
     def line_start(name, region):
         for way, to, back in (("up", 1, -1), ("down", -1, 1)):
@@ -495,7 +498,9 @@
 
                 @pl.when(there[to])
                 def _():
-                    start((name, way, 1), lambda: region(0), lambda: region(0), (s, t, around[to]), there[to])
+                    start(
+                        (name, 0, back % dp), lambda: region(0), lambda: region(0), (s, t, around[to]), there[to], way
+                    )
 
     def line_hop(name, region, n, after=None):
         for way, to, back in (("up", 1, -1), ("down", -1, 1)):
@@ -504,14 +509,14 @@
                 @pl.when(there[back * n])
                 def _():
                     j = back * n
-                    arrived((name, way, n), region(j))
+                    arrived((name, 0, j % dp), region(j))
                     if n + 1 < groups:
 
                         @pl.when(there[to])
                         def _():
                             start(
-                                (name, way, n + 1), lambda: region(j), lambda: region(j),
-                                (s, t, around[to]), through[j, to],
+                                (name, 0, (j + back) % dp), lambda: region(j), lambda: region(j),
+                                (s, t, around[to]), through[j, to], way,
                             )
 
                     if after is not None:
@@ -523,8 +528,8 @@
     def share(ref, c):
         def go(name, j):
             rows = lambda: ref.at[pl.ds(base_of[j], T), c]
-            start((name, "y", j), rows, lambda: ref.at[pl.ds(second_of[j], T), c], yp, there[j])
-            start((name, "core", j), rows, lambda: ref.at[pl.ds(high_of[j], T), c], sib, there[j])
+            start((name, 1, j % dp), rows, lambda: ref.at[pl.ds(second_of[j], T), c], yp, there[j], j)
+            start((name, 2, 0), rows, lambda: ref.at[pl.ds(high_of[j], T), c], sib, there[j], j)
 
         return go
 
@@ -535,17 +540,11 @@
                 @pl.when(there[j])
                 def _():
                     rows = lambda: ref.at[pl.ds(second_of[j], T), c]
-                    arrived((name, "y", j), rows())
-                    start((name, "core2", j), rows, lambda: ref.at[pl.ds(last_of[j], T), c], sib, there[j])
+                    arrived((name, 1, j % dp), rows())
+                    start((name, 2, 0), rows, lambda: ref.at[pl.ds(last_of[j], T), c], sib, there[j], dp + j)
 
     def shared(name, ref, c):
-        for j in reach:
-            if j:
-
-                @pl.when(there[j])
-                def _():
-                    arrived((name, "core", j), ref.at[pl.ds(high_of[j], T), c])
-                    arrived((name, "core2", j), ref.at[pl.ds(last_of[j], T), c])
+        all_arrived((name, 2, 0), 2 * (groups - 1) * size_of(ref.at[own, c]))
 
     every = block(0, 4)
     sf_cols = pl.ds(0, 2 * C)
@@ -576,7 +575,52 @@
 
     Sf[own] = SfSt[0]
     for k in (1, 2, 3):
-        start(("sf", k), lambda k=k: SfSt.at[k], lambda k=k: Sf.at[place(k)], peers[k])
+        start("sf", lambda k=k: SfSt.at[k], lambda k=k: Sf.at[place(k)], peers[k], None, k)
+
+    written = []
+
+    def write(src, dst):
+        copy = pltpu.make_async_copy(src, dst, os.at[len(written)])
+        copy.start()
+        written.append(copy)
+
+    R = Nall.shape[0]
+    row_blocks = [slice(r, r + R4) for r in range(0, R, R4)]
+
+    def slope(h, sig):
+        return sig * (1.0 + h * (1.0 - sig))
+
+    def hidden_rows(j, i):
+        for rows in row_blocks:
+            h = dot(Nall[rows, i * width : (i + 1) * width], Win[j, 0])
+            sig = jax.nn.sigmoid(h)
+            ACT[j, rows] = (h * sig).astype(bf16)
+            SLOPE[j, rows] = slope(h, sig)
+
+    def second_feed_grads():
+        c = slice(3 * width, 4 * width)
+        for rows in row_blocks:
+            HG[rows] = (dot(Ball[rows, c], Wout[1, 0], 1, 1) * SLOPE[1, rows]).astype(bf16)
+        gin1[...] = dot(Nall[:, c], HG[...], 0, 0)
+        write(gin1, in1_out)
+        gout1[...] = dot(ACT[1], Ball[:, c], 0, 0)
+        write(gout1, out1_out)
+
+    def convolution_grads():
+        gates = dot(Nall[:, 2 * width : 3 * width], Sb[:, 3 * C : 5 * C], 0, 0)
+        for i in range(2):
+            gci[pl.ds(i, width, stride=2), :] = gates[:, C * i : C * (i + 1)]
+        write(gci, ci_out)
+        gco[...] = dot(Sf[:, C : 2 * C], Ball[:, 2 * width : 3 * width], 0, 0)
+        write(gco, co_out)
+
+    def attention_grads():
+        grads = dot(Nall[:, width : 2 * width], Sb[:, 0 : 3 * C], 0, 0)
+        for i in range(3):
+            gqkv[i] = grads[:, C * i : C * (i + 1)]
+        write(gqkv, qkv_out)
+        gao[...] = dot(Sf[:, 0:C], Ball[:, width : 2 * width], 0, 0)
+        write(gao, ao_out)
 
     @pl.when(first)
     def _():
@@ -619,7 +663,7 @@
         for k in range(4):
             h = H[j, k]
             sig = jax.nn.sigmoid(h)
-            hg = (dot(b, Wout[j, k], 1, 1) * (sig * (1.0 + h * (1.0 - sig)))).astype(bf16)
+            hg = (dot(b, Wout[j, k], 1, 1) * slope(h, sig)).astype(bf16)
             part = dot(hg, Win[j, k], 1, 1)
             grad = part if grad is None else grad + part
         return g + norm_back(i, grad)
@@ -631,7 +675,7 @@
     hat = CT[...]
     y = hat * SM[2:3] + SM[3:4]
     sig = jax.nn.sigmoid(y)
-    dy = dot(b, Wco[...], 1, 1) * (sig * (1.0 + y * (1.0 - sig)))
+    dy = dot(b, Wco[...], 1, 1) * slope(y, sig)
     PAst[2:3] = total_of(dy * hat)
     PAst[3:4] = total_of(dy)
     dhat = dy * SM[2:3]
@@ -670,7 +714,7 @@
 
     def sb_to_tensor(name, c):
         for k in (1, 2, 3):
-            start((name, k), lambda k=k: SbSt.at[k, :, c], lambda k=k: Sb.at[place(k), c], peers[k])
+            start(name, lambda k=k: SbSt.at[k, :, c], lambda k=k: Sb.at[place(k), c], peers[k], None, k)
 
     sb_to_tensor("gates", gate_cols)
     g = g + norm_back(2, dot(dvalue, Wci[0], 1, 1) + dot(dgate, Wci[1], 1, 1))
@@ -738,7 +782,7 @@
     set_off(("b", 0))
     PAb[...] = PAst[...].astype(bf16)
     for k in (1, 2, 3):
-        start(("pa", k), lambda k=k: PAb.at[:, cols(k)], lambda k=k: PAin.at[k], peers[k])
+        start("pa", lambda k=k: PAb.at[:, cols(k)], lambda k=k: PAin.at[k], peers[k], None, k)
 
 
     @pl.when(second)
@@ -746,15 +790,21 @@
         from_tensor("gates", Sb, gate_cols)
         set_off("gates")
 
+    @pl.when(first)
+    def _():
+        shared("n", Nall, every)
+        hidden_rows(1, 3)
+
     from_tensor("qkv", Sb, qkv_cols)
     set_off("qkv")
 
     @pl.when(first)
     def _():
+        hidden_rows(0, 0)
         from_tensor(("b", 0), Ball, block(0))
         h = dot(Nall[four, 0:width], Win[0, 0])
         sig = jax.nn.sigmoid(h)
-        hg = dot(Ball[four, 0:width], Wout[0, 0], 1, 1) * (sig * (1.0 + h * (1.0 - sig)))
+        hg = dot(Ball[four, 0:width], Wout[0, 0], 1, 1) * slope(h, sig)
         total = sum_to_owner("s2", 2, dot(hg.astype(bf16), Win[0, 0], 1, 1))
         hop(2, ("b", 3), ("b", 2))
         hop(1, "gates", ("b", 1))
@@ -764,11 +814,10 @@
 
     PBin[t] = PBst[...].astype(bf16)
     for k in (1, 2, 3):
-        start(("pb", k), lambda: PBin.at[t], lambda: PBin.at[t], peers[k])
-        start(("grad", k), back_rows, back_rows, peers[k])
+        start("pb", lambda: PBin.at[t], lambda: PBin.at[t], peers[k], None, k)
+        start("grad", back_rows, back_rows, peers[k], None, k)
     PAin[0] = PAb[:, 0:C]
-    for k in (1, 2, 3):
-        arrived(("pa", k), PAin.at[k])
+    all_arrived("pa", 3 * size_of(PAin.at[0]))
     PA[mine] = sum(PAin[k].astype(f32) for k in range(4)).astype(bf16)
     set_off("pa")
 
@@ -781,8 +830,7 @@
     hop(1, ("b", 0), "qkv")
     hop(3, ("b", 3), ("b", 2))
     hop(2, "gates", ("b", 1))
-    for k in (1, 2, 3):
-        arrived(("pb", k), PBin.at[t ^ k])
+    all_arrived("pb", 3 * size_of(PBin.at[0]))
     PB[mine] = sum(PBin[k].astype(f32) for k in range(4)).astype(bf16)
     set_off("pb")
     hop(1, "pa")
@@ -803,100 +851,92 @@
     @pl.when(second)
     def _():
         hand_on(3, "n")
-    hop(3, ("b", 0), "qkv")
+    hop(3, ("b", 0))
+
+    @pl.when(second)
+    def _():
+        for i in range(4):
+            from_tensor(("n", i), Nall, block(i))
+        shared("n", Nall, every)
+        hidden_rows(1, 3)
+        hidden_rows(0, 0)
+
+    write(Nall.at[:, block(0)], n0_out)
+    write(ACT.at[0], act0_out)
+    write(SLOPE.at[0], slope0_out)
+    for i in (3, 2):
+        from_tensor(("b", i), Ball, block(i))
+        shared(("b", i), Ball, block(i))
+    second_feed_grads()
+    hand_on(3, ("b", 1), ("b", 0))
+    hop(3, "qkv")
     hop(2, "pb")
     hop(3, "pa")
-    hand_on(3, ("b", 1), ("b", 0))
+    convolution_grads()
+    from_tensor(("b", 1), Ball, block(1))
+    shared(("b", 1), Ball, block(1))
+    attention_grads()
     hop(3, "pb")
-    for k in (1, 2, 3):
-        theirs = pl.ds(pl.multiple_of((t ^ k) * T, T), T)
-        arrived(("out", k), LO.at[theirs])
-        arrived(("grad", k), IG.at[theirs])
-    for i in (3, 2, 1):
-        from_tensor(("b", i), Ball, block(i))
 
     @pl.when(second)
     def _():
         from_tensor(("b", 0), Ball, block(0))
-        for i in range(4):
-            from_tensor(("n", i), Nall, block(i))
-
-    shared("n", Nall, every)
-    for i in (3, 2, 1, 0):
-        shared(("b", i), Ball, block(i))
-    conds = {}
-    for cond, copy in pending.values():
-        conds.setdefault(id(cond), (cond, []))[1].append(copy)
-    for cond, copies in conds.values():
-        if cond is None:
-            for copy in copies:
-                copy().wait_send()
-        else:
-
-            @pl.when(cond)
-            def _():
-                for copy in copies:
-                    copy().wait_send()
-
-
-def gradient_kernel(*refs):
-    given, outs, held, made = refs[:11], refs[11:25], refs[25:36], refs[36:50]
-    active, hidden, in_sems, out_sems = refs[50:]
-    nall, ball, sf, sb, lo, ig, pa, pb, fin, fout, table = held
-    (LO, IG, ng, nb, w_in, w_out, w_ain, pos, w_aout, w_cin, w_dw, bng, bns, w_cout) = made
-    R, width, C = nall.shape[0], fin.shape[1], sf.shape[1] // 2
-    loads = [pltpu.make_async_copy(given[i], held[i], in_sems.at[i]) for i in range(len(given))]
-    for i in (8, 9, 0, 1, 2, 3, 4, 5, 6, 7, 10):
+
+    shared(("b", 0), Ball, block(0))
+    write(Ball.at[:, block(0)], b0_out)
+    all_arrived("out", 3 * size_of(out_rows()))
+    all_arrived("grad", 3 * size_of(back_rows()))
+    for copy in written:
+        copy.wait()
+    for cond, sizes in sent.values():
+
+        def all_sent():
+            view = room(sum(sizes.values()))
+            copy_of("out", view, view, partner, cond).wait_send()
+
+        all_sent() if cond is None else pl.when(cond)(all_sent)
+    assert len(recv_index) <= rs.shape[0] and len(send_index) <= ss.shape[0]
+
+
+def last_kernel(*refs):
+    given, outs, held, made, in_sems, out_sems = refs[:16], refs[16:30], refs[30:46], refs[46:57], refs[57], refs[58]
+    lo, ig, pa, pb, n0, b0, act0, slope0, fout, table, in1, out1, qkv, ao, ci, co = held
+    LO, IG, ng, nb, w_in, w_out, w_rel, pos, w_dw, bng, bns = made
+    copies = []
+
+    def send(src, dst):
+        copy = pltpu.make_async_copy(src, dst, out_sems.at[len(copies)])
+        copy.start()
+        copies.append(copy)
+
+    given = [m.at[0] if i == 8 else m for i, m in enumerate(given)]
+    loads = [pltpu.make_async_copy(given[i], held[i], in_sems.at[i]) for i in range(len(held))]
+    for i in (5, 8, 7, 4, 6, 10, 11, 12, 14, 13, 15, 2, 3, 0, 1, 9):
         loads[i].start()
-    stores = []
-
-    def store(src, dst, sem):
-        copy = pltpu.make_async_copy(src, dst, out_sems.at[sem])
-        copy.start()
-        stores.append(copy)
-
-    def block(ref, i, n):
-        return ref[:, i * n : (i + 1) * n]
-
-    for i in (8, 9, 0, 1):
+    for i in (5, 8, 7, 4):
         loads[i].wait()
-    step = min(128, R)
-    for j, i in ((0, 0), (1, 3)):
-        c = slice(i * width, (i + 1) * width)
-        for r in range(0, R, step):
-            rows = slice(r, r + step)
-            h = dot(nall[rows, c], fin[j])
-            sig = jax.nn.sigmoid(h)
-            active[rows] = (h * sig).astype(bf16)
-            grad = dot(ball[rows, c], fout[j], 1, 1)
-            hidden[rows] = (grad * (sig * (1.0 + h * (1.0 - sig)))).astype(bf16)
-        w_in[j] = dot(nall[:, c], hidden[...], 0, 0)
-        store(w_in.at[j], outs[4].at[j], 4 if j == 0 else 14)
-        w_out[j] = dot(active[...], ball[:, c], 0, 0)
-        store(w_out.at[j], outs[5].at[j], 5 if j == 0 else 15)
-    for i in (2, 3, 4, 5, 6, 7, 10):
+    hidden = (dot(b0[...], fout[...], 1, 1) * slope0[...]).astype(bf16)
+    w_in[...] = dot(n0[...], hidden, 0, 0)
+    send(w_in, outs[4].at[0])
+    loads[6].wait()
+    w_out[...] = dot(act0[...], b0[...], 0, 0)
+    send(w_out, outs[5].at[0])
+    for i, dst in (
+        (10, outs[4].at[1]), (11, outs[5].at[1]), (12, outs[6].at[pl.ds(0, 3)]), (14, outs[9]), (13, outs[8]),
+        (15, outs[13]),
+    ):
         loads[i].wait()
-    qkv = dot(block(nall, 1, width), sb[:, 0 : 3 * C], 0, 0)
-    for i in range(3):
-        w_ain[i] = qkv[:, C * i : C * (i + 1)]
-    sums = pa[0].astype(f32)
+        send(held[i], dst)
+    for i in (2, 3, 0, 1, 9):
+        loads[i].wait()
+    sums, norms = pa[0].astype(f32), pb[0].astype(f32)
     for g in range(1, pa.shape[0]):
         sums += pa[g].astype(f32)
-    w_ain[3] = dot(table[...], sums[SMALL_ROWS:].astype(bf16), 0, 0)
-    store(w_ain, outs[6], 6)
-    gates = dot(block(nall, 2, width), sb[:, 3 * C : 5 * C], 0, 0)
-    for i in range(2):
-        w_cin[pl.ds(i, width, stride=2), :] = gates[:, C * i : C * (i + 1)]
-    store(w_cin, outs[9], 9)
-    w_aout[...] = dot(sf[:, 0:C], block(ball, 1, width), 0, 0)
-    store(w_aout, outs[8], 8)
-    w_cout[...] = dot(sf[:, C : 2 * C], block(ball, 2, width), 0, 0)
-    store(w_cout, outs[13], 13)
+        norms += pb[g].astype(f32)
+    w_rel[...] = dot(table[...], sums[SMALL_ROWS:].astype(bf16), 0, 0)
+    send(w_rel, outs[6].at[3])
     LO[...] = lo[...].astype(f32)
     IG[...] = ig[...].astype(f32)
-    norms = pb[0].astype(f32)
-    for g in range(1, pb.shape[0]):
-        norms += pb[g].astype(f32)
     for i in range(5):
         ng[i] = norms[i : i + 1]
         nb[i] = norms[8 + i : 9 + i]
@@ -905,9 +945,9 @@
     bns[...] = sums[3:4]
     for k in range(w_dw.shape[0]):
         w_dw[k] = sums[4 + k : 5 + k]
-    for i in (0, 1, 2, 3, 7, 10, 11, 12):
-        store(made[i], outs[i], i)
-    for copy in stores:
+    for i, src in ((0, LO), (1, IG), (2, ng), (3, nb), (7, pos), (10, w_dw), (11, bng), (12, bns)):
+        send(src, outs[i])
+    for copy in copies:
         copy.wait()
 
 
@@ -929,21 +969,27 @@
     def shape(dims, dtype=bf16):
         return jax.ShapeDtypeStruct(dims, dtype)
 
-    n_copies = 200 + 50 * (groups - 1) + 2 * dp
+    made_first = [
+        shape((width, width), f32), shape((width, width), f32), shape((3, width, C), f32), shape((C, width), f32),
+        shape((2 * width, C), f32), shape((C, width), f32),
+    ]
+    n_recv = 73 + 15 * (groups - 1)
+    n_send = 3 + 2 * (groups - 1) + 2 * max(groups - 2, 0)
     operands = (
         lengths, inputs, cotangent, norm_gain.transpose(1, 0, 2), norm_bias.transpose(1, 0, 2), ffn_in[0],
         ffn_out[0], attn_in[0], attn_out[0], conv_in.reshape(2 * width, C), conv_out[0], pos_bias[0], bn_gain,
         bn_shift, depthwise.transpose(1, 0, 2), table,
     )
-    nall, ball, sf, sb, lo, ig, pa, pb = pl.pallas_call(
+    lo, ig, pa, pb, n0, b0, act0, slope0, *ready = pl.pallas_call(
         lambda *refs: layer_kernel((frames, width, dp, groups), *refs),
         out_shape=[
-            shape((R, 4 * width)), shape((R, 4 * width)), shape((R, 2 * C)), shape((R, 5 * C)),
             shape((group * frames, width)), shape((group * frames, width)),
             shape((groups, sums_rows, C)), shape((groups, 16, width)),
-        ],
+            shape((R, width)), shape((R, width)), shape((R, width)), shape((R, width), f32),
+        ]
+        + made_first,
         in_specs=[hbm] * 16,
-        out_specs=[vm] * 8,
+        out_specs=[vm] * 4 + [hbm] * 10,
         scratch_shapes=[
             pltpu.VMEM((2, 4, width, width), bf16),
             pltpu.VMEM((2, 4, width, width), bf16),
@@ -988,9 +1034,21 @@
             pltpu.SMEM((group,), jnp.int32),
             pltpu.VMEM((2 * width, C), bf16),
             pltpu.VMEM((2 * width, C), f32),
-            pltpu.SemaphoreType.DMA((n_copies,)),
-            pltpu.SemaphoreType.DMA((n_copies,)),
+            pltpu.VMEM((R, 4 * width), bf16),
+            pltpu.VMEM((R, 4 * width), bf16),
+            pltpu.VMEM((R, 2 * C), bf16),
+            pltpu.VMEM((R, 5 * C), bf16),
+            pltpu.VMEM((2, R, width), bf16),
+            pltpu.VMEM((2, R, width), f32),
+            pltpu.VMEM((R, width), bf16),
+        ]
+        + [pltpu.VMEM(m.shape, m.dtype) for m in made_first]
+        + [
+            pltpu.VMEM((2**23 // 512, 128), f32),
+            pltpu.SemaphoreType.DMA((n_send,)),
+            pltpu.SemaphoreType.DMA((n_recv,)),
             pltpu.SemaphoreType.DMA((21,)),
+            pltpu.SemaphoreType.DMA((10,)),
         ],
         compiler_params=pltpu.CompilerParams(
             collective_id=0, has_side_effects=True, vmem_limit_bytes=62 * 2**20
@@ -1003,20 +1061,20 @@
         shape((4, width, C), f32), shape((2, C), f32), shape((C, width), f32), shape((2 * width, C), f32),
         shape((taps, 1, C), f32), shape((1, C), f32), shape((1, C), f32), shape((C, width), f32),
     ]
-    given = (nall, ball, sf, sb, lo, ig, pa, pb, ffn_in[0], ffn_out[0], table[2 * frames :])
+    given = (lo, ig, pa, pb, n0, b0, act0, slope0, ffn_out[0], table[2 * frames :], *ready)
+    held = list(given)
+    held[8] = shape((width, width))
+    made = [m for i, m in enumerate(gradients) if i not in (8, 9, 13)]
+    made[4] = made[5] = shape((width, width), f32)
+    made[6] = shape((width, C), f32)
     outs = pl.pallas_call(
-        gradient_kernel,
+        last_kernel,
         out_shape=gradients,
-        in_specs=[hbm] * len(given),
+        in_specs=[hbm] * 16,
         out_specs=[hbm] * len(gradients),
-        scratch_shapes=[pltpu.VMEM(m.shape, m.dtype) for m in given]
-        + [pltpu.VMEM(m.shape, m.dtype) for m in gradients]
-        + [
-            pltpu.VMEM((R, width), bf16),
-            pltpu.VMEM((R, width), bf16),
-            pltpu.SemaphoreType.DMA((len(given),)),
-            pltpu.SemaphoreType.DMA((len(gradients) + 2,)),
-        ],
+        scratch_shapes=[pltpu.VMEM(m.shape, m.dtype) for m in held]
+        + [pltpu.VMEM(m.shape, m.dtype) for m in made]
+        + [pltpu.SemaphoreType.DMA((len(given),)), pltpu.SemaphoreType.DMA((len(gradients) + 4,))],
         compiler_params=pltpu.CompilerParams(vmem_limit_bytes=62 * 2**20),
     )(*given)
     if groups == 1:

time: 121 us -> 112 us (0.926)
  Pallas kernels: 120 us -> 111 us
    pallas_call x1, Pallas kernels: 112 us -> 105 us  [on_device(): pl.pallas_call(lambda *refs: layer_kernel((frames, width, dp, groups), *r...]
    pallas_call x1, Pallas kernels: 8.35 us -> 5.77 us  [on_device(): pl.pallas_call(last_kernel, out_shape=gradients, in_specs=[hbm] * 16, out...]
where the time goes in v3:
time: 112 us
  Pallas kernels  111 us (99%)
    pallas_call x1, Pallas kernels, on_device(): pl.pallas_call(lambda *refs: layer_kernel((frames, width, dp, groups), *r...  105 us
    pallas_call x1, Pallas kernels, on_device(): pl.pallas_call(last_kernel, out_shape=gradients, in_specs=[hbm] * 16, out...  5.77 us

profile of v3, /device:TPU:0, one launch (start us, length us, event | category | flops | bytes accessed | tf_op | source)
XLA Modules:
  0.0 111.6 jit_solution(10029786305363197323)
XLA Ops:
  0.7 105.0 %shard_map.263 = (bf16[128,512]{1,0:T(8,128)(2,1)}, bf16[128,512]{1,0:T(8,128)(2,1)}, bf16[4,112,128]{2,1,0:T(8,128)(2,1)}, bf16[4,16,512]{2,1,0:T(8,128)(2,1)},...) custom-call(s32[4]{0:T(128)} %refs_0_.1, ...), custom_call_target="tpu_custom_call" | custom-call | tf_op jit(solution)/shard_map/pallas_call | solution.py:983
  105.7 5.8 %shard_map.264 = (f32[128,512]{1,0:T(8,128)}, f32[128,512]{1,0:T(8,128)}, f32[5,1,512]{2,1,0:T(1,128)}, f32[5,1,512]{2,1,0:T(1,128)}, f32[2,512,512]{2,1,0:T(8,1...) custom-call(bf16[128,512]{1,0:T(8,128)(2,1)} %get-tuple-element.42.r, ...), custom_call_target="tpu_custom_call" | custom-call | tf_op jit(solution)/shard_map/pallas_call | solution.py:1070

commit v4 on v3

--- a/solution.py
+++ b/solution.py
@@ -14,6 +14,12 @@
 SECTION, TENSOR, DATA = "section", "tensor", "dp"
 PLACE = (0, 2, 1, 3)
 SMALL_ROWS = 48
+
+
+def relative_at(groups):
+    return 16 if groups > 1 else SMALL_ROWS
+
+
 bf16, f32 = jnp.bfloat16, jnp.float32
 
 
@@ -38,14 +44,17 @@
     T, width, dp, groups = dims
     C = width // 4
     (lengths, inputs, cot, ng_in, nb_in, fin, fout, ain, aout, cin, cout, pos_in, bng_in, bns_in, dw_in, e2_in) = refs[:16]
-    (LO, IG, PA, PB, n0_out, b0_out, act0_out, slope0_out, in1_out, out1_out, qkv_out, ao_out, ci_out, co_out) = refs[16:30]
-    refs = refs[30:]
+    (LO, IG, PA, PB, CS, n0_out, b0_out, act0_out, slope0_out) = refs[16:25]
+    (in1_out, out1_out, qkv_out, ao_out, ci_out, co_out) = refs[25:31]
+    refs = refs[31:]
     (Win, Wout, Wqkv, Wr, Wo, Wci, Wco, R2, SM) = refs[:9]
     (H, XH, RS, X, G, ARR, HOP, QKV, PRB, GVG, CT, UP, DP) = refs[9:22]
     (SfSt, SbSt, PAst, PAb, PAin, PBst, PBin, STF, STB, RSst, RSin) = refs[22:33]
     (ng, nb, pos, bng, bns, dw, e2, lens, pairs, spread) = refs[33:43]
     (Nall, Ball, Sf, Sb, ACT, SLOPE, HG, gin1, gout1, gqkv, gao, gci, gco) = refs[43:56]
-    dummy, ss, rs, ls, os = refs[56:61]
+    GA, HATA, UA, DYA, DA, DWACC, INVA = refs[56:63]
+    dummy, ss, rs, ls, os = refs[63:68]
+    gathered = groups > 1
 
     s, t, d = lax.axis_index(SECTION), lax.axis_index(TENSOR), lax.axis_index(DATA)
     first, second = s == 0, s == 1
@@ -185,18 +194,21 @@
         for w in ("own", "other"):
             lines(at, n, w)
     only = {i: second for i in range(4)}
+    over_y = {i: "own" for i in range(14)}
 
     def send_chunks(names):
         for i in names:
             src, dst = chunks[i]
             start(("sib", i), lambda src=src: src(None), lambda dst=dst: dst(1, None), sib, only.get(i))
-            start(("y", i), lambda src=src: src("own"), lambda dst=dst: dst(2, "own"), yp, only.get(i))
+            w = over_y.get(i)
+            start(("y", i), lambda src=src, w=w: src(w), lambda dst=dst, w=w: dst(2, w), yp, only.get(i))
 
     def step_a(i):
-        dst = chunks[i][1]
-        arrived(("y", i), dst(2, "own"))
-        start(("z", i), lambda: dst(2, "own"), lambda: dst(2, "own"), zpair, only.get(i))
-        start(("sib", i), lambda: dst(2, "own"), lambda: dst(3, "own"), sib, only.get(i), 1)
+        dst, w = chunks[i][1], over_y.get(i)
+        arrived(("y", i), dst(2, w))
+        if w:
+            start(("z", i), lambda: dst(2, w), lambda: dst(2, w), zpair, only.get(i))
+        start(("sib", i), lambda: dst(2, w), lambda: dst(3, w), sib, only.get(i), 1)
 
     def step_b(i):
         dst = chunks[i][1]
@@ -286,24 +298,14 @@
 
     @pl.when(first)
     def _():
-        send_chunks((4,))
         pltpu.make_async_copy(inputs.at[t], X.at[0], ls.at[20]).wait()
         Nall[own, 0:width] = norm(0, X[0]).astype(bf16)
         to_tensor(("n", 0), Nall, block(0))
-        send_chunks((5,))
 
     @pl.when(second)
     def _():
         send_chunks(range(4))
         pltpu.make_async_copy(cot.at[t], G, ls.at[20]).wait()
-
-    fetched("in0", "out0")
-
-    @pl.when(first)
-    def _():
-        X[1] = shared_feed(0, 0)
-        send_chunks((6,))
-        step_a(4)
 
     fetched("pos", "bng", "bns", "dw", "wr", "e2", "len", "ci")
     spread[...] = pairs[...].astype(f32)
@@ -316,20 +318,29 @@
     for k in range(taps):
         SM[4 + k : 5 + k, 0:C] = dw[k]
     R2[:, 0:C] = dot(e2[...], Wr[...]).astype(bf16)
+    fetched("in0", "out0")
+
+    @pl.when(first)
+    def _():
+        send_chunks((8,))
+        X[1] = shared_feed(0, 0)
+        send_chunks((9, 10))
+
     for k in (1, 2, 3):
         start("small", lambda: SM.at[:, cols(0)], lambda k=k: SM.at[:, cols(k)], peers[k], None, k)
-        start("small", lambda: R2.at[:, cols(0)], lambda k=k: R2.at[:, cols(k)], peers[k], None, 3 + k)
-    @pl.when(first)
-    def _():
-        send_chunks(range(7, 13))
-        step_a(5)
+
+    def send_relative():
+        for k in (1, 2, 3):
+            start("rel", lambda: R2.at[:, cols(0)], lambda k=k: R2.at[:, cols(k)], peers[k], None, k)
+
+    @pl.when(first)
+    def _():
+        step_a(8)
         X[1] = X[0] + 0.5 * summed_here(("s", 0), 0, X[1])
-        step_a(6)
-        step_b(4)
-        step_b(5)
 
     @pl.when(second)
     def _():
+        send_relative()
         send_chunks(range(4, 15))
 
     fetched("qkv", "o", "co", "in1", "out1")
@@ -338,10 +349,15 @@
     DP[...] = jnp.zeros(DP.shape, f32)
     PAst[...] = jnp.zeros(PAst.shape, f32)
     PBst[...] = jnp.zeros(PBst.shape, f32)
-
-    length = lens[t]
-    row_mask = (lax.broadcasted_iota(jnp.int32, (T, 1), 0) < length).astype(f32)
-    key_mask = lax.broadcasted_iota(jnp.int32, (2 * T, T), 1) < length
+    CS[...] = jnp.zeros(CS.shape, f32)
+    if gathered:
+        DA[...] = jnp.zeros(DA.shape, f32)
+        DWACC[...] = jnp.zeros(DWACC.shape, f32)
+
+    def keys_of(length):
+        return lax.broadcasted_iota(jnp.int32, (2 * T, T), 1) < length
+
+    row_mask = (lax.broadcasted_iota(jnp.int32, (T, 1), 0) < lens[t]).astype(f32)
     first_head = lax.broadcasted_iota(jnp.int32, (T, 2 * HEAD), 1) < HEAD
     flip = (
         lax.broadcasted_iota(jnp.int32, (T, 4 * T), 0) + lax.broadcasted_iota(jnp.int32, (T, 4 * T), 1)
@@ -354,43 +370,9 @@
     def unpair(v):
         return jnp.where(first_head, v[:T], v[T:])
 
-    @pl.when(second)
-    def _():
-        for i in range(14):
-            step_a(i)
-            if i > 1:
-                step_b(i - 2)
-        for i in range(7):
-            step_c(i)
-        arrived("hop", ARR)
-        X[0] = ARR[...].astype(f32)
-        feed(0, 0, 0, 1)
-
-    def send_rows_second(i):
-        @pl.when(second)
-        def _():
-            to_tensor(("n", i), Nall, block(i))
-
-    x = X[1]
-    a = norm(1, x).astype(bf16)
-    Nall[own, width : 2 * width] = a
-    send_rows_second(1)
-    steps(second, (A, 14), (B, 12))
-    steps(first, (W, 4), (W, 5))
-    all_arrived("small", 3 * (size_of(SM.at[:, cols(0)]) + size_of(R2.at[:, cols(0)])))
-    steps(first, (A, 7), (B, 6), (W, 6))
-    q = dot(a, Wqkv[0])
-    QKV[0] = q + SM[0:1]
-    QKV[1] = q + SM[1:2]
-    QKV[2] = dot(a, Wqkv[1])
-    QKV[3] = dot(a, Wqkv[2])
-    mixed = []
-    for p in range(4):
-        c = pl.ds(2 * HEAD * p, 2 * HEAD)
-        qu = pair_rows(QKV[0, :, c]).astype(bf16)
-        qv = pair_rows(QKV[1, :, c]).astype(bf16)
-        content = dot(qu, QKV[2, :, c].astype(bf16), 1, 1)
-        whole = dot(qv, R2[:, c], 1, 1)
+    def attend(qu, qv, key, value, relative, keys):
+        content = dot(pair_rows(qu).astype(bf16), key, 1, 1)
+        whole = dot(pair_rows(qv).astype(bf16), relative, 1, 1)
         placed = jnp.concatenate(
             [
                 pltpu.roll(whole[e * T : (e + 1) * T], 4 * T - (T - 1), 1, stride=1, stride_axis=0)[:, :T]
@@ -398,25 +380,103 @@
             ],
             0,
         )
-        scores = jnp.where(key_mask, (content + placed) * HEAD ** (-0.5), -1e30)
+        scores = jnp.where(keys, (content + placed) * HEAD ** (-0.5), -1e30)
         e = jnp.exp(scores - jnp.max(scores, -1, keepdims=True))
         probs = e / jnp.sum(e, -1, keepdims=True)
-        PRB[p] = probs
-        mixed.append(unpair(dot(probs.astype(bf16), QKV[3, :, c].astype(bf16))).astype(bf16))
-    for k in range(4):
-        SfSt[k, :, 0:C] = mixed[k]
-    steps(first, (A, 8), (B, 7), (A, 9))
-    step_c(7)
-    total = dot(mixed[0], Wo[0:C])
-    for k in range(1, 4):
-        total += dot(mixed[k], Wo[C * k : C * (k + 1)])
-    x = x + total
-    X[2] = x
-
-    a = norm(2, x).astype(bf16)
+        return probs, unpair(dot(probs.astype(bf16), value)).astype(bf16)
+
+    def attention_here():
+        a = Nall[own, width : 2 * width]
+        q = dot(a, Wqkv[0])
+        QKV[0] = q + SM[0:1]
+        QKV[1] = q + SM[1:2]
+        QKV[2] = dot(a, Wqkv[1])
+        QKV[3] = dot(a, Wqkv[2])
+        keys, mixed = keys_of(lens[t]), []
+        for p in range(4):
+            c = pl.ds(2 * HEAD * p, 2 * HEAD)
+            probs, out = attend(
+                QKV[0, :, c], QKV[1, :, c], QKV[2, :, c].astype(bf16), QKV[3, :, c].astype(bf16), R2[:, c], keys
+            )
+            PRB[p] = probs
+            mixed.append(out)
+        return mixed
+
+    def shared_attention():
+        a = Nall[four, width : 2 * width]
+        q, key, value = (dot(a, Wqkv[i, :, 0:C]) for i in range(3))
+        qu, qv, key, value = q + SM[0:1, 0:C], q + SM[1:2, 0:C], key.astype(bf16), value.astype(bf16)
+        mixed = []
+        for p in range(4):
+            rows = slice(T * p, T * (p + 1))
+            keys = keys_of(lens[t ^ PLACE[p]])
+            mixed.append(attend(qu[rows], qv[rows], key[rows], value[rows], R2[:, 0:C], keys)[1])
+        mixed = jnp.concatenate(mixed, 0)
+        Sf[four, 0:C] = mixed
+        return sum_to_owner(("s", 3), 3, dot(mixed, Wo[0:C]))
+
+    def small_arrived():
+        all_arrived("small", 3 * size_of(SM.at[:, cols(0)]))
+
+    def relative_arrived():
+        all_arrived("rel", 3 * size_of(R2.at[:, cols(0)]))
+
+
+    @pl.when(first)
+    def _():
+        Nall[own, width : 2 * width] = norm(1, X[1]).astype(bf16)
+        to_tensor(("n", 1), Nall, block(1))
+        send_chunks((4, 5))
+        step_a(9)
+        step_a(10)
+        step_b(8)
+        step_b(9)
+        from_tensor(("n", 1), Nall, block(1))
+        total = shared_attention()
+        send_chunks((6,))
+        send_relative()
+        send_chunks((7,))
+        step_b(10)
+        X[2] = X[1] + summed_here(("s", 3), 3, total)
+        small_arrived()
+
+    @pl.when(second)
+    def _():
+        for i in range(13):
+            step_a(i)
+            if i > 1:
+                step_b(i - 2)
+        for i in range(7):
+            step_c(i)
+        small_arrived()
+        relative_arrived()
+        arrived("hop", ARR)
+        X[0] = ARR[...].astype(f32)
+        feed(0, 0, 0, 1)
+        Nall[own, width : 2 * width] = norm(1, X[1]).astype(bf16)
+        to_tensor(("n", 1), Nall, block(1))
+        step_b(11)
+        mixed = attention_here()
+        step_a(13)
+        step_b(12)
+        for k in range(4):
+            SfSt[k, :, 0:C] = mixed[k]
+        step_c(7)
+        X[2] = X[1] + dot(jnp.concatenate(mixed, 1), Wo[...])
+
+    def send_rows_second(i):
+        @pl.when(second)
+        def _():
+            to_tensor(("n", i), Nall, block(i))
+
+    a = norm(2, X[2]).astype(bf16)
     Nall[own, 2 * width : 3 * width] = a
     send_rows_second(2)
-    steps(first, (B, 8), (A, 10), (B, 9))
+
+    @pl.when(first)
+    def _():
+        send_chunks((11,))
+
     step_c(8)
     step_c(9)
     GVG[0] = dot(a, Wci[0])
@@ -449,18 +509,24 @@
 
     masked = conv * row_mask
     frames_row = jnp.broadcast_to(total_of(row_mask), (1, width))
-    dp_sums("bnf", STF, [total_of(masked), total_of(masked * conv), frames_row])
-    steps(first, (B, 10))
+    lengths_row = jnp.concatenate(
+        [jnp.broadcast_to(lens[t ^ PLACE[p]].astype(f32), (1, C)) for p in range(4)], 1
+    )
+    dp_sums("bnf", STF, [total_of(masked), total_of(masked * conv), frames_row, lengths_row])
+    steps(second, (A, 14))
     step_c(10)
     sums = summed("bnf", STF)
+    steps(first, (A, 4), (A, 5), (A, 6))
+    steps(second, (B, 13))
     count = sums[2:3]
     bn_mean = sums[0:1] / count
     inv_std = lax.rsqrt(sums[1:2] / count - bn_mean * bn_mean + EPSILON)
     hat = (conv - bn_mean) * inv_std
     CT[...] = hat
     active = silu(hat * SM[2:3] + SM[3:4]).astype(bf16)
-    for k in range(4):
-        SfSt[k, :, C : 2 * C] = active[:, C * k : C * (k + 1)]
+    if not gathered:
+        for k in range(4):
+            SfSt[k, :, C : 2 * C] = active[:, C * k : C * (k + 1)]
     X[3] = X[2] + dot(active, Wco[...])
 
     @pl.when(first)
@@ -468,15 +534,14 @@
         Nall[own, 3 * width : 4 * width] = norm(3, X[3]).astype(bf16)
         to_tensor(("n", 3), Nall, block(3))
         total = shared_feed(1, 3)
-        send_chunks((13, 14))
+        send_chunks((12, 13, 14))
+        step_a(7)
         step_a(11)
-        step_a(12)
+        step_b(4)
         X[4] = X[3] + 0.5 * summed_here(("s", 1), 1, total)
 
     @pl.when(second)
     def _():
-        for i in (13, 14):
-            step_b(i)
         for i in range(11, 15):
             step_c(i)
         feed(1, 3, 3, 4)
@@ -547,15 +612,12 @@
         all_arrived((name, 2, 0), 2 * (groups - 1) * size_of(ref.at[own, c]))
 
     every = block(0, 4)
-    sf_cols = pl.ds(0, 2 * C)
+    sf_cols = pl.ds(0, C if gathered else 2 * C)
     qkv_cols, gate_cols = pl.ds(0, 3 * C), pl.ds(3 * C, 2 * C)
     lines_of = {
         "n": (rows_region(Nall, T, every), share(Nall, every)),
         "sf": (rows_region(Sf, R4, sf_cols), None),
-        "gates": (rows_region(Sb, R4, gate_cols), None),
         "qkv": (rows_region(Sb, R4, qkv_cols), None),
-        "pa": (lambda j: PA.at[around[j] if groups > 1 else 0], None),
-        "pb": (lambda j: PB.at[around[j] if groups > 1 else 0], None),
     }
     for i in range(4):
         lines_of["b", i] = (rows_region(Ball, T, block(i)), share(Ball, block(i)))
@@ -573,9 +635,13 @@
             ref, c = (Nall, every) if name == "n" else (Ball, block(name[1]))
             share_on(name, ref, c, n)
 
-    Sf[own] = SfSt[0]
-    for k in (1, 2, 3):
-        start("sf", lambda k=k: SfSt.at[k], lambda k=k: Sf.at[place(k)], peers[k], None, k)
+    for cond, c in ((first, pl.ds(C, C)), (second, sf_cols))[gathered:]:
+
+        @pl.when(cond)
+        def _():
+            Sf[own, c] = SfSt[0, :, c]
+            for k in (1, 2, 3):
+                start("sf", lambda k=k: SfSt.at[k, :, c], lambda k=k: Sf.at[place(k), c], peers[k], cond, k)
 
     written = []
 
@@ -606,6 +672,86 @@
         gout1[...] = dot(ACT[1], Ball[:, c], 0, 0)
         write(gout1, out1_out)
 
+    def mask_of(g, p):
+        return (lax.broadcasted_iota(jnp.int32, (T, C), 0).astype(f32) < STF[g, 3:4, C * p : C * (p + 1)]).astype(f32)
+
+    places = [(p, [(g, slice(R4 * g + T * p, R4 * g + T * (p + 1))) for g in range(groups)]) for p in range(4)]
+
+    def convolution_rows():
+        for i in range(2):
+            GA[i] = dot(Nall[:, 2 * width : 3 * width], Wci[i, :, 0:C])
+        UA[...] = jnp.zeros(UA.shape, f32)
+        for p, parts in places:
+            for g, rows in parts:
+                UA[4 * g + p, margin : margin + T] = GA[0, rows] * jax.nn.sigmoid(GA[1, rows]) * mask_of(g, p)
+
+        def one(b, carry):
+            acc = SM[4:5, 0:C] * UA[b, margin - taps // 2 : margin - taps // 2 + T]
+            for k in range(1, taps):
+                o = margin - taps // 2 + k
+                acc += SM[4 + k : 5 + k, 0:C] * UA[b, o : o + T]
+            HATA[pl.ds(b * T, T)] = acc
+            return carry
+
+        lax.fori_loop(0, 4 * groups, one, 0)
+        for p, parts in places:
+            n = sum(STF[g, 3:4, C * p : C * (p + 1)] for g, _ in parts)
+            masked = [HATA[rows] * mask_of(g, p) for g, rows in parts]
+            mean = sum(total_of(m) for m in masked) / n
+            square = sum(total_of(m * HATA[rows]) for m, (_, rows) in zip(masked, parts)) / n
+            inv = lax.rsqrt(square - mean * mean + EPSILON)
+            INVA[p, 0:1] = inv
+            INVA[p, 1:2] = n
+            for g, rows in parts:
+                h = (HATA[rows] - mean) * inv
+                HATA[rows] = h
+                Sf[rows, C : 2 * C] = silu(h * SM[2:3, 0:C] + SM[3:4, 0:C]).astype(bf16)
+
+    def convolution_rows_back():
+        DYA[...] = dot(Ball[:, 2 * width : 3 * width], Wco[0:C], 1, 1)
+        gain_sum = shift_sum = jnp.zeros((1, C), f32)
+        for p, parts in places:
+            first_sum = second_sum = jnp.zeros((1, C), f32)
+            for g, rows in parts:
+                h = HATA[rows]
+                y = h * SM[2:3, 0:C] + SM[3:4, 0:C]
+                dy = DYA[rows] * slope(y, jax.nn.sigmoid(y))
+                gain_sum += total_of(dy * h)
+                shift_sum += total_of(dy)
+                dh = dy * SM[2:3, 0:C]
+                DYA[rows] = dh
+                dh = dh * mask_of(g, p)
+                first_sum += total_of(dh)
+                second_sum += total_of(dh * h)
+            inv, n = INVA[p, 0:1], INVA[p, 1:2]
+            for g, rows in parts:
+                dc = inv * (DYA[rows] - (first_sum + HATA[rows] * second_sum) / n) * mask_of(g, p)
+                DA[4 * g + p, margin : margin + T] = dc
+        CS[taps : taps + 1] = gain_sum
+        CS[taps + 1 : taps + 2] = shift_sum
+
+        def one(b, carry):
+            here = DA[b, margin : margin + T]
+            acc = jnp.zeros((T, C), f32)
+            for k in range(taps):
+                o = margin + taps // 2 - k
+                acc += SM[4 + k : 5 + k, 0:C] * DA[b, o : o + T]
+                o = margin - taps // 2 + k
+                term = here * UA[b, o : o + T]
+                DWACC[k] += sum(term[8 * i : 8 * (i + 1)] for i in range(T // 8))
+            DYA[pl.ds(b * T, T)] = acc
+            return carry
+
+        lax.fori_loop(0, 4 * groups, one, 0)
+        for k in range(taps):
+            CS[k : k + 1] = total_of(DWACC[k])
+        for p, parts in places:
+            for g, rows in parts:
+                sig = jax.nn.sigmoid(GA[1, rows])
+                dua = DYA[rows] * mask_of(g, p)
+                Sb[rows, 3 * C : 4 * C] = (dua * sig).astype(bf16)
+                Sb[rows, 4 * C : 5 * C] = (dua * GA[0, rows] * (sig * (1.0 - sig))).astype(bf16)
+
     def convolution_grads():
         gates = dot(Nall[:, 2 * width : 3 * width], Sb[:, 3 * C : 5 * C], 0, 0)
         for i in range(2):
@@ -624,29 +770,31 @@
 
     @pl.when(first)
     def _():
-        set_off("n")
-        for i in (1, 2):
-            to_tensor(("n", i), Nall, block(i))
+        set_off("n", "sf")
+        to_tensor(("n", 2), Nall, block(2))
+        for i in (5, 6, 7):
+            step_b(i)
+        step_a(12)
         step_b(11)
+        for i in (4, 5, 6, 7):
+            step_c(i)
+        relative_arrived()
+        attention_here()
+        step_a(13)
         step_b(12)
-        from_tensor("sf", Sf, sf_cols)
-        set_off("sf")
-        step_a(13)
+        if not gathered:
+            from_tensor("sf", Sf, pl.ds(C, C))
+        step_a(14)
         hop(1, "n", "sf")
-        step_a(14)
         step_b(13)
-        hop(2, "n", "sf")
-        step_b(14)
         for i in range(11, 15):
             step_c(i)
         for k in range(4):
             H[1, k] = dot(Nall[own, 3 * width : 4 * width], Win[1, k])
+        hop(2, "n", "sf")
         hand_on(1, "n")
         hop(3, "n", "sf")
-        for i in (1, 2):
-            from_tensor(("n", i), Nall, block(i))
         hand_on(2, "n")
-        hand_on(3, "n")
 
     @pl.when(first)
     def _():
@@ -659,6 +807,8 @@
         b = (0.5 * g).astype(bf16)
         Ball[own, i * width : (i + 1) * width] = b
         to_tensor(("b", i), Ball, block(i))
+        if j:
+            set_off(("b", i))
         grad = None
         for k in range(4):
             h = H[j, k]
@@ -676,8 +826,9 @@
     y = hat * SM[2:3] + SM[3:4]
     sig = jax.nn.sigmoid(y)
     dy = dot(b, Wco[...], 1, 1) * slope(y, sig)
-    PAst[2:3] = total_of(dy * hat)
-    PAst[3:4] = total_of(dy)
+    if not gathered:
+        PAst[2:3] = total_of(dy * hat)
+        PAst[3:4] = total_of(dy)
     dhat = dy * SM[2:3]
     masked = dhat * row_mask
     dp_sums("bnb", STB, [total_of(masked), total_of(masked * hat)])
@@ -689,7 +840,12 @@
         from_tensor("sf", Sf, sf_cols)
         set_off("sf")
 
-    set_off(("b", 3), ("b", 2))
+    @pl.when(first)
+    def _():
+        hop(1, ("b", 3))
+        hand_on(3, "n")
+
+    set_off(("b", 2))
     dc = inv_std * (dhat - (sums[0:1] + hat * sums[1:2]) / count) * row_mask
     DP[margin : margin + T] = dc
     for p in range(4):
@@ -700,23 +856,24 @@
             o = margin + taps // 2 - k
             term = SM[4 + k : 5 + k, c] * DP[o : o + T, c]
             acc = term if acc is None else acc + term
-            o = margin - taps // 2 + k
-            PAst[4 + k : 5 + k, c] = total_of(here * UP[o : o + T, c])
+            if not gathered:
+                o = margin - taps // 2 + k
+                PAst[4 + k : 5 + k, c] = total_of(here * UP[o : o + T, c])
         CT[:, c] = acc
     du = CT[...] * row_mask
     sig = jax.nn.sigmoid(GVG[1])
     dvalue = (du * sig).astype(bf16)
     dgate = (du * GVG[0] * (sig * (1.0 - sig))).astype(bf16)
-    for k in range(4):
-        SbSt[k, :, 3 * C : 4 * C] = dvalue[:, C * k : C * (k + 1)]
-        SbSt[k, :, 4 * C : 5 * C] = dgate[:, C * k : C * (k + 1)]
-    Sb[own, 3 * C : 5 * C] = SbSt[0, :, 3 * C : 5 * C]
-
     def sb_to_tensor(name, c):
         for k in (1, 2, 3):
             start(name, lambda k=k: SbSt.at[k, :, c], lambda k=k: Sb.at[place(k), c], peers[k], None, k)
 
-    sb_to_tensor("gates", gate_cols)
+    if not gathered:
+        for k in range(4):
+            SbSt[k, :, 3 * C : 4 * C] = dvalue[:, C * k : C * (k + 1)]
+            SbSt[k, :, 4 * C : 5 * C] = dgate[:, C * k : C * (k + 1)]
+        Sb[own, 3 * C : 5 * C] = SbSt[0, :, 3 * C : 5 * C]
+        sb_to_tensor("gates", gate_cols)
     g = g + norm_back(2, dot(dvalue, Wci[0], 1, 1) + dot(dgate, Wci[1], 1, 1))
     b = g.astype(bf16)
     Ball[own, width : 2 * width] = b
@@ -749,7 +906,7 @@
         dq.append((du_rows + dv_rows).astype(bf16))
         PAst[0:1, c] = total_of(du_rows)
         PAst[1:2, c] = total_of(dv_rows)
-        PAst[SMALL_ROWS : SMALL_ROWS + 2 * T, c] = dot(whole, qv, 0, 0) * scale
+        PAst[relative_at(groups) : relative_at(groups) + 2 * T, c] = dot(whole, qv, 0, 0) * scale
     for k in range(4):
         SbSt[k, :, 0:C] = dq[k]
         SbSt[k, :, C : 2 * C] = dk[k]
@@ -760,9 +917,10 @@
 
     @pl.when(first)
     def _():
-        from_tensor("gates", Sb, gate_cols)
-        set_off("gates")
-        hop(1, ("b", 3), ("b", 2))
+        if not gathered:
+            from_tensor("gates", Sb, gate_cols)
+        hop(2, ("b", 3))
+        hop(1, ("b", 2))
     grad = dot(jnp.concatenate(dq, 1), Wqkv[0], 1, 1)
     grad += dot(jnp.concatenate(dk, 1), Wqkv[1], 1, 1)
     grad += dot(jnp.concatenate(dv, 1), Wqkv[2], 1, 1)
@@ -784,106 +942,116 @@
     for k in (1, 2, 3):
         start("pa", lambda k=k: PAb.at[:, cols(k)], lambda k=k: PAin.at[k], peers[k], None, k)
 
+    def sums_over_tensor(name, parts, ref):
+        all_arrived(name, 3 * size_of(parts.at[0]))
+        ref[mine] = sum(parts[k].astype(f32) for k in range(4)).astype(bf16)
+        for r in range(1, groups):
+            start((name, 3), lambda: ref.at[mine], lambda: ref.at[mine], zpeers[r], None, r)
+
+    def send_ends():
+        PBin[t] = PBst[...].astype(bf16)
+        for k in (1, 2, 3):
+            start("pb", lambda: PBin.at[t], lambda: PBin.at[t], peers[k], None, k)
+            start("grad", back_rows, back_rows, peers[k], None, k)
+
+    bs = [("b", i) for i in range(4)]
+    if not gathered:
+
+        @pl.when(second)
+        def _():
+            from_tensor("gates", Sb, gate_cols)
+
+    @pl.when(first)
+    def _():
+        from_tensor(("n", 2), Nall, block(2))
+        shared("n", Nall, every)
 
     @pl.when(second)
     def _():
-        from_tensor("gates", Sb, gate_cols)
-        set_off("gates")
-
-    @pl.when(first)
-    def _():
+        send_ends()
+        from_tensor("qkv", Sb, qkv_cols)
+        set_off("qkv")
+        hop(1, "n", "sf", bs[3], bs[2], bs[1], bs[0], "qkv")
+        hop(2, "n", "sf")
+        hand_on(1, "n")
+        hop(2, bs[3], bs[2], bs[1], bs[0], "qkv")
+        hand_on(1, bs[3], bs[2])
+        hop(3, "n", "sf")
+        hand_on(2, "n")
+        hand_on(1, bs[1], bs[0])
+        hop(3, bs[3], bs[2])
+        hand_on(3, "n")
+        hand_on(2, bs[3], bs[2], bs[1], bs[0])
+        hop(3, bs[1], bs[0])
+        for i in range(4):
+            from_tensor(("n", i), Nall, block(i))
         shared("n", Nall, every)
-        hidden_rows(1, 3)
-
-    from_tensor("qkv", Sb, qkv_cols)
-    set_off("qkv")
-
-    @pl.when(first)
-    def _():
-        hidden_rows(0, 0)
-        from_tensor(("b", 0), Ball, block(0))
+    hidden_rows(1, 3)
+
+    @pl.when(first)
+    def _():
+        from_tensor("qkv", Sb, qkv_cols)
+        set_off("qkv")
+        hop(2, bs[2])
+        hop(3, bs[3])
+        hop(1, bs[1])
+        from_tensor(bs[0], Ball, block(0))
         h = dot(Nall[four, 0:width], Win[0, 0])
         sig = jax.nn.sigmoid(h)
         hg = dot(Ball[four, 0:width], Wout[0, 0], 1, 1) * slope(h, sig)
-        total = sum_to_owner("s2", 2, dot(hg.astype(bf16), Win[0, 0], 1, 1))
-        hop(2, ("b", 3), ("b", 2))
-        hop(1, "gates", ("b", 1))
-        hand_on(1, ("b", 3), ("b", 2))
-        g = G[...] + norm_back(0, summed_here("s2", 2, total))
-        IG[pl.ds(trow, T)] = g.astype(bf16)
-
-    PBin[t] = PBst[...].astype(bf16)
-    for k in (1, 2, 3):
-        start("pb", lambda: PBin.at[t], lambda: PBin.at[t], peers[k], None, k)
-        start("grad", back_rows, back_rows, peers[k], None, k)
-    PAin[0] = PAb[:, 0:C]
-    all_arrived("pa", 3 * size_of(PAin.at[0]))
-    PA[mine] = sum(PAin[k].astype(f32) for k in range(4)).astype(bf16)
-    set_off("pa")
-
-    @pl.when(second)
-    def _():
-        for n in (1, 2):
-            hop(n, "n", "sf", ("b", 3), ("b", 2))
-        hand_on(1, "n", ("b", 3), ("b", 2))
-        hop(1, "gates", ("b", 1))
-    hop(1, ("b", 0), "qkv")
-    hop(3, ("b", 3), ("b", 2))
-    hop(2, "gates", ("b", 1))
-    all_arrived("pb", 3 * size_of(PBin.at[0]))
-    PB[mine] = sum(PBin[k].astype(f32) for k in range(4)).astype(bf16)
-    set_off("pb")
-    hop(1, "pa")
-    hand_on(1, ("b", 1), ("b", 0))
-    hand_on(2, ("b", 3), ("b", 2))
-
-    @pl.when(second)
-    def _():
-        hop(3, "n", "sf")
-        hand_on(2, "n")
-    hop(2, ("b", 0), "qkv")
-    hop(3, "gates", ("b", 1))
-    hop(1, "pb")
-    hop(2, "pa")
-    hand_on(2, ("b", 1), ("b", 0))
-    hand_on(3, ("b", 3), ("b", 2))
-
-    @pl.when(second)
-    def _():
-        hand_on(3, "n")
-    hop(3, ("b", 0))
-
-    @pl.when(second)
-    def _():
-        for i in range(4):
-            from_tensor(("n", i), Nall, block(i))
-        shared("n", Nall, every)
-        hidden_rows(1, 3)
-        hidden_rows(0, 0)
-
+        X[0] = sum_to_owner(("s", 2), 2, dot(hg.astype(bf16), Win[0, 0], 1, 1))
+        hop(1, bs[0])
+        hand_on(1, bs[3], bs[2])
+    hidden_rows(0, 0)
     write(Nall.at[:, block(0)], n0_out)
     write(ACT.at[0], act0_out)
     write(SLOPE.at[0], slope0_out)
+    if gathered:
+        convolution_rows()
+
+    @pl.when(first)
+    def _():
+        hop(1, "qkv")
+        hop(3, bs[2])
+        hop(2, bs[1])
+        g = G[...] + norm_back(0, summed_here(("s", 2), 2, X[0]))
+        IG[pl.ds(trow, T)] = g.astype(bf16)
+        send_ends()
+        hop(2, bs[0])
+        hand_on(1, bs[1], bs[0])
+        hand_on(2, bs[3], bs[2])
+
+    PAin[0] = PAb[:, 0:C]
+    sums_over_tensor("pa", PAin, PA)
+    hand_on(3, bs[3], bs[2])
     for i in (3, 2):
-        from_tensor(("b", i), Ball, block(i))
-        shared(("b", i), Ball, block(i))
+        from_tensor(bs[i], Ball, block(i))
+        shared(bs[i], Ball, block(i))
     second_feed_grads()
-    hand_on(3, ("b", 1), ("b", 0))
+    sums_over_tensor("pb", PBin, PB)
+
+    @pl.when(first)
+    def _():
+        hop(2, "qkv")
+        hop(3, bs[1], bs[0])
+        hand_on(2, bs[1], bs[0])
+    if gathered:
+        convolution_rows_back()
     hop(3, "qkv")
-    hop(2, "pb")
-    hop(3, "pa")
+    hand_on(3, bs[1], bs[0])
     convolution_grads()
-    from_tensor(("b", 1), Ball, block(1))
-    shared(("b", 1), Ball, block(1))
+    from_tensor(bs[1], Ball, block(1))
+    shared(bs[1], Ball, block(1))
     attention_grads()
-    hop(3, "pb")
 
     @pl.when(second)
     def _():
-        from_tensor(("b", 0), Ball, block(0))
-
-    shared(("b", 0), Ball, block(0))
+        from_tensor(bs[0], Ball, block(0))
+
+    shared(bs[0], Ball, block(0))
     write(Ball.at[:, block(0)], b0_out)
+    for name, ref in (("pa", PA), ("pb", PB)):
+        all_arrived((name, 3), (groups - 1) * size_of(ref.at[0]))
     all_arrived("out", 3 * size_of(out_rows()))
     all_arrived("grad", 3 * size_of(back_rows()))
     for copy in written:
@@ -899,8 +1067,8 @@
 
 
 def last_kernel(*refs):
-    given, outs, held, made, in_sems, out_sems = refs[:16], refs[16:30], refs[30:46], refs[46:57], refs[57], refs[58]
-    lo, ig, pa, pb, n0, b0, act0, slope0, fout, table, in1, out1, qkv, ao, ci, co = held
+    given, outs, held, made, in_sems, out_sems = refs[:17], refs[17:31], refs[31:48], refs[48:59], refs[59], refs[60]
+    lo, ig, pa, pb, n0, b0, act0, slope0, fout, table, in1, out1, qkv, ao, ci, co, cs = held
     LO, IG, ng, nb, w_in, w_out, w_rel, pos, w_dw, bng, bns = made
     copies = []
 
@@ -911,7 +1079,7 @@
 
     given = [m.at[0] if i == 8 else m for i, m in enumerate(given)]
     loads = [pltpu.make_async_copy(given[i], held[i], in_sems.at[i]) for i in range(len(held))]
-    for i in (5, 8, 7, 4, 6, 10, 11, 12, 14, 13, 15, 2, 3, 0, 1, 9):
+    for i in (5, 8, 7, 4, 6, 10, 11, 12, 14, 13, 15, 2, 3, 0, 1, 9, 16):
         loads[i].start()
     for i in (5, 8, 7, 4):
         loads[i].wait()
@@ -927,13 +1095,13 @@
     ):
         loads[i].wait()
         send(held[i], dst)
-    for i in (2, 3, 0, 1, 9):
+    for i in (2, 3, 0, 1, 9, 16):
         loads[i].wait()
     sums, norms = pa[0].astype(f32), pb[0].astype(f32)
     for g in range(1, pa.shape[0]):
         sums += pa[g].astype(f32)
         norms += pb[g].astype(f32)
-    w_rel[...] = dot(table[...], sums[SMALL_ROWS:].astype(bf16), 0, 0)
+    w_rel[...] = dot(table[...], sums[relative_at(pa.shape[0]) :].astype(bf16), 0, 0)
     send(w_rel, outs[6].at[3])
     LO[...] = lo[...].astype(f32)
     IG[...] = ig[...].astype(f32)
@@ -941,9 +1109,12 @@
         ng[i] = norms[i : i + 1]
         nb[i] = norms[8 + i : 9 + i]
     pos[...] = sums[0:2]
+    taps = w_dw.shape[0]
+    if pa.shape[0] > 1:
+        sums = jnp.concatenate([sums[0:2], cs[taps : taps + 2], cs[0:taps]], 0)
     bng[...] = sums[2:3]
     bns[...] = sums[3:4]
-    for k in range(w_dw.shape[0]):
+    for k in range(taps):
         w_dw[k] = sums[4 + k : 5 + k]
     for i, src in ((0, LO), (1, IG), (2, ng), (3, nb), (7, pos), (10, w_dw), (11, bng), (12, bns)):
         send(src, outs[i])
@@ -964,7 +1135,7 @@
     table = position_rows(frames, width)
     vm = pl.BlockSpec(memory_space=pltpu.VMEM)
     hbm = pl.BlockSpec(memory_space=pltpu.HBM)
-    sums_rows = SMALL_ROWS + 2 * frames
+    sums_rows = relative_at(groups) + 2 * frames
 
     def shape(dims, dtype=bf16):
         return jax.ShapeDtypeStruct(dims, dtype)
@@ -973,23 +1144,23 @@
         shape((width, width), f32), shape((width, width), f32), shape((3, width, C), f32), shape((C, width), f32),
         shape((2 * width, C), f32), shape((C, width), f32),
     ]
-    n_recv = 73 + 15 * (groups - 1)
+    n_recv = 75 + 15 * (groups - 1)
     n_send = 3 + 2 * (groups - 1) + 2 * max(groups - 2, 0)
     operands = (
         lengths, inputs, cotangent, norm_gain.transpose(1, 0, 2), norm_bias.transpose(1, 0, 2), ffn_in[0],
         ffn_out[0], attn_in[0], attn_out[0], conv_in.reshape(2 * width, C), conv_out[0], pos_bias[0], bn_gain,
         bn_shift, depthwise.transpose(1, 0, 2), table,
     )
-    lo, ig, pa, pb, n0, b0, act0, slope0, *ready = pl.pallas_call(
+    lo, ig, pa, pb, cs, n0, b0, act0, slope0, *ready = pl.pallas_call(
         lambda *refs: layer_kernel((frames, width, dp, groups), *refs),
         out_shape=[
             shape((group * frames, width)), shape((group * frames, width)),
-            shape((groups, sums_rows, C)), shape((groups, 16, width)),
+            shape((groups, sums_rows, C)), shape((groups, 16, width)), shape((40, C), f32),
             shape((R, width)), shape((R, width)), shape((R, width)), shape((R, width), f32),
         ]
         + made_first,
         in_specs=[hbm] * 16,
-        out_specs=[vm] * 4 + [hbm] * 10,
+        out_specs=[vm] * 5 + [hbm] * 10,
         scratch_shapes=[
             pltpu.VMEM((2, 4, width, width), bf16),
             pltpu.VMEM((2, 4, width, width), bf16),
@@ -1022,8 +1193,8 @@
             pltpu.VMEM((4, 16, width), bf16),
             pltpu.VMEM((dp, 8, width), f32),
             pltpu.VMEM((dp, 8, width), f32),
-            pltpu.VMEM((3, 3, frames, width), bf16),
-            pltpu.VMEM((3, 3, frames, width), bf16),
+            pltpu.VMEM((4, 3, frames, width), bf16),
+            pltpu.VMEM((4, 3, frames, width), bf16),
             pltpu.VMEM((5, 1, width), f32),
             pltpu.VMEM((5, 1, width), f32),
             pltpu.VMEM((2, C), f32),
@@ -1044,6 +1215,13 @@
         ]
         + [pltpu.VMEM(m.shape, m.dtype) for m in made_first]
         + [
+            pltpu.VMEM((2, R, C), f32),
+            pltpu.VMEM((R, C), f32),
+            pltpu.VMEM((R // frames, frames + 32, C), f32),
+            pltpu.VMEM((R, C), f32),
+            pltpu.VMEM((R // frames, frames + 32, C), f32),
+            pltpu.VMEM((taps, 8, C), f32),
+            pltpu.VMEM((4, 8, C), f32),
             pltpu.VMEM((2**23 // 512, 128), f32),
             pltpu.SemaphoreType.DMA((n_send,)),
             pltpu.SemaphoreType.DMA((n_recv,)),
@@ -1061,7 +1239,7 @@
         shape((4, width, C), f32), shape((2, C), f32), shape((C, width), f32), shape((2 * width, C), f32),
         shape((taps, 1, C), f32), shape((1, C), f32), shape((1, C), f32), shape((C, width), f32),
     ]
-    given = (lo, ig, pa, pb, n0, b0, act0, slope0, ffn_out[0], table[2 * frames :], *ready)
+    given = (lo, ig, pa, pb, n0, b0, act0, slope0, ffn_out[0], table[2 * frames :], *ready, cs)
     held = list(given)
     held[8] = shape((width, width))
     made = [m for i, m in enumerate(gradients) if i not in (8, 9, 13)]
@@ -1070,7 +1248,7 @@
     outs = pl.pallas_call(
         last_kernel,
         out_shape=gradients,
-        in_specs=[hbm] * 16,
+        in_specs=[hbm] * len(given),
         out_specs=[hbm] * len(gradients),
         scratch_shapes=[pltpu.VMEM(m.shape, m.dtype) for m in held]
         + [pltpu.VMEM(m.shape, m.dtype) for m in made]

time: 112 us -> 104 us (0.929)
  Pallas kernels: 111 us -> 103 us
    pallas_call x1, Pallas kernels: 105 us -> 97.2 us  [on_device(): pl.pallas_call(lambda *refs: layer_kernel((frames, width, dp, groups), *r...]
where the time goes in v4:
time: 104 us
  Pallas kernels  103 us (99%)
    pallas_call x1, Pallas kernels, on_device(): pl.pallas_call(lambda *refs: layer_kernel((frames, width, dp, groups), *r...  97.2 us
    pallas_call x1, Pallas kernels, on_device(): pl.pallas_call(last_kernel, out_shape=gradients, in_specs=[hbm] * len(giv...  5.78 us

profile of v4, /device:TPU:0, one launch (start us, length us, event | category | flops | bytes accessed | tf_op | source)
XLA Modules:
  0.0 103.8 jit_solution(3769930134051941707)
XLA Ops:
  0.7 97.2 %shard_map.263 = (bf16[128,512]{1,0:T(8,128)(2,1)}, bf16[128,512]{1,0:T(8,128)(2,1)}, bf16[4,80,128]{2,1,0:T(8,128)(2,1)}, bf16[4,16,512]{2,1,0:T(8,128)(2,1)}, ...) custom-call(s32[4]{0:T(128)} %refs_0_.1, ...), custom_call_target="tpu_custom_call" | custom-call | tf_op jit(solution)/shard_map/pallas_call | solution.py:1154
  97.9 5.8 %shard_map.264 = (f32[128,512]{1,0:T(8,128)}, f32[128,512]{1,0:T(8,128)}, f32[5,1,512]{2,1,0:T(1,128)}, f32[5,1,512]{2,1,0:T(1,128)}, f32[2,512,512]{2,1,0:T(8,1...) custom-call(bf16[128,512]{1,0:T(8,128)(2,1)} %get-tuple-element.43.r, ...), custom_call_target="tpu_custom_call" | custom-call | tf_op jit(solution)/shard_map/pallas_call | solution.py:1248

commit v5 on v4

--- a/solution.py
+++ b/solution.py
@@ -37,23 +37,23 @@
     angles = (offset[:, None] * rates[None, :]).astype(np.float32)
     table = np.stack([np.sin(angles), np.cos(angles)], -1).reshape(2 * frames - 1, width)
     blank = np.zeros((1, width), np.float32)
-    return jnp.asarray(np.concatenate([table[::-1], blank, table, blank]), bf16)
+    return [jnp.asarray(np.concatenate([rows, blank]), bf16) for rows in (table[::-1], table)]
 
 
 def layer_kernel(dims, *refs):
     T, width, dp, groups = dims
     C = width // 4
     (lengths, inputs, cot, ng_in, nb_in, fin, fout, ain, aout, cin, cout, pos_in, bng_in, bns_in, dw_in, e2_in) = refs[:16]
-    (LO, IG, PA, PB, CS, n0_out, b0_out, act0_out, slope0_out) = refs[16:25]
-    (in1_out, out1_out, qkv_out, ao_out, ci_out, co_out) = refs[25:31]
-    refs = refs[31:]
+    (lo_out, ig_out, pa_out, pb_out, cs_out) = refs[16:21]
+    (in_out, out_out, qkv_out, ao_out, ci_out, co_out) = refs[21:27]
+    refs = refs[27:]
     (Win, Wout, Wqkv, Wr, Wo, Wci, Wco, R2, SM) = refs[:9]
     (H, XH, RS, X, G, ARR, HOP, QKV, PRB, GVG, CT, UP, DP) = refs[9:22]
     (SfSt, SbSt, PAst, PAb, PAin, PBst, PBin, STF, STB, RSst, RSin) = refs[22:33]
     (ng, nb, pos, bng, bns, dw, e2, lens, pairs, spread) = refs[33:43]
-    (Nall, Ball, Sf, Sb, ACT, SLOPE, HG, gin1, gout1, gqkv, gao, gci, gco) = refs[43:56]
+    (Nall, Ball, Sf, Sb, ACT, SLOPE, HG, gin, gout, gqkv, gao, gci, gco) = refs[43:56]
     GA, HATA, UA, DYA, DA, DWACC, INVA = refs[56:63]
-    dummy, ss, rs, ls, os = refs[63:68]
+    LO, IG, PA, PB, CS, dummy, ss, rs, ls, os = refs[63:73]
     gathered = groups > 1
 
     s, t, d = lax.axis_index(SECTION), lax.axis_index(TENSOR), lax.axis_index(DATA)
@@ -77,7 +77,7 @@
         (j, to): there[j] & there[to] for j in reach for to in (1, -1) if j * to < 0 and groups > 1
     }
     base = base_of[0]
-    trow = pl.multiple_of(t * T, T)
+    trow, yrow = pl.multiple_of(t * T, T), pl.multiple_of((t ^ 2) * T, T)
     mine = d if groups > 1 else 0
 
     recv_index, send_index, sent = {}, {}, {}
@@ -189,6 +189,10 @@
         + column_chunks(lambda i, rows: Wci.at[i, rows, cols(0)], Wci, 2)
         + row_chunk(cout, Wco)
         + feed_chunks(1)
+        + [
+            (lambda w: SM.at[:, cols(0)], lambda k, w: SM.at[:, cols(k)]),
+            (lambda w: R2.at[pl.ds(0, 2 * T), cols(0)], lambda k, w: R2.at[pl.ds(0, 2 * T), cols(k)]),
+        ]
     )
     for n, at in ((width // 2, 0), (width // 2, width // 2), (width, 0)) + tuple((C, C * k) for k in range(4)):
         for w in ("own", "other"):
@@ -211,6 +215,8 @@
         start(("sib", i), lambda: dst(2, w), lambda: dst(3, w), sib, only.get(i), 1)
 
     def step_b(i):
+        if i not in over_y:
+            return
         dst = chunks[i][1]
         arrived(("z", i), dst(2, "other"))
         start(("sib", i), lambda: dst(2, "other"), lambda: dst(3, "other"), sib, only.get(i), 2)
@@ -243,6 +249,9 @@
             g - jnp.mean(g, -1, keepdims=True) - hat * jnp.mean(g * hat, -1, keepdims=True)
         )
 
+    def total_of(v):
+        return jnp.sum(v, 0, keepdims=True)
+
     def silu(h):
         return h * jax.nn.sigmoid(h)
 
@@ -254,18 +263,29 @@
     def block(i, n=1):
         return pl.ds(i * width, n * width)
 
-    def to_tensor(name, ref, c):
+    def to_tensor(name, ref, c, cond=None):
         for k in (1, 2, 3):
-            start(name, lambda: ref.at[own, c], lambda k=k: ref.at[place(k), c], peers[k], None, k)
+            start(name, lambda: ref.at[own, c], lambda k=k: ref.at[place(k), c], peers[k], cond, k)
 
     def from_tensor(name, ref, c):
         all_arrived(name, 3 * size_of(ref.at[own, c]))
+
+    def to_pair(name, ref, c, cond=None):
+        start(name, lambda: ref.at[own, c], lambda: ref.at[place(1), c], sib, cond, 4)
+        start((name, 4), lambda: ref.at[own, c], lambda: ref.at[place(2), c], yp, cond)
+
+    def relay(name, ref, c, cond=None):
+        arrived((name, 4), ref.at[place(2), c])
+        start(name, lambda: ref.at[place(2), c], lambda: ref.at[place(3), c], sib, cond, 5)
+
+    def from_pair(name, ref, c):
+        all_arrived(name, 2 * size_of(ref.at[own, c]))
 
     def feed(j, i, before, after):
         x = X[before]
         a = norm(i, x).astype(bf16)
         Nall[own, i * width : (i + 1) * width] = a
-        to_tensor(("n", i), Nall, block(i))
+        to_pair(("n", i), Nall, block(i), second)
         active = []
         for k in range(4):
             h = dot(a, Win[j, k])
@@ -300,7 +320,7 @@
     def _():
         pltpu.make_async_copy(inputs.at[t], X.at[0], ls.at[20]).wait()
         Nall[own, 0:width] = norm(0, X[0]).astype(bf16)
-        to_tensor(("n", 0), Nall, block(0))
+        to_tensor(("n", 0), Nall, block(0), first)
 
     @pl.when(second)
     def _():
@@ -317,21 +337,14 @@
     SM[3:4, 0:C] = bns[...]
     for k in range(taps):
         SM[4 + k : 5 + k, 0:C] = dw[k]
-    R2[:, 0:C] = dot(e2[...], Wr[...]).astype(bf16)
+    R2[0 : 2 * T, 0:C] = dot(e2[...], Wr[...]).astype(bf16)
     fetched("in0", "out0")
 
     @pl.when(first)
     def _():
         send_chunks((8,))
         X[1] = shared_feed(0, 0)
-        send_chunks((9, 10))
-
-    for k in (1, 2, 3):
-        start("small", lambda: SM.at[:, cols(0)], lambda k=k: SM.at[:, cols(k)], peers[k], None, k)
-
-    def send_relative():
-        for k in (1, 2, 3):
-            start("rel", lambda: R2.at[:, cols(0)], lambda k=k: R2.at[:, cols(k)], peers[k], None, k)
+        send_chunks((9,))
 
     @pl.when(first)
     def _():
@@ -340,8 +353,7 @@
 
     @pl.when(second)
     def _():
-        send_relative()
-        send_chunks(range(4, 15))
+        send_chunks((15, 16, *range(4, 15)))
 
     fetched("qkv", "o", "co", "in1", "out1")
     margin = 16
@@ -372,7 +384,7 @@
 
     def attend(qu, qv, key, value, relative, keys):
         content = dot(pair_rows(qu).astype(bf16), key, 1, 1)
-        whole = dot(pair_rows(qv).astype(bf16), relative, 1, 1)
+        whole = dot(pair_rows(qv).astype(bf16), jnp.concatenate([relative, jnp.zeros_like(relative)], 0), 1, 1)
         placed = jnp.concatenate(
             [
                 pltpu.roll(whole[e * T : (e + 1) * T], 4 * T - (T - 1), 1, stride=1, stride_axis=0)[:, :T]
@@ -396,7 +408,7 @@
         for p in range(4):
             c = pl.ds(2 * HEAD * p, 2 * HEAD)
             probs, out = attend(
-                QKV[0, :, c], QKV[1, :, c], QKV[2, :, c].astype(bf16), QKV[3, :, c].astype(bf16), R2[:, c], keys
+                QKV[0, :, c], QKV[1, :, c], QKV[2, :, c].astype(bf16), QKV[3, :, c].astype(bf16), R2[0 : 2 * T, c], keys
             )
             PRB[p] = probs
             mixed.append(out)
@@ -410,51 +422,53 @@
         for p in range(4):
             rows = slice(T * p, T * (p + 1))
             keys = keys_of(lens[t ^ PLACE[p]])
-            mixed.append(attend(qu[rows], qv[rows], key[rows], value[rows], R2[:, 0:C], keys)[1])
+            mixed.append(attend(qu[rows], qv[rows], key[rows], value[rows], R2[0 : 2 * T, 0:C], keys)[1])
         mixed = jnp.concatenate(mixed, 0)
         Sf[four, 0:C] = mixed
         return sum_to_owner(("s", 3), 3, dot(mixed, Wo[0:C]))
 
-    def small_arrived():
-        all_arrived("small", 3 * size_of(SM.at[:, cols(0)]))
-
     def relative_arrived():
-        all_arrived("rel", 3 * size_of(R2.at[:, cols(0)]))
+        step_c(16)
+        turned_back = (
+            lax.broadcasted_iota(jnp.int32, (2 * T, 2 * T), 0) + lax.broadcasted_iota(jnp.int32, (2 * T, 2 * T), 1)
+            == 2 * T - 2
+        ).astype(f32).astype(bf16)
+        R2[2 * T : 4 * T] = dot(turned_back, R2[0 : 2 * T]).astype(bf16)
 
 
     @pl.when(first)
     def _():
         Nall[own, width : 2 * width] = norm(1, X[1]).astype(bf16)
-        to_tensor(("n", 1), Nall, block(1))
-        send_chunks((4, 5))
+        to_tensor(("n", 1), Nall, block(1), first)
+        send_chunks((10, 15))
         step_a(9)
-        step_a(10)
         step_b(8)
-        step_b(9)
         from_tensor(("n", 1), Nall, block(1))
         total = shared_attention()
-        send_chunks((6,))
-        send_relative()
-        send_chunks((7,))
+        send_chunks((4, 5, 6, 16, 7))
+        step_a(10)
+        step_a(15)
+        step_b(9)
+        X[2] = X[1] + summed_here(("s", 3), 3, total)
         step_b(10)
-        X[2] = X[1] + summed_here(("s", 3), 3, total)
-        small_arrived()
+        step_c(15)
 
     @pl.when(second)
     def _():
-        for i in range(13):
+        coming = (*range(4), 15, 16, *range(4, 13))
+        for n, i in enumerate(coming):
             step_a(i)
-            if i > 1:
-                step_b(i - 2)
+            if n > 1:
+                step_b(coming[n - 2])
         for i in range(7):
             step_c(i)
-        small_arrived()
+        step_c(15)
         relative_arrived()
         arrived("hop", ARR)
         X[0] = ARR[...].astype(f32)
         feed(0, 0, 0, 1)
         Nall[own, width : 2 * width] = norm(1, X[1]).astype(bf16)
-        to_tensor(("n", 1), Nall, block(1))
+        to_pair(("n", 1), Nall, block(1), second)
         step_b(11)
         mixed = attention_here()
         step_a(13)
@@ -464,99 +478,6 @@
         step_c(7)
         X[2] = X[1] + dot(jnp.concatenate(mixed, 1), Wo[...])
 
-    def send_rows_second(i):
-        @pl.when(second)
-        def _():
-            to_tensor(("n", i), Nall, block(i))
-
-    a = norm(2, X[2]).astype(bf16)
-    Nall[own, 2 * width : 3 * width] = a
-    send_rows_second(2)
-
-    @pl.when(first)
-    def _():
-        send_chunks((11,))
-
-    step_c(8)
-    step_c(9)
-    GVG[0] = dot(a, Wci[0])
-    GVG[1] = dot(a, Wci[1])
-    UP[margin : margin + T] = GVG[0] * jax.nn.sigmoid(GVG[1]) * row_mask
-    for p in range(4):
-        c = pl.ds(C * p, C)
-        acc = SM[4:5, c] * UP[margin - taps // 2 : margin - taps // 2 + T, c]
-        for k in range(1, taps):
-            o = margin - taps // 2 + k
-            acc += SM[4 + k : 5 + k, c] * UP[o : o + T, c]
-        CT[:, c] = acc
-    conv = CT[...]
-
-    def dp_sums(name, ref, rows):
-        n = len(rows)
-        ref[d] = jnp.concatenate(rows + [jnp.zeros((8 - n, width), f32)], 0)
-        for r in range(1, dp):
-            start(name, lambda: ref.at[d], lambda: ref.at[d], zpeers[r], None, r)
-
-    def summed(name, ref):
-        all_arrived(name, (dp - 1) * size_of(ref.at[0]))
-        total = ref[0]
-        for r in range(1, dp):
-            total += ref[r]
-        return total
-
-    def total_of(v):
-        return jnp.sum(v, 0, keepdims=True)
-
-    masked = conv * row_mask
-    frames_row = jnp.broadcast_to(total_of(row_mask), (1, width))
-    lengths_row = jnp.concatenate(
-        [jnp.broadcast_to(lens[t ^ PLACE[p]].astype(f32), (1, C)) for p in range(4)], 1
-    )
-    dp_sums("bnf", STF, [total_of(masked), total_of(masked * conv), frames_row, lengths_row])
-    steps(second, (A, 14))
-    step_c(10)
-    sums = summed("bnf", STF)
-    steps(first, (A, 4), (A, 5), (A, 6))
-    steps(second, (B, 13))
-    count = sums[2:3]
-    bn_mean = sums[0:1] / count
-    inv_std = lax.rsqrt(sums[1:2] / count - bn_mean * bn_mean + EPSILON)
-    hat = (conv - bn_mean) * inv_std
-    CT[...] = hat
-    active = silu(hat * SM[2:3] + SM[3:4]).astype(bf16)
-    if not gathered:
-        for k in range(4):
-            SfSt[k, :, C : 2 * C] = active[:, C * k : C * (k + 1)]
-    X[3] = X[2] + dot(active, Wco[...])
-
-    @pl.when(first)
-    def _():
-        Nall[own, 3 * width : 4 * width] = norm(3, X[3]).astype(bf16)
-        to_tensor(("n", 3), Nall, block(3))
-        total = shared_feed(1, 3)
-        send_chunks((12, 13, 14))
-        step_a(7)
-        step_a(11)
-        step_b(4)
-        X[4] = X[3] + 0.5 * summed_here(("s", 1), 1, total)
-
-    @pl.when(second)
-    def _():
-        for i in range(11, 15):
-            step_c(i)
-        feed(1, 3, 3, 4)
-    out = (norm(4, X[4]) * row_mask).astype(bf16)
-    HOP[...] = out
-
-    @pl.when(first)
-    def _():
-        start("hop", lambda: HOP, lambda: ARR, partner, first)
-
-    LO[pl.ds(trow, T)] = out
-    out_rows = lambda: LO.at[pl.ds(trow, T)]
-    for k in (1, 2, 3):
-        start("out", out_rows, out_rows, peers[k], None, k)
-
     def line_start(name, region):
         for way, to, back in (("up", 1, -1), ("down", -1, 1)):
             if groups > 1:
@@ -611,11 +532,36 @@
     def shared(name, ref, c):
         all_arrived((name, 2, 0), 2 * (groups - 1) * size_of(ref.at[own, c]))
 
-    every = block(0, 4)
+    def set_off_to_all(name):
+        ref, c = whole_rows(name)
+        mine = lambda: ref.at[own, c]
+        for r in range(1, groups):
+            start((name, 0, (-r) % dp), mine, mine, zpeers[r], None, r)
+
+    def from_all(name):
+        ref, c = whole_rows(name)
+        for r in range(1, groups):
+            rows = lambda r=r: ref.at[pl.ds(base_of[r], T), c]
+            arrived((name, 0, r), rows())
+            start((name, 1, r), rows, lambda r=r: ref.at[pl.ds(second_of[r], T), c], yp, None, r)
+            start((name, 2, 0), rows, lambda r=r: ref.at[pl.ds(high_of[r], T), c], sib, None, r)
+
+    def hand_on_all(name):
+        ref, c = whole_rows(name)
+        for r in range(1, groups):
+            rows = lambda r=r: ref.at[pl.ds(second_of[r], T), c]
+            arrived((name, 1, r), rows())
+            start((name, 2, 0), rows, lambda r=r: ref.at[pl.ds(last_of[r], T), c], sib, None, dp + r)
+
+    def all_shared(*names):
+        for name in names:
+            shared(name, *whole_rows(name))
+
     sf_cols = pl.ds(0, C if gathered else 2 * C)
     qkv_cols, gate_cols = pl.ds(0, 3 * C), pl.ds(3 * C, 2 * C)
     lines_of = {
-        "n": (rows_region(Nall, T, every), share(Nall, every)),
+        "n": (rows_region(Nall, T, block(0, 3)), share(Nall, block(0, 3))),
+        "m": (rows_region(Nall, T, block(3)), share(Nall, block(3))),
         "sf": (rows_region(Sf, R4, sf_cols), None),
         "qkv": (rows_region(Sb, R4, qkv_cols), None),
     }
@@ -630,25 +576,20 @@
         for name in names:
             line_hop(name, lines_of[name][0], n, lines_of[name][1])
 
+    def whole_rows(name):
+        if name in ("n", "m"):
+            return Nall, block(0, 3) if name == "n" else block(3)
+        return Ball, block(name[1])
+
     def hand_on(n, *names):
         for name in names:
-            ref, c = (Nall, every) if name == "n" else (Ball, block(name[1]))
-            share_on(name, ref, c, n)
-
-    for cond, c in ((first, pl.ds(C, C)), (second, sf_cols))[gathered:]:
-
-        @pl.when(cond)
-        def _():
-            Sf[own, c] = SfSt[0, :, c]
-            for k in (1, 2, 3):
-                start("sf", lambda k=k: SfSt.at[k, :, c], lambda k=k: Sf.at[place(k), c], peers[k], cond, k)
+            share_on(name, *whole_rows(name), n)
 
     written = []
 
     def write(src, dst):
-        copy = pltpu.make_async_copy(src, dst, os.at[len(written)])
-        copy.start()
-        written.append(copy)
+        pltpu.make_async_copy(src, dst, os.at[0]).start()
+        written.append(size_of(src))
 
     R = Nall.shape[0]
     row_blocks = [slice(r, r + R4) for r in range(0, R, R4)]
@@ -663,14 +604,14 @@
             ACT[j, rows] = (h * sig).astype(bf16)
             SLOPE[j, rows] = slope(h, sig)
 
-    def second_feed_grads():
-        c = slice(3 * width, 4 * width)
+    def feed_grads(j, i):
+        c = slice(i * width, (i + 1) * width)
         for rows in row_blocks:
-            HG[rows] = (dot(Ball[rows, c], Wout[1, 0], 1, 1) * SLOPE[1, rows]).astype(bf16)
-        gin1[...] = dot(Nall[:, c], HG[...], 0, 0)
-        write(gin1, in1_out)
-        gout1[...] = dot(ACT[1], Ball[:, c], 0, 0)
-        write(gout1, out1_out)
+            HG[rows] = (dot(Ball[rows, c], Wout[j, 0], 1, 1) * SLOPE[j, rows]).astype(bf16)
+        gin[j] = dot(Nall[:, c], HG[...], 0, 0).astype(bf16)
+        write(gin.at[j], in_out.at[j])
+        gout[j] = dot(ACT[j], Ball[:, c], 0, 0).astype(bf16)
+        write(gout.at[j], out_out.at[j])
 
     def mask_of(g, p):
         return (lax.broadcasted_iota(jnp.int32, (T, C), 0).astype(f32) < STF[g, 3:4, C * p : C * (p + 1)]).astype(f32)
@@ -753,26 +694,132 @@
                 Sb[rows, 4 * C : 5 * C] = (dua * GA[0, rows] * (sig * (1.0 - sig))).astype(bf16)
 
     def convolution_grads():
-        gates = dot(Nall[:, 2 * width : 3 * width], Sb[:, 3 * C : 5 * C], 0, 0)
-        for i in range(2):
-            gci[pl.ds(i, width, stride=2), :] = gates[:, C * i : C * (i + 1)]
+        gci[...] = dot(Nall[:, 2 * width : 3 * width], Sb[:, 3 * C : 5 * C], 0, 0).astype(bf16)
         write(gci, ci_out)
-        gco[...] = dot(Sf[:, C : 2 * C], Ball[:, 2 * width : 3 * width], 0, 0)
+        gco[...] = dot(Sf[:, C : 2 * C], Ball[:, 2 * width : 3 * width], 0, 0).astype(bf16)
         write(gco, co_out)
 
     def attention_grads():
         grads = dot(Nall[:, width : 2 * width], Sb[:, 0 : 3 * C], 0, 0)
         for i in range(3):
-            gqkv[i] = grads[:, C * i : C * (i + 1)]
+            gqkv[i] = grads[:, C * i : C * (i + 1)].astype(bf16)
         write(gqkv, qkv_out)
-        gao[...] = dot(Sf[:, 0:C], Ball[:, width : 2 * width], 0, 0)
+        gao[...] = dot(Sf[:, 0:C], Ball[:, width : 2 * width], 0, 0).astype(bf16)
         write(gao, ao_out)
 
-    @pl.when(first)
-    def _():
-        set_off("n", "sf")
-        to_tensor(("n", 2), Nall, block(2))
-        for i in (5, 6, 7):
+    def forward_values():
+        hidden_rows(1, 3)
+        hidden_rows(0, 0)
+        if gathered:
+            convolution_rows()
+
+    a = norm(2, X[2]).astype(bf16)
+    Nall[own, 2 * width : 3 * width] = a
+    to_pair(("n", 2), Nall, block(2))
+
+    step_c(8)
+    step_c(9)
+    GVG[0] = dot(a, Wci[0])
+    GVG[1] = dot(a, Wci[1])
+    UP[margin : margin + T] = GVG[0] * jax.nn.sigmoid(GVG[1]) * row_mask
+    for p in range(4):
+        c = pl.ds(C * p, C)
+        acc = SM[4:5, c] * UP[margin - taps // 2 : margin - taps // 2 + T, c]
+        for k in range(1, taps):
+            o = margin - taps // 2 + k
+            acc += SM[4 + k : 5 + k, c] * UP[o : o + T, c]
+        CT[:, c] = acc
+    conv = CT[...]
+
+    def dp_sums(name, ref, rows):
+        n = len(rows)
+        ref[d] = jnp.concatenate(rows + [jnp.zeros((8 - n, width), f32)], 0)
+        for r in range(1, dp):
+            start(name, lambda: ref.at[d], lambda: ref.at[d], zpeers[r], None, r)
+
+    def summed(name, ref):
+        all_arrived(name, (dp - 1) * size_of(ref.at[0]))
+        total = ref[0]
+        for r in range(1, dp):
+            total += ref[r]
+        return total
+
+    masked = conv * row_mask
+    frames_row = jnp.broadcast_to(total_of(row_mask), (1, width))
+    lengths_row = jnp.concatenate(
+        [jnp.broadcast_to(lens[t ^ PLACE[p]].astype(f32), (1, C)) for p in range(4)], 1
+    )
+    dp_sums("bnf", STF, [total_of(masked), total_of(masked * conv), frames_row, lengths_row])
+    steps(second, (A, 14), (B, 13))
+    step_c(10)
+    sums = summed("bnf", STF)
+    steps(first, (A, 4), (A, 5), (A, 6), (A, 16))
+
+    @pl.when(second)
+    def _():
+        set_off("n")
+    count = sums[2:3]
+    bn_mean = sums[0:1] / count
+    inv_std = lax.rsqrt(sums[1:2] / count - bn_mean * bn_mean + EPSILON)
+    hat = (conv - bn_mean) * inv_std
+    CT[...] = hat
+    active = silu(hat * SM[2:3] + SM[3:4]).astype(bf16)
+    if not gathered:
+        for k in range(4):
+            SfSt[k, :, C : 2 * C] = active[:, C * k : C * (k + 1)]
+    X[3] = X[2] + dot(active, Wco[...])
+
+    @pl.when(first)
+    def _():
+        Nall[own, 3 * width : 4 * width] = norm(3, X[3]).astype(bf16)
+        to_tensor(("n", 3), Nall, block(3), first)
+        send_chunks((11,))
+        total = shared_feed(1, 3)
+        send_chunks((12, 13, 14))
+        step_a(7)
+        step_b(4)
+        step_b(5)
+        X[4] = X[3] + 0.5 * summed_here(("s", 1), 1, total)
+
+    @pl.when(second)
+    def _():
+        for i in range(11, 15):
+            step_c(i)
+        feed(1, 3, 3, 4)
+    out = (norm(4, X[4]) * row_mask).astype(bf16)
+    HOP[...] = out
+
+    @pl.when(first)
+    def _():
+        start("hop", lambda: HOP, lambda: ARR, partner, first)
+
+    LO[pl.ds(trow, T)] = out
+    def output_to_pair(name, ref):
+        rows = lambda: ref.at[pl.ds(trow, T)]
+        start(name, rows, rows, sib)
+        start((name, 4), rows, rows, yp)
+
+    def relay_output(name, ref):
+        rows = lambda: ref.at[pl.ds(yrow, T)]
+        arrived((name, 4), rows())
+        start(name, rows, rows, sib, None, 1)
+
+    output_to_pair("out", LO)
+
+    for cond, c in ((first, pl.ds(C, C)), (second, sf_cols))[gathered:]:
+
+        @pl.when(cond)
+        def _():
+            Sf[own, c] = SfSt[0, :, c]
+            for k in (1, 2, 3):
+                start("sf", lambda k=k: SfSt.at[k, :, c], lambda k=k: Sf.at[place(k), c], peers[k], cond, k)
+
+    @pl.when(first)
+    def _():
+        set_off("n", "m", "sf")
+        relay(("n", 2), Nall, block(2))
+        step_a(11)
+        for i in (6, 7):
             step_b(i)
         step_a(12)
         step_b(11)
@@ -785,16 +832,16 @@
         if not gathered:
             from_tensor("sf", Sf, pl.ds(C, C))
         step_a(14)
-        hop(1, "n", "sf")
+        hop(1, "n", "m", "sf")
         step_b(13)
         for i in range(11, 15):
             step_c(i)
         for k in range(4):
             H[1, k] = dot(Nall[own, 3 * width : 4 * width], Win[1, k])
-        hop(2, "n", "sf")
-        hand_on(1, "n")
-        hop(3, "n", "sf")
-        hand_on(2, "n")
+        hop(2, "n", "m", "sf")
+        hand_on(1, "n", "m")
+        hop(3, "n", "m", "sf")
+        hand_on(2, "n", "m")
 
     @pl.when(first)
     def _():
@@ -806,9 +853,11 @@
     def feed_back(j, i, g):
         b = (0.5 * g).astype(bf16)
         Ball[own, i * width : (i + 1) * width] = b
-        to_tensor(("b", i), Ball, block(i))
         if j:
+            to_pair(("b", i), Ball, block(i))
             set_off(("b", i))
+        else:
+            to_tensor(("b", i), Ball, block(i))
         grad = None
         for k in range(4):
             h = H[j, k]
@@ -821,7 +870,7 @@
     g = feed_back(1, 3, g)
     b = g.astype(bf16)
     Ball[own, 2 * width : 3 * width] = b
-    to_tensor(("b", 2), Ball, block(2))
+    to_pair(("b", 2), Ball, block(2))
     hat = CT[...]
     y = hat * SM[2:3] + SM[3:4]
     sig = jax.nn.sigmoid(y)
@@ -832,20 +881,30 @@
     dhat = dy * SM[2:3]
     masked = dhat * row_mask
     dp_sums("bnb", STB, [total_of(masked), total_of(masked * hat)])
+
+    @pl.when(first)
+    def _():
+        hand_on(3, "n", "m")
+        from_pair(("n", 2), Nall, block(2))
+        all_shared("n", "m")
+        forward_values()
+        hop(1, ("b", 3))
+
+    relay(("b", 3), Ball, block(3))
     sums = summed("bnb", STB)
 
     @pl.when(second)
     def _():
-        set_off("n")
+        for i in range(4):
+            relay(("n", i), Nall, block(i), None if i == 2 else second)
+        hop(1, "n")
+        set_off("m")
         from_tensor("sf", Sf, sf_cols)
         set_off("sf")
 
-    @pl.when(first)
-    def _():
-        hop(1, ("b", 3))
-        hand_on(3, "n")
-
-    set_off(("b", 2))
+    relay_output("out", LO)
+    relay(("b", 2), Ball, block(2))
+    set_off_to_all(("b", 2))
     dc = inv_std * (dhat - (sums[0:1] + hat * sums[1:2]) / count) * row_mask
     DP[margin : margin + T] = dc
     for p in range(4):
@@ -864,24 +923,25 @@
     sig = jax.nn.sigmoid(GVG[1])
     dvalue = (du * sig).astype(bf16)
     dgate = (du * GVG[0] * (sig * (1.0 - sig))).astype(bf16)
-    def sb_to_tensor(name, c):
-        for k in (1, 2, 3):
-            start(name, lambda k=k: SbSt.at[k, :, c], lambda k=k: Sb.at[place(k), c], peers[k], None, k)
+    def sb_to_tensor(name, c, k):
+        start(name, lambda: SbSt.at[k, :, c], lambda: Sb.at[place(k), c], peers[k], None, k)
 
     if not gathered:
         for k in range(4):
             SbSt[k, :, 3 * C : 4 * C] = dvalue[:, C * k : C * (k + 1)]
             SbSt[k, :, 4 * C : 5 * C] = dgate[:, C * k : C * (k + 1)]
         Sb[own, 3 * C : 5 * C] = SbSt[0, :, 3 * C : 5 * C]
-        sb_to_tensor("gates", gate_cols)
+        for k in (1, 2, 3):
+            sb_to_tensor("gates", gate_cols, k)
     g = g + norm_back(2, dot(dvalue, Wci[0], 1, 1) + dot(dgate, Wci[1], 1, 1))
     b = g.astype(bf16)
     Ball[own, width : 2 * width] = b
-    to_tensor(("b", 1), Ball, block(1))
+    to_pair(("b", 1), Ball, block(1))
+    set_off(("b", 1))
     dmix = dot(b, Wo[...], 1, 1).astype(bf16).astype(f32)
     scale = HEAD ** (-0.5)
-    dq, dk, dv = [], [], []
-    for p in range(4):
+    dq, dk, dv = [None] * 4, [None] * 4, [None] * 4
+    for p in (2, 3, 1, 0):
         c = pl.ds(2 * HEAD * p, 2 * HEAD)
         qu = pair_rows(QKV[0, :, c]).astype(bf16)
         qv = pair_rows(QKV[1, :, c]).astype(bf16)
@@ -901,26 +961,24 @@
             0,
         ).astype(bf16)
         dv_rows = unpair(dot(whole, R2[2 * T : 4 * T, c])) * scale
-        dk.append((dot(ds, qu, 0, 0) * scale).astype(bf16))
-        dv.append(dot(probs.astype(bf16), do, 0, 0).astype(bf16))
-        dq.append((du_rows + dv_rows).astype(bf16))
+        dk[p] = (dot(ds, qu, 0, 0) * scale).astype(bf16)
+        dv[p] = dot(probs.astype(bf16), do, 0, 0).astype(bf16)
+        dq[p] = (du_rows + dv_rows).astype(bf16)
+        SbSt[p, :, 0:C] = dq[p]
+        SbSt[p, :, C : 2 * C] = dk[p]
+        SbSt[p, :, 2 * C : 3 * C] = dv[p]
+        if p:
+            sb_to_tensor("qkv", qkv_cols, p)
         PAst[0:1, c] = total_of(du_rows)
         PAst[1:2, c] = total_of(dv_rows)
         PAst[relative_at(groups) : relative_at(groups) + 2 * T, c] = dot(whole, qv, 0, 0) * scale
-    for k in range(4):
-        SbSt[k, :, 0:C] = dq[k]
-        SbSt[k, :, C : 2 * C] = dk[k]
-        SbSt[k, :, 2 * C : 3 * C] = dv[k]
     Sb[own, 0 : 3 * C] = SbSt[0, :, 0 : 3 * C]
-    sb_to_tensor("qkv", qkv_cols)
-    set_off(("b", 1))
-
     @pl.when(first)
     def _():
         if not gathered:
             from_tensor("gates", Sb, gate_cols)
         hop(2, ("b", 3))
-        hop(1, ("b", 2))
+        relay(("b", 1), Ball, block(1))
     grad = dot(jnp.concatenate(dq, 1), Wqkv[0], 1, 1)
     grad += dot(jnp.concatenate(dk, 1), Wqkv[1], 1, 1)
     grad += dot(jnp.concatenate(dv, 1), Wqkv[2], 1, 1)
@@ -937,22 +995,24 @@
         to_tensor(("b", 0), Ball, block(0))
         G[...] = g
 
-    set_off(("b", 0))
-    PAb[...] = PAst[...].astype(bf16)
-    for k in (1, 2, 3):
-        start("pa", lambda k=k: PAb.at[:, cols(k)], lambda k=k: PAin.at[k], peers[k], None, k)
-
+    set_off_to_all(("b", 0))
+    from_all(("b", 2))
     def sums_over_tensor(name, parts, ref):
         all_arrived(name, 3 * size_of(parts.at[0]))
         ref[mine] = sum(parts[k].astype(f32) for k in range(4)).astype(bf16)
         for r in range(1, groups):
             start((name, 3), lambda: ref.at[mine], lambda: ref.at[mine], zpeers[r], None, r)
 
+    def send_sums():
+        PAb[...] = PAst[...].astype(bf16)
+        for k in (1, 2, 3):
+            start("pa", lambda k=k: PAb.at[:, cols(k)], lambda k=k: PAin.at[k], peers[k], None, k)
+
     def send_ends():
+        output_to_pair("grad", IG)
         PBin[t] = PBst[...].astype(bf16)
         for k in (1, 2, 3):
             start("pb", lambda: PBin.at[t], lambda: PBin.at[t], peers[k], None, k)
-            start("grad", back_rows, back_rows, peers[k], None, k)
 
     bs = [("b", i) for i in range(4)]
     if not gathered:
@@ -961,101 +1021,102 @@
         def _():
             from_tensor("gates", Sb, gate_cols)
 
-    @pl.when(first)
-    def _():
-        from_tensor(("n", 2), Nall, block(2))
-        shared("n", Nall, every)
-
     @pl.when(second)
     def _():
         send_ends()
+        send_sums()
+        hop(2, "n")
+        hop(1, "m", "sf", bs[3])
+        relay(bs[1], Ball, block(1))
         from_tensor("qkv", Sb, qkv_cols)
         set_off("qkv")
-        hop(1, "n", "sf", bs[3], bs[2], bs[1], bs[0], "qkv")
-        hop(2, "n", "sf")
+        hop(1, bs[1])
         hand_on(1, "n")
-        hop(2, bs[3], bs[2], bs[1], bs[0], "qkv")
-        hand_on(1, bs[3], bs[2])
-        hop(3, "n", "sf")
+        from_all(bs[0])
+        hand_on_all(bs[2])
+        hop(3, "n")
+        hop(2, "m", "sf", bs[3], bs[1])
         hand_on(2, "n")
-        hand_on(1, bs[1], bs[0])
-        hop(3, bs[3], bs[2])
+        hop(1, "qkv")
+        hand_on(1, "m", bs[3], bs[1])
+        hop(3, "m", "sf", bs[3])
         hand_on(3, "n")
-        hand_on(2, bs[3], bs[2], bs[1], bs[0])
-        hop(3, bs[1], bs[0])
+        hand_on_all(bs[0])
+        hop(3, bs[1])
+        hand_on(2, "m", bs[3], bs[1])
+        hop(2, "qkv")
+        hand_on(3, "m")
         for i in range(4):
-            from_tensor(("n", i), Nall, block(i))
-        shared("n", Nall, every)
-    hidden_rows(1, 3)
+            from_pair(("n", i), Nall, block(i))
+        all_shared("n", "m")
+        forward_values()
 
     @pl.when(first)
     def _():
         from_tensor("qkv", Sb, qkv_cols)
         set_off("qkv")
-        hop(2, bs[2])
         hop(3, bs[3])
         hop(1, bs[1])
+        hand_on(1, bs[3])
+        hand_on(2, bs[3])
         from_tensor(bs[0], Ball, block(0))
         h = dot(Nall[four, 0:width], Win[0, 0])
         sig = jax.nn.sigmoid(h)
         hg = dot(Ball[four, 0:width], Wout[0, 0], 1, 1) * slope(h, sig)
         X[0] = sum_to_owner(("s", 2), 2, dot(hg.astype(bf16), Win[0, 0], 1, 1))
-        hop(1, bs[0])
-        hand_on(1, bs[3], bs[2])
-    hidden_rows(0, 0)
-    write(Nall.at[:, block(0)], n0_out)
-    write(ACT.at[0], act0_out)
-    write(SLOPE.at[0], slope0_out)
-    if gathered:
-        convolution_rows()
-
-    @pl.when(first)
-    def _():
+        send_sums()
+        hand_on_all(bs[2])
+        from_all(bs[0])
         hop(1, "qkv")
-        hop(3, bs[2])
         hop(2, bs[1])
+    hand_on(3, bs[3])
+    from_pair(bs[3], Ball, block(3))
+    shared(bs[3], *whole_rows(bs[3]))
+    feed_grads(1, 3)
+
+    @pl.when(first)
+    def _():
         g = G[...] + norm_back(0, summed_here(("s", 2), 2, X[0]))
         IG[pl.ds(trow, T)] = g.astype(bf16)
         send_ends()
-        hop(2, bs[0])
-        hand_on(1, bs[1], bs[0])
-        hand_on(2, bs[3], bs[2])
+        hand_on_all(bs[0])
+        hop(2, "qkv")
 
     PAin[0] = PAb[:, 0:C]
     sums_over_tensor("pa", PAin, PA)
-    hand_on(3, bs[3], bs[2])
-    for i in (3, 2):
-        from_tensor(bs[i], Ball, block(i))
-        shared(bs[i], Ball, block(i))
-    second_feed_grads()
-    sums_over_tensor("pb", PBin, PB)
-
-    @pl.when(first)
-    def _():
-        hop(2, "qkv")
-        hop(3, bs[1], bs[0])
-        hand_on(2, bs[1], bs[0])
+    from_pair(bs[2], Ball, block(2))
+    shared(bs[2], *whole_rows(bs[2]))
     if gathered:
         convolution_rows_back()
+    sums_over_tensor("pb", PBin, PB)
+
+    @pl.when(first)
+    def _():
+        hop(3, bs[1])
+        hand_on(1, bs[1])
+        hand_on(2, bs[1])
+
+    convolution_grads()
+    relay_output("grad", IG)
+
+    @pl.when(second)
+    def _():
+        from_tensor(bs[0], Ball, block(0))
+
+    shared(bs[0], *whole_rows(bs[0]))
+    feed_grads(0, 0)
+    hand_on(3, bs[1])
     hop(3, "qkv")
-    hand_on(3, bs[1], bs[0])
-    convolution_grads()
-    from_tensor(bs[1], Ball, block(1))
-    shared(bs[1], Ball, block(1))
+    from_pair(bs[1], Ball, block(1))
+    shared(bs[1], *whole_rows(bs[1]))
     attention_grads()
-
-    @pl.when(second)
-    def _():
-        from_tensor(bs[0], Ball, block(0))
-
-    shared(bs[0], Ball, block(0))
-    write(Ball.at[:, block(0)], b0_out)
     for name, ref in (("pa", PA), ("pb", PB)):
         all_arrived((name, 3), (groups - 1) * size_of(ref.at[0]))
-    all_arrived("out", 3 * size_of(out_rows()))
-    all_arrived("grad", 3 * size_of(back_rows()))
-    for copy in written:
-        copy.wait()
+    all_arrived("out", 2 * size_of(back_rows()))
+    all_arrived("grad", 2 * size_of(back_rows()))
+    for src, dst in ((LO, lo_out), (IG, ig_out), (PA, pa_out), (PB, pb_out), (CS, cs_out)):
+        write(src, dst)
+    pltpu.make_async_copy(room(sum(written)), room(sum(written)), os.at[0]).wait()
     for cond, sizes in sent.values():
 
         def all_sent():
@@ -1067,9 +1128,10 @@
 
 
 def last_kernel(*refs):
-    given, outs, held, made, in_sems, out_sems = refs[:17], refs[17:31], refs[31:48], refs[48:59], refs[59], refs[60]
-    lo, ig, pa, pb, n0, b0, act0, slope0, fout, table, in1, out1, qkv, ao, ci, co, cs = held
-    LO, IG, ng, nb, w_in, w_out, w_rel, pos, w_dw, bng, bns = made
+    given, outs, held, made, in_sems, out_sems = refs[:12], refs[12:26], refs[26:38], refs[38:52], refs[52], refs[53]
+    in_grad, out_grad, qkv, ao, ci, co, pa, pb, cs, lo, ig, table = held
+    (LO, IG, ng, nb, w_in, w_out, w_ain, pos, w_aout, w_cin, w_dw, bng, bns, w_cout) = made
+    C, width = ao.shape
     copies = []
 
     def send(src, dst):
@@ -1077,32 +1139,35 @@
         copy.start()
         copies.append(copy)
 
-    given = [m.at[0] if i == 8 else m for i, m in enumerate(given)]
     loads = [pltpu.make_async_copy(given[i], held[i], in_sems.at[i]) for i in range(len(held))]
-    for i in (5, 8, 7, 4, 6, 10, 11, 12, 14, 13, 15, 2, 3, 0, 1, 9, 16):
-        loads[i].start()
-    for i in (5, 8, 7, 4):
+    for load in loads:
+        load.start()
+    for i, src, dst, out in ((0, in_grad, w_in, outs[4]), (1, out_grad, w_out, outs[5])):
         loads[i].wait()
-    hidden = (dot(b0[...], fout[...], 1, 1) * slope0[...]).astype(bf16)
-    w_in[...] = dot(n0[...], hidden, 0, 0)
-    send(w_in, outs[4].at[0])
-    loads[6].wait()
-    w_out[...] = dot(act0[...], b0[...], 0, 0)
-    send(w_out, outs[5].at[0])
-    for i, dst in (
-        (10, outs[4].at[1]), (11, outs[5].at[1]), (12, outs[6].at[pl.ds(0, 3)]), (14, outs[9]), (13, outs[8]),
-        (15, outs[13]),
-    ):
-        loads[i].wait()
-        send(held[i], dst)
-    for i in (2, 3, 0, 1, 9, 16):
-        loads[i].wait()
+        for j in range(2):
+            dst[j] = src[j].astype(f32)
+            send(dst.at[j], out.at[j])
+    loads[2].wait()
+    w_ain[0:3] = qkv[...].astype(f32)
+    send(w_ain.at[pl.ds(0, 3)], outs[6].at[pl.ds(0, 3)])
+    loads[3].wait()
+    w_aout[...] = ao[...].astype(f32)
+    send(w_aout, outs[8])
+    loads[4].wait()
+    for i in range(2):
+        w_cin[pl.ds(i, width, stride=2), :] = ci[:, C * i : C * (i + 1)].astype(f32)
+    send(w_cin, outs[9])
+    loads[5].wait()
+    w_cout[...] = co[...].astype(f32)
+    send(w_cout, outs[13])
+    for load in loads[6:]:
+        load.wait()
     sums, norms = pa[0].astype(f32), pb[0].astype(f32)
     for g in range(1, pa.shape[0]):
         sums += pa[g].astype(f32)
         norms += pb[g].astype(f32)
-    w_rel[...] = dot(table[...], sums[relative_at(pa.shape[0]) :].astype(bf16), 0, 0)
-    send(w_rel, outs[6].at[3])
+    w_ain[3] = dot(table[...], sums[relative_at(pa.shape[0]) :].astype(bf16), 0, 0)
+    send(w_ain.at[3], outs[6].at[3])
     LO[...] = lo[...].astype(f32)
     IG[...] = ig[...].astype(f32)
     for i in range(5):
@@ -1116,8 +1181,8 @@
     bns[...] = sums[3:4]
     for k in range(taps):
         w_dw[k] = sums[4 + k : 5 + k]
-    for i, src in ((0, LO), (1, IG), (2, ng), (3, nb), (7, pos), (10, w_dw), (11, bng), (12, bns)):
-        send(src, outs[i])
+    for i in (0, 1, 2, 3, 7, 10, 11, 12):
+        send(made[i], outs[i])
     for copy in copies:
         copy.wait()
 
@@ -1133,34 +1198,32 @@
     groups = dp if dp <= 4 else 1
     R = groups * group * frames
     table = position_rows(frames, width)
-    vm = pl.BlockSpec(memory_space=pltpu.VMEM)
     hbm = pl.BlockSpec(memory_space=pltpu.HBM)
     sums_rows = relative_at(groups) + 2 * frames
 
     def shape(dims, dtype=bf16):
         return jax.ShapeDtypeStruct(dims, dtype)
 
+    small_first = [
+        shape((group * frames, width)), shape((group * frames, width)), shape((groups, sums_rows, C)),
+        shape((groups, 16, width)), shape((40, C), f32),
+    ]
     made_first = [
-        shape((width, width), f32), shape((width, width), f32), shape((3, width, C), f32), shape((C, width), f32),
-        shape((2 * width, C), f32), shape((C, width), f32),
+        shape((2, width, width)), shape((2, width, width)), shape((3, width, C)), shape((C, width)),
+        shape((width, 2 * C)), shape((C, width)),
     ]
-    n_recv = 75 + 15 * (groups - 1)
+    n_recv = 84 + 15 * (groups - 1)
     n_send = 3 + 2 * (groups - 1) + 2 * max(groups - 2, 0)
     operands = (
         lengths, inputs, cotangent, norm_gain.transpose(1, 0, 2), norm_bias.transpose(1, 0, 2), ffn_in[0],
         ffn_out[0], attn_in[0], attn_out[0], conv_in.reshape(2 * width, C), conv_out[0], pos_bias[0], bn_gain,
-        bn_shift, depthwise.transpose(1, 0, 2), table,
+        bn_shift, depthwise.transpose(1, 0, 2), table[0],
     )
-    lo, ig, pa, pb, cs, n0, b0, act0, slope0, *ready = pl.pallas_call(
+    lo, ig, pa, pb, cs, *ready = pl.pallas_call(
         lambda *refs: layer_kernel((frames, width, dp, groups), *refs),
-        out_shape=[
-            shape((group * frames, width)), shape((group * frames, width)),
-            shape((groups, sums_rows, C)), shape((groups, 16, width)), shape((40, C), f32),
-            shape((R, width)), shape((R, width)), shape((R, width)), shape((R, width), f32),
-        ]
-        + made_first,
+        out_shape=small_first + made_first,
         in_specs=[hbm] * 16,
-        out_specs=[vm] * 5 + [hbm] * 10,
+        out_specs=[hbm] * 11,
         scratch_shapes=[
             pltpu.VMEM((2, 4, width, width), bf16),
             pltpu.VMEM((2, 4, width, width), bf16),
@@ -1201,7 +1264,7 @@
             pltpu.VMEM((1, C), f32),
             pltpu.VMEM((1, C), f32),
             pltpu.VMEM((taps, 1, C), f32),
-            pltpu.VMEM((4 * frames, width), bf16),
+            pltpu.VMEM((2 * frames, width), bf16),
             pltpu.SMEM((group,), jnp.int32),
             pltpu.VMEM((2 * width, C), bf16),
             pltpu.VMEM((2 * width, C), f32),
@@ -1222,11 +1285,14 @@
             pltpu.VMEM((R // frames, frames + 32, C), f32),
             pltpu.VMEM((taps, 8, C), f32),
             pltpu.VMEM((4, 8, C), f32),
+        ]
+        + [pltpu.VMEM(m.shape, m.dtype) for m in small_first]
+        + [
             pltpu.VMEM((2**23 // 512, 128), f32),
             pltpu.SemaphoreType.DMA((n_send,)),
             pltpu.SemaphoreType.DMA((n_recv,)),
             pltpu.SemaphoreType.DMA((21,)),
-            pltpu.SemaphoreType.DMA((10,)),
+            pltpu.SemaphoreType.DMA((1,)),
         ],
         compiler_params=pltpu.CompilerParams(
             collective_id=0, has_side_effects=True, vmem_limit_bytes=62 * 2**20
@@ -1239,19 +1305,14 @@
         shape((4, width, C), f32), shape((2, C), f32), shape((C, width), f32), shape((2 * width, C), f32),
         shape((taps, 1, C), f32), shape((1, C), f32), shape((1, C), f32), shape((C, width), f32),
     ]
-    given = (lo, ig, pa, pb, n0, b0, act0, slope0, ffn_out[0], table[2 * frames :], *ready, cs)
-    held = list(given)
-    held[8] = shape((width, width))
-    made = [m for i, m in enumerate(gradients) if i not in (8, 9, 13)]
-    made[4] = made[5] = shape((width, width), f32)
-    made[6] = shape((width, C), f32)
+    given = (*ready, pa, pb, cs, lo, ig, table[1])
     outs = pl.pallas_call(
         last_kernel,
         out_shape=gradients,
         in_specs=[hbm] * len(given),
         out_specs=[hbm] * len(gradients),
-        scratch_shapes=[pltpu.VMEM(m.shape, m.dtype) for m in held]
-        + [pltpu.VMEM(m.shape, m.dtype) for m in made]
+        scratch_shapes=[pltpu.VMEM(m.shape, m.dtype) for m in given]
+        + [pltpu.VMEM(m.shape, m.dtype) for m in gradients]
         + [pltpu.SemaphoreType.DMA((len(given),)), pltpu.SemaphoreType.DMA((len(gradients) + 4,))],
         compiler_params=pltpu.CompilerParams(vmem_limit_bytes=62 * 2**20),
     )(*given)

time: 104 us -> 97.6 us (0.938)
  Pallas kernels: 103 us -> 96.5 us
    pallas_call x1, Pallas kernels: 97.2 us -> 92.1 us  [on_device(): pl.pallas_call(lambda *refs: layer_kernel((frames, width, dp, groups), *r...]
    pallas_call x1, Pallas kernels: 5.78 us -> 4.37 us  [on_device(): pl.pallas_call(last_kernel, out_shape=gradients, in_specs=[hbm] * len(giv...]
where the time goes in v5:
time: 97.6 us; the launch traced here: 97.3 us
  Pallas kernels  96.5 us (99%)
    pallas_call x1, Pallas kernels, on_device(): pl.pallas_call(lambda *refs: layer_kernel((frames, width, dp, groups), *r...  92.1 us
    pallas_call x1, Pallas kernels, on_device(): pl.pallas_call(last_kernel, out_shape=gradients, in_specs=[hbm] * len(giv...  4.37 us

profile of v5, /device:TPU:0, one launch (start us, length us, event | category | flops | bytes accessed | tf_op | source)
XLA Modules:
  0.0 97.3 jit_solution(4899784728874946076)
XLA Ops:
  0.7 92.1 %shard_map.272 = (bf16[128,512]{1,0:T(8,128)(2,1)}, bf16[128,512]{1,0:T(8,128)(2,1)}, bf16[4,80,128]{2,1,0:T(8,128)(2,1)}, bf16[4,16,512]{2,1,0:T(8,128)(2,1)}, ...) custom-call(s32[4]{0:T(128)} %refs_0_.1, ...), custom_call_target="tpu_custom_call" | custom-call | tf_op jit(solution)/shard_map/pallas_call | solution.py:1222
  92.8 4.4 %shard_map.273 = (f32[128,512]{1,0:T(8,128)}, f32[128,512]{1,0:T(8,128)}, f32[5,1,512]{2,1,0:T(1,128)}, f32[5,1,512]{2,1,0:T(1,128)}, f32[2,512,512]{2,1,0:T(8,1...) custom-call(bf16[2,512,512]{2,1,0:T(8,128)(2,1)} %get-tuple-element., ...), custom_call_target="tpu_custom_call" | custom-call | tf_op jit(solution)/shard_map/pallas_call | solution.py:1309

commit v6 on v5

--- a/solution.py
+++ b/solution.py
@@ -52,8 +52,8 @@
     (SfSt, SbSt, PAst, PAb, PAin, PBst, PBin, STF, STB, RSst, RSin) = refs[22:33]
     (ng, nb, pos, bng, bns, dw, e2, lens, pairs, spread) = refs[33:43]
     (Nall, Ball, Sf, Sb, ACT, SLOPE, HG, gin, gout, gqkv, gao, gci, gco) = refs[43:56]
-    GA, HATA, UA, DYA, DA, DWACC, INVA = refs[56:63]
-    LO, IG, PA, PB, CS, dummy, ss, rs, ls, os = refs[63:73]
+    GA, HATA, UA, DYA, DA, DWACC, INVA, OST, STL, VIA = refs[56:66]
+    LO, IG, PA, PB, CS, dummy, ss, rs, ls, os = refs[66:76]
     gathered = groups > 1
 
     s, t, d = lax.axis_index(SECTION), lax.axis_index(TENSOR), lax.axis_index(DATA)
@@ -200,29 +200,50 @@
     only = {i: second for i in range(4)}
     over_y = {i: "own" for i in range(14)}
 
-    def send_chunks(names):
+    def send_core(names):
         for i in names:
             src, dst = chunks[i]
-            start(("sib", i), lambda src=src: src(None), lambda dst=dst: dst(1, None), sib, only.get(i))
-            w = over_y.get(i)
-            start(("y", i), lambda src=src, w=w: src(w), lambda dst=dst, w=w: dst(2, w), yp, only.get(i))
-
-    def step_a(i):
+            start(("sib", i), lambda src=src: src(None), lambda dst=dst: dst(1, None), sib)
+
+    def send_y(names):
+        for i in names:
+            (src, dst), w = chunks[i], over_y.get(i)
+            cond = first if i == 13 else only.get(i)
+            start(("y", i), lambda src=src, w=w: src(w), lambda dst=dst, w=w: dst(2, w), yp, cond)
+
+    def send_round():
+        start(("r", 0), lambda: chunks[13][0]("own"), lambda: VIA.at[0], partner, second)
+
+    def pass_round(n):
+        arrived(("r", n - 1), VIA.at[n - 1])
+        if n == 1:
+            start(("r", 1), lambda: VIA.at[0], lambda: VIA.at[1], yp, first)
+        else:
+            start(("r", 2), lambda: VIA.at[1], lambda: chunks[13][1](2, "own"), partner, first)
+
+    def step_a(i, by="y"):
         dst, w = chunks[i][1], over_y.get(i)
-        arrived(("y", i), dst(2, w))
+        arrived(("r", 2) if by == "r" else ("y", i), dst(2, w))
         if w:
             start(("z", i), lambda: dst(2, w), lambda: dst(2, w), zpair, only.get(i))
-        start(("sib", i), lambda: dst(2, w), lambda: dst(3, w), sib, only.get(i), 1)
+        start(("on", i), lambda: dst(2, w), lambda: dst(3, w), sib, only.get(i), 1)
 
     def step_b(i):
         if i not in over_y:
             return
         dst = chunks[i][1]
         arrived(("z", i), dst(2, "other"))
-        start(("sib", i), lambda: dst(2, "other"), lambda: dst(3, "other"), sib, only.get(i), 2)
+        start(("on", i), lambda: dst(2, "other"), lambda: dst(3, "other"), sib, only.get(i), 2)
+
+    def core_part(i):
+        arrived(("sib", i), chunks[i][1](1, None))
+
+    def passed_part(i):
+        all_arrived(("on", i), size_of(chunks[i][1](1, None)))
 
     def step_c(i):
-        all_arrived(("sib", i), 2 * size_of(chunks[i][1](1, None)))
+        core_part(i)
+        passed_part(i)
 
     def steps(cond, *plan):
         @pl.when(cond)
@@ -258,14 +279,10 @@
     def place(k):
         return pl.ds(base + T * PLACE[k], T)
 
-    own, four = pl.ds(base, T), pl.ds(base, R4)
+    own, two = pl.ds(base, T), pl.ds(base, 2 * T)
 
     def block(i, n=1):
         return pl.ds(i * width, n * width)
-
-    def to_tensor(name, ref, c, cond=None):
-        for k in (1, 2, 3):
-            start(name, lambda: ref.at[own, c], lambda k=k: ref.at[place(k), c], peers[k], cond, k)
 
     def from_tensor(name, ref, c):
         all_arrived(name, 3 * size_of(ref.at[own, c]))
@@ -285,34 +302,40 @@
         x = X[before]
         a = norm(i, x).astype(bf16)
         Nall[own, i * width : (i + 1) * width] = a
-        to_pair(("n", i), Nall, block(i), second)
+        to_pair(("n", i), Nall, block(i))
+        if j:
+            step_c(11)
+            step_c(12)
         active = []
         for k in range(4):
             h = dot(a, Win[j, k])
             H[j, k] = h
             active.append(silu(h).astype(bf16))
-        total = dot(active[0], Wout[j, 0])
-        for k in range(1, 4):
-            total += dot(active[k], Wout[j, k])
+        Q, total = width // 2, 0.0
+        for q in range(2):
+            if j:
+                step_c(13 + q)
+            for k in range(4):
+                total += dot(active[k][:, Q * q : Q * (q + 1)], Wout[j, k, Q * q : Q * (q + 1)])
         X[after] = x + 0.5 * total
 
     def sum_to_owner(name, slot, total):
-        for k in (1, 2, 3):
-            RSst[slot, k - 1] = total[T * PLACE[k] : T * (PLACE[k] + 1)].astype(bf16)
-        for k in (1, 2, 3):
-            start(name, lambda k=k: RSst.at[slot, k - 1], lambda k=k: RSin.at[slot, k - 1], peers[k], first, k)
+        RSst[slot] = total[T : 2 * T].astype(bf16)
+        start(name, lambda: RSst.at[slot], lambda: RSin.at[slot], yp, first)
         return total[0:T]
 
     def summed_here(name, slot, total):
-        all_arrived(name, size_of(RSin.at[slot]))
-        for k in (1, 2, 3):
-            total += RSin[slot, k - 1].astype(f32)
-        return total
+        arrived(name, RSin.at[slot])
+        return total + RSin[slot].astype(f32)
 
     def shared_feed(j, i):
-        from_tensor(("n", i), Nall, block(i))
-        active = silu(dot(Nall[four, i * width : (i + 1) * width], Win[j, 0])).astype(bf16)
-        return sum_to_owner(("s", j), j, dot(active, Wout[j, 0]))
+        relay(("n", i), Nall, block(i))
+        a = Nall[two, i * width : (i + 1) * width]
+        total = dot(silu(dot(a, Win[j, 0])).astype(bf16), Wout[j, 0])
+        for k in range(11 * j, 11 * j + 4):
+            core_part(k)
+        total += dot(silu(dot(a, Win[j, 1])).astype(bf16), Wout[j, 1])
+        return sum_to_owner(("s", j), j, total)
 
     fetched("ng", "nb")
 
@@ -320,11 +343,14 @@
     def _():
         pltpu.make_async_copy(inputs.at[t], X.at[0], ls.at[20]).wait()
         Nall[own, 0:width] = norm(0, X[0]).astype(bf16)
-        to_tensor(("n", 0), Nall, block(0), first)
+        to_pair(("n", 0), Nall, block(0))
+
+    send_core(range(4))
 
     @pl.when(second)
     def _():
-        send_chunks(range(4))
+        send_round()
+        send_y(range(4))
         pltpu.make_async_copy(cot.at[t], G, ls.at[20]).wait()
 
     fetched("pos", "bng", "bns", "dw", "wr", "e2", "len", "ci")
@@ -338,13 +364,18 @@
     for k in range(taps):
         SM[4 + k : 5 + k, 0:C] = dw[k]
     R2[0 : 2 * T, 0:C] = dot(e2[...], Wr[...]).astype(bf16)
+    lengths_here = [jnp.broadcast_to(lens[t ^ PLACE[p]].astype(f32), (1, C)) for p in range(4)]
+    STL[d] = jnp.concatenate(lengths_here + [jnp.zeros((4, C), f32)], 0)
+    for r in range(1, dp):
+        start("len", lambda: STL.at[d], lambda: STL.at[d], zpeers[r], None, r)
     fetched("in0", "out0")
 
     @pl.when(first)
     def _():
-        send_chunks((8,))
+        send_core((15, 16, 4, 5, 6, 7, 8, 9, 10))
+        send_y((8,))
         X[1] = shared_feed(0, 0)
-        send_chunks((9,))
+        send_y((9,))
 
     @pl.when(first)
     def _():
@@ -353,7 +384,10 @@
 
     @pl.when(second)
     def _():
-        send_chunks((15, 16, *range(4, 15)))
+        for i in (15, 16, *range(4, 15)):
+            send_core((i,))
+            if i != 13:
+                send_y((i,))
 
     fetched("qkv", "o", "co", "in1", "out1")
     margin = 16
@@ -415,20 +449,28 @@
         return mixed
 
     def shared_attention():
-        a = Nall[four, width : 2 * width]
-        q, key, value = (dot(a, Wqkv[i, :, 0:C]) for i in range(3))
-        qu, qv, key, value = q + SM[0:1, 0:C], q + SM[1:2, 0:C], key.astype(bf16), value.astype(bf16)
-        mixed = []
-        for p in range(4):
-            rows = slice(T * p, T * (p + 1))
-            keys = keys_of(lens[t ^ PLACE[p]])
-            mixed.append(attend(qu[rows], qv[rows], key[rows], value[rows], R2[0 : 2 * T, 0:C], keys)[1])
-        mixed = jnp.concatenate(mixed, 0)
-        Sf[four, 0:C] = mixed
-        return sum_to_owner(("s", 3), 3, dot(mixed, Wo[0:C]))
+        for i in (4, 5, 6, 15, 16):
+            core_part(i)
+        a = Nall[two, width : 2 * width]
+        q, key, value = (dot(a, Wqkv[i, :, 0 : 2 * C]) for i in range(3))
+        qu, qv, key, value = q + SM[0:1, 0 : 2 * C], q + SM[1:2, 0 : 2 * C], key.astype(bf16), value.astype(bf16)
+        mixed = [[], []]
+        for p in range(2):
+            rows, keys = slice(T * p, T * (p + 1)), keys_of(lens[t ^ PLACE[p]])
+            for k in range(2):
+                c = slice(C * k, C * (k + 1))
+                mixed[k].append(
+                    attend(qu[rows, c], qv[rows, c], key[rows, c], value[rows, c], R2[0 : 2 * T, c], keys)[1]
+                )
+        mixed = [jnp.concatenate(m, 0) for m in mixed]
+        Sf[two, 0:C] = mixed[0]
+        OST[...] = mixed[1]
+        start("sf", lambda: OST, lambda: Sf.at[pl.ds(high_of[0], 2 * T), pl.ds(0, C)], sib, first, 4)
+        core_part(7)
+        return sum_to_owner(("s", 3), 3, dot(mixed[0], Wo[0:C]) + dot(mixed[1], Wo[C : 2 * C]))
 
     def relative_arrived():
-        step_c(16)
+        passed_part(16)
         turned_back = (
             lax.broadcasted_iota(jnp.int32, (2 * T, 2 * T), 0) + lax.broadcasted_iota(jnp.int32, (2 * T, 2 * T), 1)
             == 2 * T - 2
@@ -439,39 +481,41 @@
     @pl.when(first)
     def _():
         Nall[own, width : 2 * width] = norm(1, X[1]).astype(bf16)
-        to_tensor(("n", 1), Nall, block(1), first)
-        send_chunks((10, 15))
+        to_pair(("n", 1), Nall, block(1))
+        send_y((15,))
+        pass_round(1)
+        send_y((10,))
         step_a(9)
         step_b(8)
-        from_tensor(("n", 1), Nall, block(1))
+        relay(("n", 1), Nall, block(1))
         total = shared_attention()
-        send_chunks((4, 5, 6, 16, 7))
-        step_a(10)
+        send_y((4, 5, 6, 16, 7))
         step_a(15)
         step_b(9)
         X[2] = X[1] + summed_here(("s", 3), 3, total)
-        step_b(10)
-        step_c(15)
+        pass_round(2)
+        step_a(10)
+        passed_part(15)
 
     @pl.when(second)
     def _():
-        coming = (*range(4), 15, 16, *range(4, 13))
+        coming = (*range(4), 15, 16, *range(4, 14))
         for n, i in enumerate(coming):
-            step_a(i)
-            if n > 1:
+            step_a(i, "r" if i == 13 else "y")
+            if n > 1 and i != 13:
                 step_b(coming[n - 2])
         for i in range(7):
             step_c(i)
         step_c(15)
+        core_part(16)
         relative_arrived()
         arrived("hop", ARR)
         X[0] = ARR[...].astype(f32)
         feed(0, 0, 0, 1)
         Nall[own, width : 2 * width] = norm(1, X[1]).astype(bf16)
-        to_pair(("n", 1), Nall, block(1), second)
+        to_pair(("n", 1), Nall, block(1))
         step_b(11)
         mixed = attention_here()
-        step_a(13)
         step_b(12)
         for k in range(4):
             SfSt[k, :, 0:C] = mixed[k]
@@ -614,7 +658,7 @@
         write(gout.at[j], out_out.at[j])
 
     def mask_of(g, p):
-        return (lax.broadcasted_iota(jnp.int32, (T, C), 0).astype(f32) < STF[g, 3:4, C * p : C * (p + 1)]).astype(f32)
+        return (lax.broadcasted_iota(jnp.int32, (T, C), 0).astype(f32) < STL[g, p : p + 1]).astype(f32)
 
     places = [(p, [(g, slice(R4 * g + T * p, R4 * g + T * (p + 1))) for g in range(groups)]) for p in range(4)]
 
@@ -636,7 +680,7 @@
 
         lax.fori_loop(0, 4 * groups, one, 0)
         for p, parts in places:
-            n = sum(STF[g, 3:4, C * p : C * (p + 1)] for g, _ in parts)
+            n = sum(STL[g, p : p + 1] for g, _ in parts)
             masked = [HATA[rows] * mask_of(g, p) for g, rows in parts]
             mean = sum(total_of(m) for m in masked) / n
             square = sum(total_of(m * HATA[rows]) for m, (_, rows) in zip(masked, parts)) / n
@@ -732,8 +776,7 @@
     conv = CT[...]
 
     def dp_sums(name, ref, rows):
-        n = len(rows)
-        ref[d] = jnp.concatenate(rows + [jnp.zeros((8 - n, width), f32)], 0)
+        ref[d] = jnp.concatenate([row[:, C * k : C * (k + 1)] for row in rows for k in range(4)], 0)
         for r in range(1, dp):
             start(name, lambda: ref.at[d], lambda: ref.at[d], zpeers[r], None, r)
 
@@ -742,25 +785,24 @@
         total = ref[0]
         for r in range(1, dp):
             total += ref[r]
-        return total
+        return [jnp.concatenate([total[4 * i + k : 4 * i + k + 1] for k in range(4)], 1) for i in range(2)]
 
     masked = conv * row_mask
-    frames_row = jnp.broadcast_to(total_of(row_mask), (1, width))
-    lengths_row = jnp.concatenate(
-        [jnp.broadcast_to(lens[t ^ PLACE[p]].astype(f32), (1, C)) for p in range(4)], 1
-    )
-    dp_sums("bnf", STF, [total_of(masked), total_of(masked * conv), frames_row, lengths_row])
-    steps(second, (A, 14), (B, 13))
+    dp_sums("bnf", STF, [total_of(masked), total_of(masked * conv)])
+    steps(second, (A, 14))
+    steps(first, (B, 10))
     step_c(10)
     sums = summed("bnf", STF)
+    steps(second, (B, 13))
     steps(first, (A, 4), (A, 5), (A, 6), (A, 16))
 
     @pl.when(second)
     def _():
         set_off("n")
-    count = sums[2:3]
-    bn_mean = sums[0:1] / count
-    inv_std = lax.rsqrt(sums[1:2] / count - bn_mean * bn_mean + EPSILON)
+    all_arrived("len", (dp - 1) * size_of(STL.at[0]))
+    count = sum(STL[r, 0:1, 0:1] for r in range(dp))
+    bn_mean = sums[0] / count
+    inv_std = lax.rsqrt(sums[1] / count - bn_mean * bn_mean + EPSILON)
     hat = (conv - bn_mean) * inv_std
     CT[...] = hat
     active = silu(hat * SM[2:3] + SM[3:4]).astype(bf16)
@@ -772,10 +814,10 @@
     @pl.when(first)
     def _():
         Nall[own, 3 * width : 4 * width] = norm(3, X[3]).astype(bf16)
-        to_tensor(("n", 3), Nall, block(3), first)
-        send_chunks((11,))
+        to_pair(("n", 3), Nall, block(3))
+        send_core((11, 12, 13, 14))
         total = shared_feed(1, 3)
-        send_chunks((12, 13, 14))
+        send_y((11, 12, 13, 14))
         step_a(7)
         step_b(4)
         step_b(5)
@@ -783,8 +825,6 @@
 
     @pl.when(second)
     def _():
-        for i in range(11, 15):
-            step_c(i)
         feed(1, 3, 3, 4)
     out = (norm(4, X[4]) * row_mask).astype(bf16)
     HOP[...] = out
@@ -816,7 +856,10 @@
 
     @pl.when(first)
     def _():
-        set_off("n", "m", "sf")
+        set_off("n", "m")
+        if gathered:
+            all_arrived("sf", size_of(OST))
+            set_off("sf")
         relay(("n", 2), Nall, block(2))
         step_a(11)
         for i in (6, 7):
@@ -824,18 +867,18 @@
         step_a(12)
         step_b(11)
         for i in (4, 5, 6, 7):
-            step_c(i)
+            passed_part(i)
         relative_arrived()
         attention_here()
         step_a(13)
         step_b(12)
         if not gathered:
-            from_tensor("sf", Sf, pl.ds(C, C))
+            all_arrived("sf", size_of(OST) + 3 * size_of(Sf.at[own, pl.ds(C, C)]))
         step_a(14)
         hop(1, "n", "m", "sf")
         step_b(13)
         for i in range(11, 15):
-            step_c(i)
+            passed_part(i)
         for k in range(4):
             H[1, k] = dot(Nall[own, 3 * width : 4 * width], Win[1, k])
         hop(2, "n", "m", "sf")
@@ -853,11 +896,9 @@
     def feed_back(j, i, g):
         b = (0.5 * g).astype(bf16)
         Ball[own, i * width : (i + 1) * width] = b
+        to_pair(("b", i), Ball, block(i))
         if j:
-            to_pair(("b", i), Ball, block(i))
             set_off(("b", i))
-        else:
-            to_tensor(("b", i), Ball, block(i))
         grad = None
         for k in range(4):
             h = H[j, k]
@@ -885,7 +926,8 @@
     @pl.when(first)
     def _():
         hand_on(3, "n", "m")
-        from_pair(("n", 2), Nall, block(2))
+        for i in range(4):
+            from_pair(("n", i), Nall, block(i))
         all_shared("n", "m")
         forward_values()
         hop(1, ("b", 3))
@@ -896,7 +938,7 @@
     @pl.when(second)
     def _():
         for i in range(4):
-            relay(("n", i), Nall, block(i), None if i == 2 else second)
+            relay(("n", i), Nall, block(i))
         hop(1, "n")
         set_off("m")
         from_tensor("sf", Sf, sf_cols)
@@ -905,7 +947,7 @@
     relay_output("out", LO)
     relay(("b", 2), Ball, block(2))
     set_off_to_all(("b", 2))
-    dc = inv_std * (dhat - (sums[0:1] + hat * sums[1:2]) / count) * row_mask
+    dc = inv_std * (dhat - (sums[0] + hat * sums[1]) / count) * row_mask
     DP[margin : margin + T] = dc
     for p in range(4):
         c = pl.ds(C * p, C)
@@ -992,7 +1034,7 @@
     @pl.when(first)
     def _():
         Ball[own, 0:width] = (0.5 * g).astype(bf16)
-        to_tensor(("b", 0), Ball, block(0))
+        to_pair(("b", 0), Ball, block(0))
         G[...] = g
 
     set_off_to_all(("b", 0))
@@ -1028,6 +1070,7 @@
         hop(2, "n")
         hop(1, "m", "sf", bs[3])
         relay(bs[1], Ball, block(1))
+        relay(bs[0], Ball, block(0))
         from_tensor("qkv", Sb, qkv_cols)
         set_off("qkv")
         hop(1, bs[1])
@@ -1059,11 +1102,13 @@
         hop(1, bs[1])
         hand_on(1, bs[3])
         hand_on(2, bs[3])
-        from_tensor(bs[0], Ball, block(0))
-        h = dot(Nall[four, 0:width], Win[0, 0])
-        sig = jax.nn.sigmoid(h)
-        hg = dot(Ball[four, 0:width], Wout[0, 0], 1, 1) * slope(h, sig)
-        X[0] = sum_to_owner(("s", 2), 2, dot(hg.astype(bf16), Win[0, 0], 1, 1))
+        relay(bs[0], Ball, block(0))
+        total = 0.0
+        for k in range(2):
+            h = dot(Nall[two, 0:width], Win[0, k])
+            hg = dot(Ball[two, 0:width], Wout[0, k], 1, 1) * slope(h, jax.nn.sigmoid(h))
+            total += dot(hg.astype(bf16), Win[0, k], 1, 1)
+        X[0] = sum_to_owner(("s", 2), 2, total)
         send_sums()
         hand_on_all(bs[2])
         from_all(bs[0])
@@ -1081,6 +1126,7 @@
         send_ends()
         hand_on_all(bs[0])
         hop(2, "qkv")
+        hop(3, bs[1])
 
     PAin[0] = PAb[:, 0:C]
     sums_over_tensor("pa", PAin, PA)
@@ -1092,20 +1138,16 @@
 
     @pl.when(first)
     def _():
-        hop(3, bs[1])
         hand_on(1, bs[1])
         hand_on(2, bs[1])
 
     convolution_grads()
     relay_output("grad", IG)
-
-    @pl.when(second)
-    def _():
-        from_tensor(bs[0], Ball, block(0))
-
+    hand_on(3, bs[1])
+
+    from_pair(bs[0], Ball, block(0))
     shared(bs[0], *whole_rows(bs[0]))
     feed_grads(0, 0)
-    hand_on(3, bs[1])
     hop(3, "qkv")
     from_pair(bs[1], Ball, block(1))
     shared(bs[1], *whole_rows(bs[1]))
@@ -1212,7 +1254,7 @@
         shape((2, width, width)), shape((2, width, width)), shape((3, width, C)), shape((C, width)),
         shape((width, 2 * C)), shape((C, width)),
     ]
-    n_recv = 84 + 15 * (groups - 1)
+    n_recv = 109 + 15 * (groups - 1)
     n_send = 3 + 2 * (groups - 1) + 2 * max(groups - 2, 0)
     operands = (
         lengths, inputs, cotangent, norm_gain.transpose(1, 0, 2), norm_bias.transpose(1, 0, 2), ffn_in[0],
@@ -1254,10 +1296,10 @@
             pltpu.VMEM((4, sums_rows, C), bf16),
             pltpu.VMEM((16, width), f32),
             pltpu.VMEM((4, 16, width), bf16),
-            pltpu.VMEM((dp, 8, width), f32),
-            pltpu.VMEM((dp, 8, width), f32),
-            pltpu.VMEM((4, 3, frames, width), bf16),
-            pltpu.VMEM((4, 3, frames, width), bf16),
+            pltpu.VMEM((dp, 8, C), f32),
+            pltpu.VMEM((dp, 8, C), f32),
+            pltpu.VMEM((4, frames, width), bf16),
+            pltpu.VMEM((4, frames, width), bf16),
             pltpu.VMEM((5, 1, width), f32),
             pltpu.VMEM((5, 1, width), f32),
             pltpu.VMEM((2, C), f32),
@@ -1285,10 +1327,13 @@
             pltpu.VMEM((R // frames, frames + 32, C), f32),
             pltpu.VMEM((taps, 8, C), f32),
             pltpu.VMEM((4, 8, C), f32),
+            pltpu.VMEM((2 * frames, C), bf16),
+            pltpu.VMEM((dp, 8, C), f32),
+            pltpu.VMEM((2, width // 4, width), bf16),
         ]
         + [pltpu.VMEM(m.shape, m.dtype) for m in small_first]
         + [
-            pltpu.VMEM((2**23 // 512, 128), f32),
+            pltpu.VMEM((10 * 2**20 // 512, 128), f32),
             pltpu.SemaphoreType.DMA((n_send,)),
             pltpu.SemaphoreType.DMA((n_recv,)),
             pltpu.SemaphoreType.DMA((21,)),

time: 97.6 us -> 95.2 us (0.975)
  Pallas kernels: 96.5 us -> 94.2 us
    pallas_call x1, Pallas kernels: 92.1 us -> 89.8 us  [on_device(): pl.pallas_call(lambda *refs: layer_kernel((frames, width, dp, groups), *r...]
where the time goes in v6:
time: 95.2 us; the launch traced here: 95 us
  Pallas kernels  94.2 us (99%)
    pallas_call x1, Pallas kernels, on_device(): pl.pallas_call(lambda *refs: layer_kernel((frames, width, dp, groups), *r...  89.8 us
    pallas_call x1, Pallas kernels, on_device(): pl.pallas_call(last_kernel, out_shape=gradients, in_specs=[hbm] * len(giv...  4.37 us

profile of v6, /device:TPU:0, one launch (start us, length us, event | category | flops | bytes accessed | tf_op | source)
XLA Modules:
  0.0 95.0 jit_solution(10458121887188568614)
XLA Ops:
  0.7 89.8 %shard_map.272 = (bf16[128,512]{1,0:T(8,128)(2,1)}, bf16[128,512]{1,0:T(8,128)(2,1)}, bf16[4,80,128]{2,1,0:T(8,128)(2,1)}, bf16[4,16,512]{2,1,0:T(8,128)(2,1)}, ...) custom-call(s32[4]{0:T(128)} %refs_0_.1, ...), custom_call_target="tpu_custom_call" | custom-call | tf_op jit(solution)/shard_map/pallas_call | solution.py:1264
  90.5 4.4 %shard_map.273 = (f32[128,512]{1,0:T(8,128)}, f32[128,512]{1,0:T(8,128)}, f32[5,1,512]{2,1,0:T(1,128)}, f32[5,1,512]{2,1,0:T(1,128)}, f32[2,512,512]{2,1,0:T(8,1...) custom-call(bf16[2,512,512]{2,1,0:T(8,128)(2,1)} %get-tuple-element., ...), custom_call_target="tpu_custom_call" | custom-call | tf_op jit(solution)/shard_map/pallas_call | solution.py:1354

commit v7 on v6

--- a/solution.py
+++ b/solution.py
@@ -514,9 +514,8 @@
         feed(0, 0, 0, 1)
         Nall[own, width : 2 * width] = norm(1, X[1]).astype(bf16)
         to_pair(("n", 1), Nall, block(1))
+        mixed = attention_here()
         step_b(11)
-        mixed = attention_here()
-        step_b(12)
         for k in range(4):
             SfSt[k, :, 0:C] = mixed[k]
         step_c(7)
@@ -789,7 +788,7 @@
 
     masked = conv * row_mask
     dp_sums("bnf", STF, [total_of(masked), total_of(masked * conv)])
-    steps(second, (A, 14))
+    steps(second, (B, 12), (A, 14))
     steps(first, (B, 10))
     step_c(10)
     sums = summed("bnf", STF)
@@ -1181,28 +1180,33 @@
         copy.start()
         copies.append(copy)
 
-    loads = [pltpu.make_async_copy(given[i], held[i], in_sems.at[i]) for i in range(len(held))]
+    whole = [5, 3, 4, 2, 6, 7, 8, 9, 10, 11]
+    halves = [(i, j) for i in range(2) for j in range(2)]
+    pieces = [(given[i], held[i]) for i in whole[:4]]
+    pieces += [(given[i].at[j], held[i].at[j]) for i, j in halves]
+    pieces += [(given[i], held[i]) for i in whole[4:]]
+    loads = [pltpu.make_async_copy(src, dst, in_sems.at[n]) for n, (src, dst) in enumerate(pieces)]
     for load in loads:
         load.start()
-    for i, src, dst, out in ((0, in_grad, w_in, outs[4]), (1, out_grad, w_out, outs[5])):
-        loads[i].wait()
-        for j in range(2):
-            dst[j] = src[j].astype(f32)
-            send(dst.at[j], out.at[j])
-    loads[2].wait()
-    w_ain[0:3] = qkv[...].astype(f32)
-    send(w_ain.at[pl.ds(0, 3)], outs[6].at[pl.ds(0, 3)])
-    loads[3].wait()
+    loads[0].wait()
+    w_cout[...] = co[...].astype(f32)
+    send(w_cout, outs[13])
+    loads[1].wait()
     w_aout[...] = ao[...].astype(f32)
     send(w_aout, outs[8])
-    loads[4].wait()
+    loads[2].wait()
     for i in range(2):
         w_cin[pl.ds(i, width, stride=2), :] = ci[:, C * i : C * (i + 1)].astype(f32)
     send(w_cin, outs[9])
-    loads[5].wait()
-    w_cout[...] = co[...].astype(f32)
-    send(w_cout, outs[13])
-    for load in loads[6:]:
+    loads[3].wait()
+    w_ain[0:3] = qkv[...].astype(f32)
+    send(w_ain.at[pl.ds(0, 3)], outs[6].at[pl.ds(0, 3)])
+    for n, (i, j) in enumerate(halves):
+        loads[4 + n].wait()
+        src, dst, out = ((in_grad, w_in, outs[4]), (out_grad, w_out, outs[5]))[i]
+        dst[j] = src[j].astype(f32)
+        send(dst.at[j], out.at[j])
+    for load in loads[8:]:
         load.wait()
     sums, norms = pa[0].astype(f32), pb[0].astype(f32)
     for g in range(1, pa.shape[0]):
@@ -1358,7 +1362,7 @@
         out_specs=[hbm] * len(gradients),
         scratch_shapes=[pltpu.VMEM(m.shape, m.dtype) for m in given]
         + [pltpu.VMEM(m.shape, m.dtype) for m in gradients]
-        + [pltpu.SemaphoreType.DMA((len(given),)), pltpu.SemaphoreType.DMA((len(gradients) + 4,))],
+        + [pltpu.SemaphoreType.DMA((len(given) + 2,)), pltpu.SemaphoreType.DMA((len(gradients) + 4,))],
         compiler_params=pltpu.CompilerParams(vmem_limit_bytes=62 * 2**20),
     )(*given)
     if groups == 1:

time: 95.2 us -> 93.8 us (0.985)
  Pallas kernels: 94.2 us -> 92.9 us
    pallas_call x1, Pallas kernels: 89.8 us -> 88.8 us  [on_device(): pl.pallas_call(lambda *refs: layer_kernel((frames, width, dp, groups), *r...]
where the time goes in v7:
time: 93.8 us; the launch traced here: 93.7 us
  Pallas kernels  92.9 us (99%)
    pallas_call x1, Pallas kernels, on_device(): pl.pallas_call(lambda *refs: layer_kernel((frames, width, dp, groups), *r...  88.8 us
    pallas_call x1, Pallas kernels, on_device(): pl.pallas_call(last_kernel, out_shape=gradients, in_specs=[hbm] * len(giv...  4.06 us

profile of v7, /device:TPU:0, one launch (start us, length us, event | category | flops | bytes accessed | tf_op | source)
XLA Modules:
  0.0 93.7 jit_solution(9378613902622449682)
XLA Ops:
  0.7 88.8 %shard_map.272 = (bf16[128,512]{1,0:T(8,128)(2,1)}, bf16[128,512]{1,0:T(8,128)(2,1)}, bf16[4,80,128]{2,1,0:T(8,128)(2,1)}, bf16[4,16,512]{2,1,0:T(8,128)(2,1)}, ...) custom-call(s32[4]{0:T(128)} %refs_0_.1, ...), custom_call_target="tpu_custom_call" | custom-call | tf_op jit(solution)/shard_map/pallas_call | solution.py:1268
  89.5 4.1 %shard_map.273 = (f32[128,512]{1,0:T(8,128)}, f32[128,512]{1,0:T(8,128)}, f32[5,1,512]{2,1,0:T(1,128)}, f32[5,1,512]{2,1,0:T(1,128)}, f32[2,512,512]{2,1,0:T(8,1...) custom-call(bf16[2,512,512]{2,1,0:T(8,128)(2,1)} %get-tuple-element., ...), custom_call_target="tpu_custom_call" | custom-call | tf_op jit(solution)/shard_map/pallas_call | solution.py:1358

commit v8 on v7

--- a/solution.py
+++ b/solution.py
@@ -1113,6 +1113,9 @@
         from_all(bs[0])
         hop(1, "qkv")
         hop(2, bs[1])
+        g = G[...] + norm_back(0, summed_here(("s", 2), 2, X[0]))
+        IG[pl.ds(trow, T)] = g.astype(bf16)
+        send_ends()
     hand_on(3, bs[3])
     from_pair(bs[3], Ball, block(3))
     shared(bs[3], *whole_rows(bs[3]))
@@ -1120,20 +1123,17 @@
 
     @pl.when(first)
     def _():
-        g = G[...] + norm_back(0, summed_here(("s", 2), 2, X[0]))
-        IG[pl.ds(trow, T)] = g.astype(bf16)
-        send_ends()
         hand_on_all(bs[0])
         hop(2, "qkv")
         hop(3, bs[1])
 
     PAin[0] = PAb[:, 0:C]
     sums_over_tensor("pa", PAin, PA)
+    sums_over_tensor("pb", PBin, PB)
     from_pair(bs[2], Ball, block(2))
     shared(bs[2], *whole_rows(bs[2]))
     if gathered:
         convolution_rows_back()
-    sums_over_tensor("pb", PBin, PB)
 
     @pl.when(first)
     def _():

time: 93.8 us -> 93.4 us (level)
  no operation moved by 1% of the time
where the time goes in v8:
time: 93.4 us; the launch traced here: 93.2 us
  Pallas kernels  92.4 us (99%)
    pallas_call x1, Pallas kernels, on_device(): pl.pallas_call(lambda *refs: layer_kernel((frames, width, dp, groups), *r...  88.3 us
    pallas_call x1, Pallas kernels, on_device(): pl.pallas_call(last_kernel, out_shape=gradients, in_specs=[hbm] * len(giv...  4.06 us

profile of v8, /device:TPU:0, one launch (start us, length us, event | category | flops | bytes accessed | tf_op | source)
XLA Modules:
  0.0 93.2 jit_solution(10624447727016570593)
XLA Ops:
  0.7 88.3 %shard_map.272 = (bf16[128,512]{1,0:T(8,128)(2,1)}, bf16[128,512]{1,0:T(8,128)(2,1)}, bf16[4,80,128]{2,1,0:T(8,128)(2,1)}, bf16[4,16,512]{2,1,0:T(8,128)(2,1)}, ...) custom-call(s32[4]{0:T(128)} %refs_0_.1, ...), custom_call_target="tpu_custom_call" | custom-call | tf_op jit(solution)/shard_map/pallas_call | solution.py:1268
  89.0 4.1 %shard_map.273 = (f32[128,512]{1,0:T(8,128)}, f32[128,512]{1,0:T(8,128)}, f32[5,1,512]{2,1,0:T(1,128)}, f32[5,1,512]{2,1,0:T(1,128)}, f32[2,512,512]{2,1,0:T(8,1...) custom-call(bf16[2,512,512]{2,1,0:T(8,128)(2,1)} %get-tuple-element., ...), custom_call_target="tpu_custom_call" | custom-call | tf_op jit(solution)/shard_map/pallas_call | solution.py:1358
